TPU v7x, 512 devices: a whole 4x8x8 slice. The times are simulated.
512 devices in a mesh: dp: 32 (over x, y), tensor: 16 (over z, core).
Axes of the slice: x: 4, y: 8, z: 8, core: 2. Of those that a mesh axis runs over, the one named last changes fastest.
Arguments:
- hidden: bfloat16 [65536, 8192], P('dp', 'tensor'), may hold values from -6 to 6
- value_matrix: bfloat16 [8192, 1024], P('tensor'), may hold values from -0.09375 to 0.09375
- adapter_down_store: bfloat16 [64, 8192, 64], P('dp', 'tensor'), may hold values from -0.0625 to 0.0625
- adapter_up_store: bfloat16 [64, 64, 1024], P('dp', None, 'tensor'), may hold values from -0.75 to 0.75
- adapter_slot: int32 [64], replicated, may hold values from 0 to 63, each once
- rollout_adapter: int32 [128], P('dp'), may hold values from 0 to 63
- lengths: int32 [128], P('dp'), may hold values from 128 to 512, as said below
Outputs:
- values: bfloat16 [65536, 1024], P('dp', 'tensor')
Inputs may be any that keep to these rules, and one draw needn't show every extreme that they name: `adapter_slot`: each slot once. `lengths`: in every draw some rollout has exactly 512 valid tokens and some exactly a quarter of 512.
All inputs are finite; a program needn't handle non-finite values.
Results may differ from a plain program's by a relative error of at most 0.024.
Values may be sent and summed in bfloat16 or wider, within the bound.
No kernel may reach another device: no remote copies, remote signals or barrier semaphores. Data moves between devices by JAX's collectives and lax.ppermute only.
A program may use at most 64 MiB of HBM per device.

v0:
```python
import jax
import jax.numpy as jnp
from jax import lax
from jax.sharding import PartitionSpec as P

ADAPTER_SCALE = 2.0


def on_device(
    hidden,
    value_matrix,
    adapter_down_store,
    adapter_up_store,
    adapter_slot,
    rollout_adapter,
    lengths,
):
    rollouts_here = rollout_adapter.shape[0]
    length = hidden.shape[0] // rollouts_here
    features = hidden.shape[1]
    column_range = adapter_up_store.shape[2]
    table_size = adapter_slot.shape[0]
    matches = rollout_adapter[:, None] == jnp.arange(table_size, dtype=jnp.int32)[None, :]
    chosen = jnp.sum(jnp.where(matches, adapter_slot[None, :], 0), axis=1)
    down_fragment = lax.all_gather(adapter_down_store, "dp", axis=0, tiled=True)
    up_fragment = lax.all_gather(adapter_up_store, "dp", axis=0, tiled=True)
    piece_count = down_fragment.shape[0]
    offsets = jnp.arange(piece_count, dtype=jnp.int32)[None, :]
    picker = (chosen[:, None] == offsets).astype(jnp.bfloat16)
    down_next = jnp.einsum("rs,sdk->rdk", picker, down_fragment, preferred_element_type=jnp.float32)
    up_next = jnp.einsum("rs,skc->rkc", picker, up_fragment, preferred_element_type=jnp.float32)
    down_chosen = down_next
    up_chosen = up_next
    down_chosen = down_chosen.astype(jnp.bfloat16)
    up_chosen = up_chosen.astype(jnp.bfloat16)
    token_rows = hidden.reshape(rollouts_here, length, features)
    partial_down = jnp.einsum(
        "rld,rdk->rlk", token_rows, down_chosen, preferred_element_type=jnp.float32
    )
    down_total = lax.psum(partial_down.astype(jnp.bfloat16), "tensor")
    partial_value = jnp.dot(hidden, value_matrix, preferred_element_type=jnp.float32)
    base_output = lax.psum_scatter(
        partial_value.astype(jnp.bfloat16), "tensor", scatter_dimension=1, tiled=True
    ).astype(jnp.float32)
    adapter_update = jnp.einsum(
        "rlk,rkc->rlc", down_total, up_chosen, preferred_element_type=jnp.float32
    )
    base_output = base_output.reshape(rollouts_here, length, column_range)
    positions = jnp.arange(length, dtype=jnp.int32)
    validity_mask = (positions[None, :] < lengths[:, None])[:, :, None]
    scored_output = jnp.where(
        validity_mask, base_output + ADAPTER_SCALE * adapter_update, jnp.float32(0.0)
    ).astype(jnp.bfloat16)
    return scored_output.reshape(rollouts_here * length, column_range)


def solution(mesh):
    in_specs = (
        P("dp", "tensor"),
        P("tensor", None),
        P("dp", "tensor", None),
        P("dp", None, "tensor"),
        P(),
        P("dp"),
        P("dp"),
    )
    out_specs = P("dp", "tensor")
    return jax.shard_map(
        on_device, mesh=mesh, in_specs=in_specs, out_specs=out_specs, check_vma=False
    )
```

profile of v0, /device:TPU:1, one launch (start us, length us, event | category | flops | bytes accessed | tf_op | source)
XLA Modules:
  0.0 233.4 jit_solution(17433668516628191250)
XLA Ops:
  7.4 0.0 copy-start
  7.4 0.0 all-gather.2.cloned.1.call-start
  7.4 0.7 all-gather.2.cloned.1.call-update
  8.1 0.0 reduce-scatter.2.cloned.1.call-start
  8.1 0.8 copy-done
  9.0 5.5 %convolution_convert_fusion = bf16[2048,1024]{0,1:T(8,128)(2,1)} fusion(bf16[2048,512]{1,0:T(8,128)(2,1)S(1)} %copy-done, bf16[512,1024]{1,0:T(8,128)(2,1)} %param.8), kind=kOutput, calls=%fused_computation.2 | convolution fusion | flops 2149580800 | bytes 7340032 | tf_op jit(solution)/shard_map/dot_general | solution.py:41
  14.5 0.0 reduce-scatter.2.cloned.1.call-update
  14.5 0.0 all-reduce.2.cloned.1.call-start
  14.6 0.6 copy-done.3
  15.2 0.0 copy-done.4
  15.2 0.2 select_reduce_fusion
  15.4 0.0 copy-done.1
  15.4 43.3 %all_gather.7 = bf16[64,64,64]{2,1,0:T(8,128)(2,1)S(1)} all-gather(bf16[2,64,64]{2,1,0:T(8,128)(2,1)S(1)} %copy-done.1), channel_id=1, replica_groups=mesh['dp'=32,'tensor'=16] {'dp'}, dimensions={0}, use_global_device_ids=true | all-gather | bytes 540672 | tf_op jit(solution)/shard_map/all_gather | solution.py:26
  58.6 0.7 convolution_convert_fusion.2
  59.3 41.8 %all-gather.2.cloned.1.call-done = bf16[64,512,64]{1,2,0:T(8,128)(2,1)} async-done(((bf16[2,512,64]{1,2,0:T(8,128)(2,1)}), bf16[64,512,64]{1,2,0:T(8,128)(2,1)}) %all-gather.2.cloned.1.call-update) | async-done | bytes 4194320 | tf_op jit(solution)/shard_map/all_gather | solution.py:25
  101.1 6.7 %fusion.5 = bf16[4,512,64]{1,0,2:T(4,128)(2,1)S(1)} fusion(bf16[64,512,64]{1,2,0:T(8,128)(2,1)} %all-gather.2.cloned.1.call-done, s32[4]{0:T(128)S(1)} %select_reduce_fusion), kind=kOutput, calls=%fused_computation.8 | convolution fusion | flops 16908544 | bytes 4456464 | tf_op jit(solution)/shard_map/rs,sdk->rdk/dot_general | solution.py:30
  107.9 1.5 fusion.8
  109.3 0.0 all-reduce.2.cloned.1.call-update
  109.3 0.0 copy-done.2
  109.3 0.1 iota_compare_fusion
  109.4 1.0 reshape.40
  110.4 113.6 %all-reduce.2.cloned.1.call-done = bf16[4,512,64]{1,2,0:T(8,128)(2,1)} async-done(((bf16[4,512,64]{1,2,0:T(8,128)(2,1)}), bf16[4,512,64]{1,2,0:T(8,128)(2,1)}) %all-reduce.2.cloned.1.call-update) | async-done | bytes 262160 | tf_op jit(solution)/shard_map/psum | solution.py:40
  224.0 1.2 fusion.9
  225.3 0.7 copy.24
  (5 shorter events, 0.0 us)
Async XLA Ops:
  7.4 1.6 copy-start
  7.4 93.8 %all-gather.2.cloned.1.call-start = ((), (), s32[]{:S(2)}) async-start(), calls=%async_computation.2 | async-start | bytes 4325376 | tf_op jit(solution)/shard_map/all_gather | solution.py:25
  8.1 101.3 %reduce-scatter.2.cloned.1.call-start = ((), (), s32[]{:S(2)}) async-start(), calls=%async_computation.1 | async-start | bytes 4456448 | tf_op jit(solution)/shard_map/reduce_scatter | solution.py:42
  14.5 0.7 copy-start.3
  14.5 0.7 copy-start.4
  14.5 0.9 copy-start.1
  14.5 209.5 %all-reduce.2.cloned.1.call-start = ((), (), s32[]{:S(2)}) async-start(), calls=%async_computation.3 | async-start | bytes 524288 | tf_op jit(solution)/shard_map/psum | solution.py:40
  58.6 50.7 %copy-start.2 = (s32[4]{0:T(128)S(1)}, s32[4]{0:T(128)}, u32[]{:S(2)}) copy-start(s32[4]{0:T(128)} %param.13) | copy-start | bytes 52
Sparse Core Ops, SparseCore 0:
  11.4 89.7 all-gather.1
Sparse Core Ops, SparseCore 1:
  14.6 69.8 reduce-scatter.1
  109.4 114.6 all-reduce.1
where the time goes:
time: 234 us; the launch traced here: 233 us
  waiting for transfers between devices  156 us (67%)
  blocking collectives  43.3 us (19%)
  matrix products  15.6 us (7%)
  between operations  14.9 us (6%)
    psum x1, waiting for transfers between devices, on_device(): down_total = lax.psum(partial_down.astype(jnp.bfloat16), 'tensor')  114 us
    all_gather x1, blocking collectives, on_device(): up_fragment = lax.all_gather(adapter_up_store, 'dp', axis=0, tiled=True)  43.3 us
    all_gather x1, waiting for transfers between devices, on_device(): down_fragment = lax.all_gather(adapter_down_store, 'dp', axis=0, tiled=True)  41.8 us
    dot_general x1, matrix products, on_device(): jnp.einsum('rs,sdk->rdk', picker, down_fragment, preferred_element_type=j...  6.7 us
    dot_general x1, matrix products, on_device(): jnp.dot(hidden, value_matrix, preferred_element_type=jnp.float32)  5.54 us
  transfers between devices with their start and end apart: 3, of which 2 were waited for; matrix products, arithmetic and copies ran while one was open for 7% of the time, Pallas kernels for 0%

commit v1 on v0

v1 whole, which is shorter than its diff:
```python
import functools

import jax
import jax.numpy as jnp
from jax import lax
from jax.experimental import pallas as pl
from jax.experimental.pallas import tpu as pltpu
from jax.sharding import Mesh
from jax.sharding import PartitionSpec as P

ADAPTER_SCALE = 2.0
X, CORES = 4, 2
DP, TENSOR = ("x", "y"), ("z", "core")
LANES = 128
KERNEL_VMEM = 8 << 20
PROJECT_VMEM = 32 << 20
PROJECT_CHIPS, PROJECT_ROWS = 4, 1024
NO_COST = pl.CostEstimate(flops=0, bytes_accessed=0, transcendentals=0)


def pick_kernel(index_ref, store_ref, out_ref, sems):
    copies = [
        pltpu.make_async_copy(store_ref.at[index_ref[i]], out_ref.at[i], sems.at[i])
        for i in range(out_ref.shape[0])
    ]
    for copy in copies:
        copy.start()
    for copy in copies:
        copy.wait()


def pick(store, index):
    count = index.shape[0]
    out = jax.ShapeDtypeStruct((count, *store.shape[1:]), store.dtype)
    size = out.size * out.dtype.itemsize
    return pl.pallas_call(
        pick_kernel,
        out_shape=out,
        in_specs=[pl.BlockSpec(memory_space=pltpu.SMEM), pl.BlockSpec(memory_space=pl.ANY)],
        out_specs=pl.BlockSpec(memory_space=pltpu.VMEM),
        scratch_shapes=[pltpu.SemaphoreType.DMA((count,))],
        cost_estimate=pl.CostEstimate(flops=0, bytes_accessed=2 * size, transcendentals=0),
        compiler_params=pltpu.CompilerParams(vmem_limit_bytes=KERNEL_VMEM),
        name="pick_slots",
    )(index, store)


def down_kernel(chunk, index_ref, hidden_ref, factor_ref, out_ref):
    product = lax.dot_general(
        hidden_ref[...],
        factor_ref[0],
        (((1,), (1,)), ((), ())),
        preferred_element_type=jnp.float32,
    ).T.astype(out_ref.dtype)
    for i in range(out_ref.shape[0]):
        out_ref[i] = product[:, i * chunk : (i + 1) * chunk]


def down_projection(hidden, factors, index, members):
    tokens, features = hidden.shape
    _, rank, _ = factors.shape
    count = index.shape[0]
    length, chunk = tokens // count, tokens // members
    per = length // chunk
    return pl.pallas_call(
        functools.partial(down_kernel, chunk),
        grid_spec=pltpu.PrefetchScalarGridSpec(
            num_scalar_prefetch=1,
            grid=(count,),
            in_specs=[
                pl.BlockSpec((length, features), lambda r, index: (r, 0)),
                pl.BlockSpec((1, rank, features), lambda r, index: (index[r], 0, 0)),
            ],
            out_specs=pl.BlockSpec((per, rank, chunk), lambda r, index: (r, 0, 0)),
        ),
        out_shape=jax.ShapeDtypeStruct((members, rank, chunk), hidden.dtype),
        cost_estimate=pl.CostEstimate(
            flops=2 * tokens * features * rank,
            bytes_accessed=2 * (hidden.size + count * rank * features + tokens * rank),
            transcendentals=0,
        ),
        compiler_params=pltpu.CompilerParams(vmem_limit_bytes=KERNEL_VMEM),
        name="down_projection",
    )(index, hidden, factors)


def final_kernel(slots_ref, lengths_ref, base_ref, down_ref, up_ref, out_ref):
    r = pl.program_id(0)
    columns, length = base_ref.shape
    down = jnp.concatenate([down_ref[i] for i in range(down_ref.shape[0])], axis=1)
    update = lax.dot_general(
        up_ref[0, :, :columns],
        down,
        (((0,), (0,)), ((), ())),
        preferred_element_type=jnp.float32,
    )
    total = base_ref[...].astype(jnp.float32) + ADAPTER_SCALE * update
    position = lax.broadcasted_iota(jnp.int32, (columns, length), 1)
    out_ref[...] = jnp.where(position < lengths_ref[r], total, 0.0).astype(out_ref.dtype)


def final(slots, lengths, base, down, up_store):
    columns, tokens = base.shape
    _, rank, width = up_store.shape
    count = slots.shape[0]
    members, _, chunk = down.shape
    per = members // count
    length = tokens // count
    return pl.pallas_call(
        final_kernel,
        grid_spec=pltpu.PrefetchScalarGridSpec(
            num_scalar_prefetch=2,
            grid=(count,),
            in_specs=[
                pl.BlockSpec((columns, length), lambda r, slots, lengths: (0, r)),
                pl.BlockSpec((per, rank, chunk), lambda r, slots, lengths: (r, 0, 0)),
                pl.BlockSpec((1, rank, width), lambda r, slots, lengths: (slots[r], 0, 0)),
            ],
            out_specs=pl.BlockSpec((columns, length), lambda r, slots, lengths: (0, r)),
        ),
        out_shape=jax.ShapeDtypeStruct(base.shape, base.dtype),
        cost_estimate=pl.CostEstimate(
            flops=2 * tokens * columns * rank,
            bytes_accessed=4 * base.size + 2 * down.size + 2 * count * rank * width,
            transcendentals=0,
        ),
        compiler_params=pltpu.CompilerParams(vmem_limit_bytes=KERNEL_VMEM),
        name="add_update",
    )(slots, lengths, base, down, up_store)


def project_kernel(keep, core_ref, hidden_ref, matrix_ref, *refs):
    came_ref, out_ref = (refs[0], refs[1]) if keep else (None, refs[0])
    blocks, columns, _ = out_ref.shape
    core = core_ref[0]
    upper = core == 1 if keep else core == 0
    parts = []
    for j in range(blocks):
        low = matrix_ref[:, (CORES * j) * columns : (CORES * j + 1) * columns]
        high = matrix_ref[:, (CORES * j + 1) * columns : (CORES * j + 2) * columns]
        parts.append(jnp.where(upper, high, low))
    product = jnp.dot(
        hidden_ref[...], jnp.concatenate(parts, axis=1), preferred_element_type=jnp.float32
    ).T
    for j in range(blocks):
        block = product[j * columns : (j + 1) * columns]
        if keep:
            block = block + came_ref[j].astype(jnp.float32)
        out_ref[j] = block.astype(out_ref.dtype)


def project(core, hidden, matrix, columns, came=None):
    tokens, features = hidden.shape
    width = matrix.shape[1]
    chips = width // (CORES * columns)
    step, rows = min(PROJECT_CHIPS, chips), min(PROJECT_ROWS, tokens)
    block = pl.BlockSpec((step, columns, rows), lambda t, j: (j, 0, t))
    operands = [core.reshape(1), hidden, matrix] + ([] if came is None else [came])
    return pl.pallas_call(
        functools.partial(project_kernel, came is not None),
        grid=(tokens // rows, chips // step),
        out_shape=jax.ShapeDtypeStruct((chips, columns, tokens), hidden.dtype),
        in_specs=[
            pl.BlockSpec(memory_space=pltpu.SMEM),
            pl.BlockSpec((rows, features), lambda t, j: (t, 0)),
            pl.BlockSpec((features, step * CORES * columns), lambda t, j: (0, j)),
        ]
        + ([] if came is None else [block]),
        out_specs=block,
        cost_estimate=NO_COST,
        compiler_params=pltpu.CompilerParams(vmem_limit_bytes=PROJECT_VMEM),
        name="project_own" if came is not None else "project_other",
    )(*operands)


def to_all(block, axis):
    copies = jnp.broadcast_to(block, (lax.axis_size(axis), *block.shape))
    return lax.all_to_all(copies, axis, 0, 0)


def on_device(
    hidden, value_matrix, adapter_down_store, adapter_up_store, adapter_slot, rollout_adapter, lengths
):
    features = hidden.shape[1]
    members = lax.axis_size(TENSOR)
    rollouts = rollout_adapter.shape[0]
    slots_here, rank, columns = adapter_up_store.shape

    copies = jnp.swapaxes(adapter_down_store, 1, 2)
    copies = jnp.broadcast_to(copies, (lax.axis_size("y"), *copies.shape))
    copies, hidden = lax.optimization_barrier((copies, hidden))
    row = lax.all_to_all(copies, "y", 0, 0)
    row = row.reshape(-1, rank, features)
    row_slots = row.shape[0]

    up_store = jnp.pad(adapter_up_store, ((0, 0), (0, 0), (0, -columns % LANES)))
    up_store = lax.all_gather(up_store, DP, axis=0, tiled=True)

    here = lax.axis_index("x")
    shifts = [
        rollout_adapter if d == 0 else lax.ppermute(rollout_adapter, "x", [(i, (i + d) % X) for i in range(X)])
        for d in range(X)
    ]
    wanted = jnp.stack(shifts)[(here - jnp.arange(X, dtype=jnp.int32)) % X].reshape(-1)
    table = jnp.arange(adapter_slot.shape[0], dtype=jnp.int32)
    matches = wanted[:, None] == table[None, :]
    slots = jnp.sum(jnp.where(matches, adapter_slot[None, :], 0), axis=1)
    local = jnp.clip(slots - here * row_slots, 0, row_slots - 1)
    own_matches = rollout_adapter[:, None] == table[None, :]
    own_slots = jnp.sum(jnp.where(own_matches, adapter_slot[None, :], 0), axis=1)
    own = (own_slots // row_slots) * rollouts + jnp.arange(rollouts, dtype=jnp.int32)
    core = lax.axis_index("core")
    other = project(core, hidden, value_matrix, columns)
    came = lax.ppermute(other, "core", [(0, 1), (1, 0)])
    chip = project(core, hidden, value_matrix, columns, came)
    chip, row, local = lax.optimization_barrier((chip, row, local))
    base = lax.psum_scatter(chip.reshape(-1, hidden.shape[0]), "z", scatter_dimension=0, tiled=True)

    sent = pick(row, local).reshape(X, rollouts * rank, features)
    came = lax.all_to_all(sent, "x", 0, 0).reshape(X * rollouts, rank, features)

    down = down_projection(hidden, came, own, members)
    down = lax.all_to_all(down, TENSOR, 0, 0)
    down = jnp.sum(down.astype(jnp.float32), axis=0).astype(jnp.bfloat16)
    down = to_all(down, TENSOR)
    return final(own_slots, lengths, base, down, up_store).T


def solution(mesh):
    dp, tensor = mesh.devices.shape
    fine = Mesh(mesh.devices.reshape(X, dp // X, tensor // CORES, CORES), (*DP, *TENSOR))
    in_specs = (
        P(DP, TENSOR),
        P(TENSOR, None),
        P(DP, TENSOR, None),
        P(DP, None, TENSOR),
        P(),
        P(DP),
        P(DP),
    )
    return jax.shard_map(
        on_device, mesh=fine, in_specs=in_specs, out_specs=P(DP, TENSOR), check_vma=False
    )
```

time: 234 us -> 134 us (0.57)
  waiting for transfers between devices: 156 us -> 38 us
  starting transfers between devices: 0.09 us -> 28.8 us
  blocking collectives: 43.3 us -> 22.9 us
  Pallas kernels: 0 us -> 15.9 us
  matrix products: 15.6 us -> 0 us
  local copies, waits for them, and re-layouts: 2.14 us -> 12.5 us
    psum x1 -> x0, waiting for transfers between devices: 114 us -> none  [on_device(): down_total = lax.psum(partial_down.astype(jnp.bfloat16), 'tensor')]
    all_gather x1 -> x0, blocking collectives: 43.3 us -> none  [on_device(): up_fragment = lax.all_gather(adapter_up_store, 'dp', axis=0, tiled=True)]
    all_gather x1, waiting for transfers between devices: 41.8 us -> 0.01 us  [on_device(): up_store = lax.all_gather(up_store, DP, axis=0, tiled=True)]
    all_to_all x0 -> x3, waiting for transfers between devices: none -> 36.2 us  [the longest x1 14 us: on_device(): came = lax.all_to_all(sent, 'x', 0, 0).reshape(X * rollouts, rank, features)]
    all_to_all x0 -> x1, blocking collectives: none -> 22.9 us  [on_device(): down = lax.all_to_all(down, TENSOR, 0, 0)]
    ppermute x0 -> x4, starting transfers between devices: none -> 17.3 us  [the longest x1 8.91 us: on_device(): came = lax.ppermute(other, 'core', [(0, 1), (1, 0)])]
    pallas_call x0 -> x5, Pallas kernels: none -> 15.9 us  [the longest x2 9.51 us: project(): pl.pallas_call(functools.partial(project_kernel, came is not None), grid=...]
    dot_general x5 -> x0, matrix products: 15.6 us -> none  [the longest x1 6.7 us: on_device(): jnp.einsum('rs,sdk->rdk', picker, down_fragment, preferred_element_type=j...]
  transfers between devices with their start and end apart: 3 -> 9, of which waited for: 2 -> 4; matrix products, arithmetic and copies ran while one was open for 7% -> 2% of each run, Pallas kernels for 0% -> 7%
where the time goes in v1:
time: 134 us
  waiting for transfers between devices  38 us (28%)
  starting transfers between devices  28.8 us (21%)
  blocking collectives  22.9 us (17%)
  Pallas kernels  15.9 us (12%)
  between operations  15 us (11%)
  local copies, waits for them, and re-layouts  12.5 us (9%)
    all_to_all x1, blocking collectives, on_device(): down = lax.all_to_all(down, TENSOR, 0, 0)  22.9 us
    all_to_all x1, waiting for transfers between devices, on_device(): came = lax.all_to_all(sent, 'x', 0, 0).reshape(X * rollouts, rank, features)  14 us
    all_to_all x1, waiting for transfers between devices, to_all(): return lax.all_to_all(copies, axis, 0, 0)  11.7 us
    all_to_all x1, waiting for transfers between devices, on_device(): row = lax.all_to_all(copies, 'y', 0, 0)  10.6 us
    pallas_call x2, Pallas kernels, project(): pl.pallas_call(functools.partial(project_kernel, came is not None), grid=...  9.51 us
    ppermute x1, starting transfers between devices, on_device(): came = lax.ppermute(other, 'core', [(0, 1), (1, 0)])  8.91 us
    unnamed x24, local copies, waits for them, and re-layouts  8.51 us
    ppermute x3, starting transfers between devices, on_device(): lax.ppermute(rollout_adapter, 'x', [(i, (i + d) % X) for i in range(X)])  8.41 us
  transfers between devices with their start and end apart: 9, of which 4 were waited for; matrix products, arithmetic and copies ran while one was open for 2% of the time, Pallas kernels for 7%

profile of v1, /device:TPU:1, one launch (start us, length us, event | category | flops | bytes accessed | tf_op | source)
XLA Modules:
  0.0 133.6 jit_solution(5695087854312251300)
XLA Ops:
  7.4 2.0 %broadcast_in_dim.38 = bf16[8,2,64,512]{3,2,1,0:T(8,128)(2,1)} broadcast(bf16[2,64,512]{2,1,0:T(8,128)(2,1)} %bitcast.17), dimensions={1,2,3} | broadcast | bytes 1179648 | tf_op jit(solution)/shard_map/broadcast_in_dim | solution.py:190
  9.4 1.6 %copy-done = bf16[2048,512]{1,0:T(8,128)(2,1)S(1)} copy-done((bf16[2048,512]{1,0:T(8,128)(2,1)S(1)}, bf16[2048,512]{1,0:T(8,128)(2,1)}, u32[]{:S(2)}) %copy-start) | copy-done | bytes 2097176
  11.0 1.2 copy-done.4
  12.2 4.5 %project_other.1 = bf16[8,64,2048]{2,1,0:T(8,128)(2,1)} custom-call(s32[1]{0:T(128)} %bitcast.core_ref, bf16[2048,512]{1,0:T(8,128)(2,1)S(1)} %copy-done, bf16[512,1024]{1,0:T(8,128)(2,1)S(1)} %copy-done.4), custom_call_target="tpu_custom_call" | custom-call | tf_op jit(solution)/shard_map/project_other/pallas_call | solution.py:159
  16.7 8.9 %collective-permute-start = (bf16[8,64,2048]{2,1,0:T(8,128)(2,1)}, bf16[8,64,2048]{2,1,0:T(8,128)(2,1)}, u32[]{:S(2)}, u32[]{:S(2)}) collective-permute-start(bf16[8,64,2048]{2,1,0:T(8,128)(2,1)} %project_other.1), channel_id=1, source_target_pairs={{0,1},{1,0},{2,3},{3,2},{4,5},{5,4},{6,7},{7,6},{8,9},{9,8},{10,11... | collective-permute-start | bytes 6291464 | tf_op jit(solution)/shard_map/ppermute | solution.py:214
  26.3 3.6 %all-to-all-start = ((bf16[8,2,64,512]{3,2,1,0:T(8,128)(2,1)}), bf16[8,2,64,512]{3,2,1,0:T(8,128)(2,1)S(1)}, u32[]{:S(2)}, u32[]{:S(2)}) async-start(bf16[8,2,64,512]{3,2,1,0:T(8,128)(2,1)} %broadcast_in_dim.38), calls=%async_computation | async-start | bytes 2097152 | tf_op jit(solution)/shard_map/all_to_all | solution.py:192
  29.9 1.9 %collective-permute-start.1 = (s32[4]{0:T(128)S(1)}, s32[4]{0:T(128)S(1)}, u32[]{:S(2)}, u32[]{:S(2)}) collective-permute-start(s32[4]{0:T(128)S(1)} %copy-done.10), channel_id=1, source_target_pairs={{0,128},{128,256},{256,384},{384,0},{1,129},{129,257},{257,385},{3... | collective-permute-start | bytes 56 | tf_op jit(solution)/shard_map/ppermute | solution.py:201
  31.9 3.4 %collective-permute-start.2 = (s32[4]{0:T(128)S(1)}, s32[4]{0:T(128)S(1)}, u32[]{:S(2)}, u32[]{:S(2)}) collective-permute-start(s32[4]{0:T(128)S(1)} %copy-done.10), channel_id=1, source_target_pairs={{0,256},{128,384},{256,0},{384,128},{1,257},{129,385},{257,1},{385... | collective-permute-start | bytes 56 | tf_op jit(solution)/shard_map/ppermute | solution.py:201
  35.3 3.1 %collective-permute-start.3 = (s32[4]{0:T(128)S(1)}, s32[4]{0:T(128)S(1)}, u32[]{:S(2)}, u32[]{:S(2)}) collective-permute-start(s32[4]{0:T(128)S(1)} %copy-done.10), channel_id=1, source_target_pairs={{0,384},{128,0},{256,128},{384,256},{1,385},{129,1},{257,129},{385... | collective-permute-start | bytes 56 | tf_op jit(solution)/shard_map/ppermute | solution.py:201
  38.4 1.7 %collective-permute-done.3 = s32[4]{0:T(128)S(1)} collective-permute-done((s32[4]{0:T(128)S(1)}, s32[4]{0:T(128)S(1)}, u32[]{:S(2)}, u32[]{:S(2)}) %collective-permute-start.3) | collective-permute-done | bytes 48 | tf_op jit(solution)/shard_map/ppermute | solution.py:201
  41.0 1.2 copy-done.5
  42.3 5.0 %project_own.1 = bf16[8,64,2048]{2,1,0:T(8,128)(2,1)S(1)} custom-call(s32[1]{0:T(128)} %bitcast.core_ref, bf16[2048,512]{1,0:T(8,128)(2,1)S(1)} %copy-done.1, bf16[512,1024]{1,0:T(8,128)(2,1)S(1)} %copy-done.5, bf16[8,64,2048]{2,1,0:T(8,128)(2,1)} %collective-permute-done.refs_0_), custom_call_target="tpu_custom_call" | custom-call | tf_op jit(solution)/shard_map/project_own/pallas_call | solution.py:159
  47.3 1.3 copy-done.2
  48.6 10.6 %all-to-all-done = bf16[8,2,64,512]{3,2,1,0:T(8,128)(2,1)S(1)} async-done(((bf16[8,2,64,512]{3,2,1,0:T(8,128)(2,1)}), bf16[8,2,64,512]{3,2,1,0:T(8,128)(2,1)S(1)}, u32[]{:S(2)}, u32[]{:S(2)}) %all-to-all-start) | async-done | bytes 1048608 | tf_op jit(solution)/shard_map/all_to_all | solution.py:192
  59.2 2.1 %pick_slots.1 = bf16[16,64,512]{2,1,0:T(8,128)(2,1)S(1)} custom-call(s32[16]{0:T(128)S(1)} %subtract_clamp_fusion.index_ref, bf16[16,64,512]{2,1,0:T(8,128)(2,1)S(1)} %bitcast.14), custom_call_target="tpu_custom_call" | custom-call | bytes 2097152 | tf_op jit(solution)/shard_map/pick_slots/pallas_call | solution.py:36
  61.3 1.0 copy-done.3
  62.2 3.5 %all-to-all-start.1 = ((bf16[4,256,512]{2,1,0:T(8,128)(2,1)}), bf16[4,256,512]{2,1,0:T(8,128)(2,1)S(1)}, u32[]{:S(2)}, u32[]{:S(2)}) async-start(bf16[4,256,512]{2,1,0:T(8,128)(2,1)} %bitcast.15), calls=%async_computation.2 | async-start | bytes 2097152 | tf_op jit(solution)/shard_map/all_to_all | solution.py:220
  66.0 14.0 %all-to-all-done.1 = bf16[4,256,512]{2,1,0:T(8,128)(2,1)S(1)} async-done(((bf16[4,256,512]{2,1,0:T(8,128)(2,1)}), bf16[4,256,512]{2,1,0:T(8,128)(2,1)S(1)}, u32[]{:S(2)}, u32[]{:S(2)}) %all-to-all-start.1) | async-done | bytes 1048608 | tf_op jit(solution)/shard_map/all_to_all | solution.py:220
  79.9 1.9 %down_projection.1 = bf16[16,64,128]{2,1,0:T(8,128)(2,1)S(1)} custom-call(s32[4]{0:T(128)S(1)} %iota_add_fusion.index_ref, bf16[2048,512]{1,0:T(8,128)(2,1)S(1)} %copy-done.1, bf16[16,64,512]{2,1,0:T(8,128)(2,1)S(1)} %bitcast.16), custom_call_target="tpu_custom_call" | custom-call | flops 134217728 | bytes 2621440 | tf_op jit(solution)/shard_map/down_projection/pallas_call | solution.py:65
  81.8 22.9 %all_to_all.20 = bf16[16,64,128]{2,1,0:T(8,128)(2,1)S(1)} all-to-all(bf16[16,64,128]{2,1,0:T(8,128)(2,1)S(1)} %down_projection.1), channel_id=1, replica_groups=mesh['x'=4,'y'=8,'z'=8,'core'=2] {'z','core'}, dimensions={0} | all-to-all | bytes 524288 | tf_op jit(solution)/shard_map/all_to_all | solution.py:223
  105.5 4.4 %all-to-all-start.3 = ((bf16[16,64,128]{2,1,0:T(8,128)(2,1)}), bf16[16,64,128]{2,1,0:T(8,128)(2,1)S(1)}, u32[]{:S(2)}, u32[]{:S(2)}) async-start(bf16[16,64,128]{2,1,0:T(8,128)(2,1)} %broadcast_in_dim.41), calls=%async_computation.4 | async-start | bytes 524288 | tf_op jit(solution)/shard_map/all_to_all | solution.py:178
  109.9 11.7 %all-to-all-done.3.down_ref = bf16[16,64,128]{2,1,0:T(8,128)(2,1)S(1)} async-done(((bf16[16,64,128]{2,1,0:T(8,128)(2,1)}), bf16[16,64,128]{2,1,0:T(8,128)(2,1)S(1)}, u32[]{:S(2)}, u32[]{:S(2)}) %all-to-all-start.3) | async-done | bytes 262176 | tf_op jit(solution)/shard_map/all_to_all | solution.py:178
  121.6 1.2 copy-done.6
  123.7 2.4 %add_update.1 = bf16[64,2048]{1,0:T(8,128)(2,1)} custom-call(s32[4]{0:T(128)S(1)} %select_reduce_fusion.1.slots_ref, s32[4]{0:T(128)S(1)} %copy-done.8, bf16[64,2048]{1,0:T(8,128)(2,1)S(1)} %copy-done.7, bf16[16,64,128]{2,1,0:T(8,128)(2,1)S(1)} %all-to-all-done.3.down_ref, bf16[64,64,128]{2,1,0:T(8,128)(2,1)S(1)} %copy-done.6), custom_call_target="tpu_custom_call" | custom-call | flops 16777216 | bytes 851968 | tf_op jit(solution)/shard_map/add_update/pallas_call | solution.py:109
  (39 shorter events, 3.6 us)
Async XLA Ops:
  7.4 102.5 %all-gather.2.cloned.1.call-start = ((), (), s32[]{:S(2)}) async-start(), calls=%async_computation.6 | async-start | bytes 1081344 | tf_op jit(solution)/shard_map/all_gather | solution.py:197
  9.4 1.6 %copy-start = (bf16[2048,512]{1,0:T(8,128)(2,1)S(1)}, bf16[2048,512]{1,0:T(8,128)(2,1)}, u32[]{:S(2)}) copy-start(bf16[2048,512]{1,0:T(8,128)(2,1)} %hidden_ref.2) | copy-start | bytes 6291460
  11.0 1.2 copy-start.4
  12.2 13.4 %copy-start.9 = (bf16[2,64,64]{2,1,0:T(8,128)(2,1)S(1)}, bf16[2,64,64]{2,1,0:T(8,128)(2,1)}, u32[]{:S(2)}) copy-start(bf16[2,64,64]{2,1,0:T(8,128)(2,1)} %param.10) | copy-start | bytes 49156
  16.7 13.2 %copy-start.10 = (s32[4]{0:T(128)S(1)}, s32[4]{0:T(128)}, u32[]{:S(2)}) copy-start(s32[4]{0:T(128)} %param.12) | copy-start | bytes 52
  16.7 24.1 %copy-start.11 = (s32[64]{0:T(128)S(1)}, s32[64]{0:T(128)}, u32[]{:S(2)}) copy-start(s32[64]{0:T(128)} %param.11) | copy-start | bytes 772
  16.7 24.3 %copy-start.1 = (bf16[2048,512]{1,0:T(8,128)(2,1)S(1)}, bf16[2048,512]{1,0:T(8,128)(2,1)}, u32[]{:S(2)}) copy-start(bf16[2048,512]{1,0:T(8,128)(2,1)} %hidden_ref.2) | copy-start | bytes 6291460
  16.7 24.3 %collective-permute-start = (bf16[8,64,2048]{2,1,0:T(8,128)(2,1)}, bf16[8,64,2048]{2,1,0:T(8,128)(2,1)}, u32[]{:S(2)}, u32[]{:S(2)}) collective-permute-start(bf16[8,64,2048]{2,1,0:T(8,128)(2,1)} %project_other.1), channel_id=1, source_target_pairs={{0,1},{1,0},{2,3},{3,2},{4,5},{5,4},{6,7},{7,6},{8,9},{9,8},{10,11... | collective-permute-start | bytes 6291464 | tf_op jit(solution)/shard_map/ppermute | solution.py:214
  26.3 32.8 %all-to-all-start = ((bf16[8,2,64,512]{3,2,1,0:T(8,128)(2,1)}), bf16[8,2,64,512]{3,2,1,0:T(8,128)(2,1)S(1)}, u32[]{:S(2)}, u32[]{:S(2)}) async-start(bf16[8,2,64,512]{3,2,1,0:T(8,128)(2,1)} %broadcast_in_dim.38), calls=%async_computation | async-start | bytes 2097152 | tf_op jit(solution)/shard_map/all_to_all | solution.py:192
  29.9 91.7 %reduce-scatter.2.cloned.1.call-start = ((), (), s32[]{:S(2)}) async-start(), calls=%async_computation.5 | async-start | bytes 2359296 | tf_op jit(solution)/shard_map/reduce_scatter | solution.py:217
  29.9 8.5 %collective-permute-start.1 = (s32[4]{0:T(128)S(1)}, s32[4]{0:T(128)S(1)}, u32[]{:S(2)}, u32[]{:S(2)}) collective-permute-start(s32[4]{0:T(128)S(1)} %copy-done.10), channel_id=1, source_target_pairs={{0,128},{128,256},{256,384},{384,0},{1,129},{129,257},{257,385},{3... | collective-permute-start | bytes 56 | tf_op jit(solution)/shard_map/ppermute | solution.py:201
  31.9 6.6 %collective-permute-start.2 = (s32[4]{0:T(128)S(1)}, s32[4]{0:T(128)S(1)}, u32[]{:S(2)}, u32[]{:S(2)}) collective-permute-start(s32[4]{0:T(128)S(1)} %copy-done.10), channel_id=1, source_target_pairs={{0,256},{128,384},{256,0},{384,128},{1,257},{129,385},{257,1},{385... | collective-permute-start | bytes 56 | tf_op jit(solution)/shard_map/ppermute | solution.py:201
  35.3 4.8 %collective-permute-start.3 = (s32[4]{0:T(128)S(1)}, s32[4]{0:T(128)S(1)}, u32[]{:S(2)}, u32[]{:S(2)}) collective-permute-start(s32[4]{0:T(128)S(1)} %copy-done.10), channel_id=1, source_target_pairs={{0,384},{128,0},{256,128},{384,256},{1,385},{129,1},{257,129},{385... | collective-permute-start | bytes 56 | tf_op jit(solution)/shard_map/ppermute | solution.py:201
  41.0 1.2 copy-start.5
  47.3 1.3 copy-start.2
  61.3 1.0 copy-start.3
  62.2 17.7 %all-to-all-start.1 = ((bf16[4,256,512]{2,1,0:T(8,128)(2,1)}), bf16[4,256,512]{2,1,0:T(8,128)(2,1)S(1)}, u32[]{:S(2)}, u32[]{:S(2)}) async-start(bf16[4,256,512]{2,1,0:T(8,128)(2,1)} %bitcast.15), calls=%async_computation.2 | async-start | bytes 2097152 | tf_op jit(solution)/shard_map/all_to_all | solution.py:220
  79.9 41.7 %copy-start.8 = (s32[4]{0:T(128)S(1)}, s32[4]{0:T(128)}, u32[]{:S(2)}) copy-start(s32[4]{0:T(128)} %lengths_ref.1) | copy-start | bytes 52
  105.5 16.1 %all-to-all-start.3 = ((bf16[16,64,128]{2,1,0:T(8,128)(2,1)}), bf16[16,64,128]{2,1,0:T(8,128)(2,1)S(1)}, u32[]{:S(2)}, u32[]{:S(2)}) async-start(bf16[16,64,128]{2,1,0:T(8,128)(2,1)} %broadcast_in_dim.41), calls=%async_computation.4 | async-start | bytes 524288 | tf_op jit(solution)/shard_map/all_to_all | solution.py:178
  121.6 1.2 copy-start.6
  122.8 0.9 copy-start.7
Sparse Core Ops, SparseCore 0:
  26.4 79.4 all-gather.1
Sparse Core Ops, SparseCore 1:
  59.3 42.2 reduce-scatter.1

commit v2 on v0

v2 whole, which is shorter than its diff:
```python
import functools

import jax
import jax.numpy as jnp
from jax import lax
from jax.experimental import pallas as pl
from jax.experimental.pallas import tpu as pltpu
from jax.sharding import Mesh
from jax.sharding import PartitionSpec as P

ADAPTER_SCALE = 2.0
X, CORES = 4, 2
DP, TENSOR = ("x", "y"), ("z", "core")
LANES = 128
KERNEL_VMEM = 8 << 20
PROJECT_VMEM, PROJECT_ROWS, PROJECT_CHIPS = 60 << 20, 1024, 4


def cost(flops, size):
    return pl.CostEstimate(flops=flops, bytes_accessed=2 * size, transcendentals=0)


def copies_kernel(down_ref, up_ref, out_ref, stage, ups, in_sems, sems):
    slots, rank, features = down_ref.shape
    packed = stage.shape[0] - slots * rank
    first = [
        pltpu.make_async_copy(down_ref.at[j], stage.at[pl.ds(j * rank, rank)], in_sems.at[j])
        for j in range(slots)
    ]
    first.append(pltpu.make_async_copy(up_ref, ups, in_sems.at[slots]))
    copies = [
        pltpu.make_async_copy(stage, out_ref.at[i], sems.at[i]) for i in range(out_ref.shape[0])
    ]
    for copy in first:
        copy.start()
    for copy in first:
        copy.wait()
    both = jnp.concatenate([ups[j] for j in range(slots)], axis=1)
    for q in range(features // LANES):
        block = both[q * packed : (q + 1) * packed]
        stage[slots * rank :, q * LANES : (q + 1) * LANES] = block
    for copy in copies:
        copy.start()
    for copy in copies:
        copy.wait()


def factor_copies(down, up, count):
    slots, rank, features = down.shape
    rows = slots * rank + rank * LANES // features
    return pl.pallas_call(
        copies_kernel,
        out_shape=jax.ShapeDtypeStruct((count, rows, features), down.dtype),
        in_specs=[pl.BlockSpec(memory_space=pl.ANY)] * 2,
        out_specs=pl.BlockSpec(memory_space=pl.ANY),
        scratch_shapes=[
            pltpu.VMEM((rows, features), down.dtype),
            pltpu.VMEM(up.shape, up.dtype),
            pltpu.SemaphoreType.DMA((slots + 1,)),
            pltpu.SemaphoreType.DMA((count,)),
        ],
        cost_estimate=cost(0, count * rows * features),
        compiler_params=pltpu.CompilerParams(vmem_limit_bytes=PROJECT_VMEM),
        name="factor_copies",
    )(down, up)


def project_kernel(hidden_ref, other_ref, matrix_ref, other_matrix_ref, *refs):
    *out_refs, own, own_other = refs
    columns = out_refs[0].shape[0]
    chips, span = len(out_refs), CORES * columns

    @pl.when(pl.program_id(0) == 0)
    def _():
        here, upper = lax.axis_index("z"), lax.axis_index("core") == 1
        low = lax.broadcasted_iota(jnp.int32, (matrix_ref.shape[0], span), 1) < columns
        for source, chosen in ((matrix_ref, own), (other_matrix_ref, own_other)):
            for k in range(0, chips, 2):
                pair = []
                for i in range(2):
                    start = pl.multiple_of(lax.rem(here + k + i, chips) * span, span)
                    block = source[:, pl.ds(start, span)]
                    turned = jnp.concatenate([block[:, columns:], block[:, :columns]], axis=1)
                    pair.append(jnp.where(upper == (i == 1), block, turned))
                chosen[:, k * columns : (k + 2) * columns] = jnp.where(low, pair[0], pair[1])

    for first in range(0, chips, PROJECT_CHIPS):
        last = min(first + PROJECT_CHIPS, chips)
        lanes = slice(first * columns, last * columns)
        product = jnp.dot(
            hidden_ref[...], own[:, lanes], preferred_element_type=jnp.float32
        ) + jnp.dot(other_ref[...], own_other[:, lanes], preferred_element_type=jnp.float32)
        product = product.astype(out_refs[0].dtype).T
        for k in range(first, last):
            out_refs[k][...] = product[(k - first) * columns : (k - first + 1) * columns]


def project(hidden, other, matrix, other_matrix, columns):
    tokens, features = hidden.shape
    width = matrix.shape[1]
    chips = width // (CORES * columns)
    rows = min(PROJECT_ROWS, tokens)
    row_spec = pl.BlockSpec((rows, features), lambda t: (t, 0))
    matrix_spec = pl.BlockSpec(matrix.shape, lambda t: (0, 0))
    return pl.pallas_call(
        project_kernel,
        grid=(tokens // rows,),
        out_shape=[jax.ShapeDtypeStruct((columns, tokens), hidden.dtype)] * chips,
        in_specs=[row_spec] * 2 + [matrix_spec] * 2,
        out_specs=[pl.BlockSpec((columns, rows), lambda t: (0, t))] * chips,
        scratch_shapes=[pltpu.VMEM((features, chips * columns), matrix.dtype)] * 2,
        cost_estimate=cost(
            2 * tokens * features * width,
            2 * hidden.size + 2 * matrix.size + tokens * chips * columns,
        ),
        compiler_params=pltpu.CompilerParams(vmem_limit_bytes=PROJECT_VMEM),
        name="project",
    )(hidden, other, matrix, other_matrix)


def add(a, b):
    return (a.astype(jnp.float32) + b.astype(jnp.float32)).astype(a.dtype)


def along(axis, value, step):
    n = lax.axis_size(axis)
    return lax.ppermute(value, axis, [(i, (i + step) % n) for i in range(n)])


def pick_kernel(slots, rank, index_ref, row_ref, out_ref):
    dests, _, features = out_ref.shape
    packed = rank * LANES // features
    rollouts = index_ref.shape[0] // dests
    half = LANES // 2
    low = lax.broadcasted_iota(jnp.int32, (packed, LANES), 1) < half
    for d in range(dests):
        ups = []
        for r in range(rollouts):
            index = index_ref[d * rollouts + r]
            owner, place = index // slots, index % slots
            start = pl.multiple_of(place * rank, rank)
            out_ref[d, r * rank : (r + 1) * rank] = row_ref[owner, pl.ds(start, rank)]
            ups.append((row_ref[owner, slots * rank :], place))
        for p in range(rollouts // 2):
            for q in range(features // LANES):
                lanes = slice(q * LANES, (q + 1) * LANES)
                pair = []
                for h in range(2):
                    block, place = ups[2 * p + h]
                    block = block[:, lanes]
                    turned = jnp.concatenate([block[:, half:], block[:, :half]], axis=1)
                    pair.append(jnp.where(place == h, block, turned))
                at = rollouts * rank + p * packed
                out_ref[d, at : at + packed, lanes] = jnp.where(low, pair[0], pair[1])


def pick(index, row, dests, slots, rank):
    features = row.shape[2]
    packed = rank * LANES // features
    rollouts = index.shape[0] // dests
    rows = rollouts * rank + rollouts // 2 * packed
    return pl.pallas_call(
        functools.partial(pick_kernel, slots, rank),
        out_shape=jax.ShapeDtypeStruct((dests, rows, features), row.dtype),
        in_specs=[
            pl.BlockSpec(memory_space=pltpu.SMEM),
            pl.BlockSpec(memory_space=pltpu.VMEM),
        ],
        out_specs=pl.BlockSpec(memory_space=pltpu.VMEM),
        cost_estimate=cost(0, 2 * dests * rows * features),
        compiler_params=pltpu.CompilerParams(vmem_limit_bytes=KERNEL_VMEM),
        name="pick_factors",
    )(index, row)


def down_kernel(own_row_ref, hidden_ref, factor_ref, out_ref):
    members, rank, chunk = out_ref.shape
    count = own_row_ref.shape[0]
    per = members // count
    length = per * chunk
    for r in range(count):
        product = lax.dot_general(
            hidden_ref[r * length : (r + 1) * length],
            factor_ref[own_row_ref[r], r * rank : (r + 1) * rank],
            (((1,), (1,)), ((), ())),
            preferred_element_type=jnp.float32,
        ).T.astype(out_ref.dtype)
        for i in range(per):
            out_ref[r * per + i] = product[:, i * chunk : (i + 1) * chunk]


def down_projection(own_row, hidden, factors, members, rank):
    tokens, features = hidden.shape
    return pl.pallas_call(
        down_kernel,
        out_shape=jax.ShapeDtypeStruct((members, rank, tokens // members), hidden.dtype),
        in_specs=[pl.BlockSpec(memory_space=pltpu.SMEM)]
        + [pl.BlockSpec(memory_space=pltpu.VMEM)] * 2,
        out_specs=pl.BlockSpec(memory_space=pltpu.VMEM),
        cost_estimate=cost(2 * tokens * features * rank, hidden.size + tokens * rank),
        compiler_params=pltpu.CompilerParams(vmem_limit_bytes=KERNEL_VMEM),
        name="down_projection",
    )(own_row, hidden, factors)


def sum_kernel(parts_ref, out_ref):
    total = parts_ref[0].astype(jnp.float32)
    for i in range(1, parts_ref.shape[0]):
        total += parts_ref[i].astype(jnp.float32)
    total = total.astype(out_ref.dtype)
    for i in range(out_ref.shape[0]):
        out_ref[i] = total


def sum_copies(parts):
    return pl.pallas_call(
        sum_kernel,
        out_shape=jax.ShapeDtypeStruct(parts.shape, parts.dtype),
        in_specs=[pl.BlockSpec(memory_space=pltpu.VMEM)],
        out_specs=pl.BlockSpec(memory_space=pltpu.VMEM),
        cost_estimate=cost(parts.size, 2 * parts.size),
        compiler_params=pltpu.CompilerParams(vmem_limit_bytes=KERNEL_VMEM),
        name="sum_parts",
    )(parts)


def final_kernel(own_row_ref, lengths_ref, *refs):
    *base_refs, down_ref, factor_ref, out_ref = refs
    columns, tokens = out_ref.shape
    members, rank, chunk = down_ref.shape
    features = factor_ref.shape[2]
    packed = rank * LANES // features
    count = own_row_ref.shape[0]
    per, length = members // count, tokens // count
    for r in range(count):
        at = count * rank + r // 2 * packed
        block = factor_ref[own_row_ref[r], at : at + packed, :]
        first = r % 2 * columns
        up = jnp.concatenate(
            [
                block[:, q * LANES + first : q * LANES + first + columns]
                for q in range(features // LANES)
            ],
            axis=0,
        )
        down = jnp.concatenate([down_ref[r * per + i] for i in range(per)], axis=1)
        update = lax.dot_general(
            up, down, (((0,), (0,)), ((), ())), preferred_element_type=jnp.float32
        )
        span = slice(r * length, (r + 1) * length)
        total = ADAPTER_SCALE * update
        for base_ref in base_refs:
            total += base_ref[:, span].astype(jnp.float32)
        position = lax.broadcasted_iota(jnp.int32, (columns, length), 1)
        out_ref[:, span] = jnp.where(position < lengths_ref[r], total, 0.0).astype(out_ref.dtype)


def final(own_row, lengths, base, down, factors):
    columns, tokens = base[0].shape
    rank = down.shape[1]
    return pl.pallas_call(
        final_kernel,
        out_shape=jax.ShapeDtypeStruct(base[0].shape, base[0].dtype),
        in_specs=[pl.BlockSpec(memory_space=pltpu.SMEM)] * 2
        + [pl.BlockSpec(memory_space=pltpu.VMEM)] * (len(base) + 2),
        out_specs=pl.BlockSpec(memory_space=pltpu.VMEM),
        cost_estimate=cost(2 * tokens * columns * rank, 4 * base[0].size + down.size),
        compiler_params=pltpu.CompilerParams(vmem_limit_bytes=KERNEL_VMEM),
        name="add_update",
    )(own_row, lengths, *base, down, factors)


def on_device(
    hidden, value_matrix, adapter_down_store, adapter_up_store, adapter_slot, rollout_adapter, lengths
):
    members = lax.axis_size(TENSOR)
    rollouts = rollout_adapter.shape[0]
    slots_here, rank, _ = adapter_up_store.shape
    row_slots = slots_here * lax.axis_size("y")

    other = along("core", hidden, 1)
    other_matrix = along("core", value_matrix, 1)
    copies = factor_copies(
        jnp.swapaxes(adapter_down_store, 1, 2), adapter_up_store, lax.axis_size("y")
    )
    row = lax.all_to_all(copies, "y", 0, 0)

    parts = project(hidden, other, value_matrix, other_matrix, adapter_up_store.shape[2])
    far = len(parts) // 2
    ahead, behind = parts[far], parts[far + 1]
    for k in range(far - 1, -1, -1):
        ahead = along("z", ahead, 1)
        if k:
            ahead = add(ahead, parts[k])
    for k in range(far + 2, len(parts) + 1):
        behind = along("z", behind, -1)
        if k < len(parts):
            behind = add(behind, parts[k])
    base = (parts[0], ahead, behind)

    here = lax.axis_index("x")
    mine = jnp.arange(X, dtype=jnp.int32)[:, None] == here
    wanted = lax.psum(jnp.where(mine, rollout_adapter[None, :], 0), "x").reshape(-1)
    table = jnp.arange(adapter_slot.shape[0], dtype=jnp.int32)
    matches = wanted[:, None] == table[None, :]
    slots = jnp.sum(jnp.where(matches, adapter_slot[None, :], 0), axis=1)
    local = jnp.clip(slots - here * row_slots, 0, row_slots - 1)
    own_row = lax.dynamic_slice_in_dim(slots, here * rollouts, rollouts) // row_slots
    local, own_row = lax.optimization_barrier((local, own_row))

    sent = pick(local, row, X, slots_here, rank)
    factors = lax.all_to_all(sent, "x", 0, 0)
    down = down_projection(own_row, hidden, factors, members, rank)
    down = lax.all_to_all(down, TENSOR, 0, 0)
    down = sum_copies(down)
    down = lax.all_to_all(down, TENSOR, 0, 0)
    return final(own_row, lengths, base, down, factors).T


def solution(mesh):
    dp, tensor = mesh.devices.shape
    fine = Mesh(mesh.devices.reshape(X, dp // X, tensor // CORES, CORES), (*DP, *TENSOR))
    in_specs = (
        P(DP, TENSOR),
        P(TENSOR, None),
        P(DP, TENSOR, None),
        P(DP, None, TENSOR),
        P(),
        P(DP),
        P(DP),
    )
    return jax.shard_map(
        on_device, mesh=fine, in_specs=in_specs, out_specs=P(DP, TENSOR), check_vma=False
    )
```

time: 234 us -> 115 us (0.49)
  waiting for transfers between devices: 156 us -> 27.9 us
  starting transfers between devices: 0.09 us -> 58.5 us
  blocking collectives: 43.3 us -> 5.59 us
  matrix products: 15.6 us -> 0 us
  Pallas kernels: 0 us -> 15.1 us
  between operations: 14.9 us -> 0.27 us
  other arithmetic: 1.24 us -> 5.13 us
    psum x1 -> x0, waiting for transfers between devices: 114 us -> none  [on_device(): down_total = lax.psum(partial_down.astype(jnp.bfloat16), 'tensor')]
    all_gather x1 -> x0, blocking collectives: 43.3 us -> none  [on_device(): up_fragment = lax.all_gather(adapter_up_store, 'dp', axis=0, tiled=True)]
    all_gather x1 -> x0, waiting for transfers between devices: 41.8 us -> none  [on_device(): down_fragment = lax.all_gather(adapter_down_store, 'dp', axis=0, tiled=True)]
    ppermute x0 -> x9, starting transfers between devices: none -> 40.8 us  [along(): return lax.ppermute(value, axis, [(i, (i + step) % n) for i in range(n)])]
    all_to_all x0 -> x4, starting transfers between devices: none -> 17.7 us  [the longest x2 10.5 us: on_device(): down = lax.all_to_all(down, TENSOR, 0, 0)]
    dot_general x5 -> x0, matrix products: 15.6 us -> none  [the longest x1 6.7 us: on_device(): jnp.einsum('rs,sdk->rdk', picker, down_fragment, preferred_element_type=j...]
    pallas_call x0 -> x6, Pallas kernels: none -> 15.1 us  [the longest x1 6.86 us: project(): pl.pallas_call(project_kernel, grid=(tokens // rows,), out_shape=[jax.Sha...]
    all_to_all x0 -> x4, waiting for transfers between devices: none -> 15 us  [the longest x1 11.8 us: on_device(): row = lax.all_to_all(copies, 'y', 0, 0)]
  transfers between devices with their start and end apart: 3 -> 13, of which waited for: 2 -> 4; matrix products, arithmetic and copies ran while one was open for 7% -> 5% of each run, Pallas kernels for 0% -> 12%
where the time goes in v2:
time: 115 us; the launch traced here: 114 us
  starting transfers between devices  58.5 us (51%)
  waiting for transfers between devices  27.9 us (24%)
  Pallas kernels  15.1 us (13%)
  blocking collectives  5.59 us (5%)
  other arithmetic  5.13 us (4%)
  local copies, waits for them, and re-layouts  1.45 us (1%)
    ppermute x9, starting transfers between devices, along(): return lax.ppermute(value, axis, [(i, (i + step) % n) for i in range(n)])  40.8 us
    ppermute x9, waiting for transfers between devices, along(): return lax.ppermute(value, axis, [(i, (i + step) % n) for i in range(n)])  12.9 us
    all_to_all x1, waiting for transfers between devices, on_device(): row = lax.all_to_all(copies, 'y', 0, 0)  11.8 us
    all_to_all x2, starting transfers between devices, on_device(): down = lax.all_to_all(down, TENSOR, 0, 0)  10.5 us
    pallas_call x1, Pallas kernels, project(): pl.pallas_call(project_kernel, grid=(tokens // rows,), out_shape=[jax.Sha...  6.86 us
    psum x1, blocking collectives, on_device(): lax.psum(jnp.where(mine, rollout_adapter[None, :], 0), 'x').reshape(-1)  5.59 us
    convert_element_type x5, other arithmetic, add(): return (a.astype(jnp.float32) + b.astype(jnp.float32)).astype(a.dtype)  4.77 us
    all_to_all x1, starting transfers between devices, on_device(): factors = lax.all_to_all(sent, 'x', 0, 0)  3.66 us
  transfers between devices with their start and end apart: 13, of which 4 were waited for; matrix products, arithmetic and copies ran while one was open for 5% of the time, Pallas kernels for 12%

profile of v2, /device:TPU:1, one launch (start us, length us, event | category | flops | bytes accessed | tf_op | source)
XLA Modules:
  0.0 114.0 jit_solution(6657231706817127380)
XLA Ops:
  0.0 8.8 %collective-permute-start = (bf16[2048,512]{1,0:T(8,128)(2,1)}, bf16[2048,512]{1,0:T(8,128)(2,1)S(1)}, u32[]{:S(2)}, u32[]{:S(2)}) collective-permute-start(bf16[2048,512]{1,0:T(8,128)(2,1)} %hidden_ref.3), channel_id=1, source_target_pairs={{0,1},{1,0},{2,3},{3,2},{4,5},{5,4},{6,7},{7,6},{8,9},{9,8},{10,11... | collective-permute-start | bytes 6291464 | tf_op jit(solution)/shard_map/ppermute | solution.py:127
  8.8 2.1 %factor_copies.1 = bf16[8,144,512]{2,1,0:T(8,128)(2,1)} custom-call(bf16[2,64,512]{2,1,0:T(8,128)(2,1)} %bitcast.2, bf16[2,64,64]{2,1,0:T(8,128)(2,1)} %up_ref.1), custom_call_target="tpu_custom_call" | custom-call | bytes 1179648 | tf_op jit(solution)/shard_map/factor_copies/pallas_call | solution.py:51
  10.9 3.6 %all-to-all-start = ((bf16[8,144,512]{2,1,0:T(8,128)(2,1)}), bf16[8,144,512]{2,1,0:T(8,128)(2,1)S(1)}, u32[]{:S(2)}, u32[]{:S(2)}) async-start(bf16[8,144,512]{2,1,0:T(8,128)(2,1)} %factor_copies.1), calls=%async_computation | async-start | bytes 2359296 | tf_op jit(solution)/shard_map/all_to_all | solution.py:286
  14.5 1.9 %collective-permute-start.1 = (bf16[512,1024]{1,0:T(8,128)(2,1)}, bf16[512,1024]{1,0:T(8,128)(2,1)}, u32[]{:S(2)}, u32[]{:S(2)}) collective-permute-start(bf16[512,1024]{1,0:T(8,128)(2,1)} %matrix_ref.1), channel_id=1, source_target_pairs={{0,1},{1,0},{2,3},{3,2},{4,5},{5,4},{6,7},{7,6},{8,9},{9,8},{10,11... | collective-permute-start | bytes 3145736 | tf_op jit(solution)/shard_map/ppermute | solution.py:127
  16.6 5.6 %psum.7 = s32[16]{0:T(128)S(1)} all-reduce(s32[16]{0:T(128)S(1)} %eq.28), channel_id=1, replica_groups=mesh['x'=4,'y'=8,'z'=8,'core'=2] {'x'}, use_global_device_ids=true, to_apply=%region_0.1 | all-reduce | flops 16 | bytes 128 | tf_op jit(solution)/shard_map/psum | solution.py:303
  23.7 6.9 %project.1 = (bf16[64,2048]{1,0:T(8,128)(2,1)}, bf16[64,2048]{1,0:T(8,128)(2,1)}, bf16[64,2048]{1,0:T(8,128)(2,1)}, bf16[64,2048]{1,0:T(8,128)(2,1)}, bf16[64,20...) custom-call(bf16[2048,512]{1,0:T(8,128)(2,1)} %hidden_ref.3, ...), custom_call_target="tpu_custom_call" | custom-call | flops 2147483648 | bytes 8388608 | tf_op jit(solution)/shard_map/project/pallas_call | solution.py:105
  30.6 4.0 %collective-permute-start.2 = (bf16[64,2048]{1,0:T(8,128)(2,1)}, bf16[64,2048]{1,0:T(8,128)(2,1)}, u32[]{:S(2)}, u32[]{:S(2)}) collective-permute-start(bf16[64,2048]{1,0:T(8,128)(2,1)} %get-tuple-element.17), channel_id=1, source_target_pairs={{0,2},{2,4},{4,6},{6,8},{8,10},{10,12},{12,14},{14,0},{1,3},{3,5},... | collective-permute-start | bytes 786440 | tf_op jit(solution)/shard_map/ppermute | solution.py:127
  34.7 11.8 %all-to-all-done.row_ref = bf16[8,144,512]{2,1,0:T(8,128)(2,1)S(1)} async-done(((bf16[8,144,512]{2,1,0:T(8,128)(2,1)}), bf16[8,144,512]{2,1,0:T(8,128)(2,1)S(1)}, u32[]{:S(2)}, u32[]{:S(2)}) %all-to-all-start) | async-done | bytes 1179680 | tf_op jit(solution)/shard_map/all_to_all | solution.py:286
  46.5 1.8 %pick_factors.1 = bf16[4,288,512]{2,1,0:T(8,128)(2,1)} custom-call(s32[16]{0:T(128)S(1)} %subtract_clamp_fusion.index_ref, bf16[8,144,512]{2,1,0:T(8,128)(2,1)S(1)} %all-to-all-done.row_ref), custom_call_target="tpu_custom_call" | custom-call | bytes 2359296 | tf_op jit(solution)/shard_map/pick_factors/pallas_call | solution.py:162
  48.3 3.7 %all-to-all-start.1 = ((bf16[4,288,512]{2,1,0:T(8,128)(2,1)}), bf16[4,288,512]{2,1,0:T(8,128)(2,1)S(1)}, u32[]{:S(2)}, u32[]{:S(2)}) async-start(bf16[4,288,512]{2,1,0:T(8,128)(2,1)} %pick_factors.1), calls=%async_computation.1 | async-start | bytes 2359296 | tf_op jit(solution)/shard_map/all_to_all | solution.py:312
  51.9 9.1 %collective-permute-start.6 = (bf16[64,2048]{1,0:T(8,128)(2,1)}, bf16[64,2048]{1,0:T(8,128)(2,1)S(1)}, u32[]{:S(2)}, u32[]{:S(2)}) collective-permute-start(bf16[64,2048]{1,0:T(8,128)(2,1)} %get-tuple-element.21), channel_id=1, source_target_pairs={{0,14},{2,0},{4,2},{6,4},{8,6},{10,8},{12,10},{14,12},{1,15},{3,1}... | collective-permute-start | bytes 786440 | tf_op jit(solution)/shard_map/ppermute | solution.py:127
  61.0 1.8 %add_convert_fusion.4 = bf16[64,2048]{1,0:T(8,128)(2,1)} fusion(bf16[64,2048]{1,0:T(8,128)(2,1)} %get-tuple-element.18, bf16[64,2048]{1,0:T(8,128)(2,1)} %collective-permute-done.2), kind=kLoop, calls=%fused_computation.4 | loop fusion | flops 524288 | bytes 786432 | tf_op jit(solution)/shard_map/convert_element_type | solution.py:122
  62.8 1.9 %collective-permute-start.3 = (bf16[64,2048]{1,0:T(8,128)(2,1)}, bf16[64,2048]{1,0:T(8,128)(2,1)}, u32[]{:S(2)}, u32[]{:S(2)}) collective-permute-start(bf16[64,2048]{1,0:T(8,128)(2,1)} %add_convert_fusion.4), channel_id=1, source_target_pairs={{0,2},{2,4},{4,6},{6,8},{8,10},{10,12},{12,14},{14,0},{1,3},{3,5},... | collective-permute-start | bytes 786440 | tf_op jit(solution)/shard_map/ppermute | solution.py:127
  64.7 1.5 %collective-permute-done.6 = bf16[64,2048]{1,0:T(8,128)(2,1)S(1)} collective-permute-done((bf16[64,2048]{1,0:T(8,128)(2,1)}, bf16[64,2048]{1,0:T(8,128)(2,1)S(1)}, u32[]{:S(2)}, u32[]{:S(2)}) %collective-permute-start.6) | collective-permute-done | bytes 262176 | tf_op jit(solution)/shard_map/ppermute | solution.py:127
  67.0 5.3 %collective-permute-start.7 = (bf16[64,2048]{1,0:T(8,128)(2,1)}, bf16[64,2048]{1,0:T(8,128)(2,1)}, u32[]{:S(2)}, u32[]{:S(2)}) collective-permute-start(bf16[64,2048]{1,0:T(8,128)(2,1)} %add_convert_fusion.1), channel_id=1, source_target_pairs={{0,14},{2,0},{4,2},{6,4},{8,6},{10,8},{12,10},{14,12},{1,15},{3,1}... | collective-permute-start | bytes 786440 | tf_op jit(solution)/shard_map/ppermute | solution.py:127
  72.3 2.0 %down_projection.1 = bf16[16,64,128]{2,1,0:T(8,128)(2,1)} custom-call(s32[4]{0:T(128)S(1)} %and_select_fusion.own_row_ref, bf16[2048,512]{1,0:T(8,128)(2,1)S(1)} %copy-done, bf16[4,288,512]{2,1,0:T(8,128)(2,1)S(1)} %all-to-all-done.1.factor_ref.refs_4_), custom_call_target="tpu_custom_call" | custom-call | flops 134217728 | bytes 2359296 | tf_op jit(solution)/shard_map/down_projection/pallas_call | solution.py:194
  74.4 5.9 %all-to-all-start.2 = ((bf16[16,64,128]{2,1,0:T(8,128)(2,1)}), bf16[16,64,128]{2,1,0:T(8,128)(2,1)S(1)}, u32[]{:S(2)}, u32[]{:S(2)}) async-start(bf16[16,64,128]{2,1,0:T(8,128)(2,1)} %down_projection.1), calls=%async_computation.2 | async-start | bytes 524288 | tf_op jit(solution)/shard_map/all_to_all | solution.py:314
  81.4 3.3 %collective-permute-start.4 = (bf16[64,2048]{1,0:T(8,128)(2,1)S(1)}, bf16[64,2048]{1,0:T(8,128)(2,1)S(1)}, u32[]{:S(2)}, u32[]{:S(2)}) collective-permute-start(bf16[64,2048]{1,0:T(8,128)(2,1)S(1)} %add_convert_fusion.3), channel_id=1, source_target_pairs={{0,2},{2,4},{4,6},{6,8},{8,10},{10,12},{12,14},{14,0},{1,3},{3,5},... | collective-permute-start | bytes 786440 | tf_op jit(solution)/shard_map/ppermute | solution.py:127
  85.8 3.2 %collective-permute-start.8 = (bf16[64,2048]{1,0:T(8,128)(2,1)S(1)}, bf16[64,2048]{1,0:T(8,128)(2,1)S(1)}, u32[]{:S(2)}, u32[]{:S(2)}) collective-permute-start(bf16[64,2048]{1,0:T(8,128)(2,1)S(1)} %add_convert_fusion), channel_id=1, source_target_pairs={{0,14},{2,0},{4,2},{6,4},{8,6},{10,8},{12,10},{14,12},{1,15},{3,1}... | collective-permute-start | bytes 786440 | tf_op jit(solution)/shard_map/ppermute | solution.py:127
  89.0 3.2 %all-to-all-done.2.parts_ref = bf16[16,64,128]{2,1,0:T(8,128)(2,1)S(1)} async-done(((bf16[16,64,128]{2,1,0:T(8,128)(2,1)}), bf16[16,64,128]{2,1,0:T(8,128)(2,1)S(1)}, u32[]{:S(2)}, u32[]{:S(2)}) %all-to-all-start.2) | async-done | bytes 262176 | tf_op jit(solution)/shard_map/all_to_all | solution.py:314
  93.0 4.6 %all-to-all-start.3 = ((bf16[16,64,128]{2,1,0:T(8,128)(2,1)}), bf16[16,64,128]{2,1,0:T(8,128)(2,1)S(1)}, u32[]{:S(2)}, u32[]{:S(2)}) async-start(bf16[16,64,128]{2,1,0:T(8,128)(2,1)} %sum_parts.1), calls=%async_computation.3 | async-start | bytes 524288 | tf_op jit(solution)/shard_map/all_to_all | solution.py:316
  97.6 3.3 %collective-permute-start.5 = (bf16[64,2048]{1,0:T(8,128)(2,1)S(1)}, bf16[64,2048]{1,0:T(8,128)(2,1)S(1)}, u32[]{:S(2)}, u32[]{:S(2)}) collective-permute-start(bf16[64,2048]{1,0:T(8,128)(2,1)S(1)} %add_convert_fusion.2), channel_id=1, source_target_pairs={{0,2},{2,4},{4,6},{6,8},{8,10},{10,12},{12,14},{14,0},{1,3},{3,5},... | collective-permute-start | bytes 786440 | tf_op jit(solution)/shard_map/ppermute | solution.py:127
  101.0 11.4 %collective-permute-done.5.refs_1_ = bf16[64,2048]{1,0:T(8,128)(2,1)S(1)} collective-permute-done((bf16[64,2048]{1,0:T(8,128)(2,1)S(1)}, bf16[64,2048]{1,0:T(8,128)(2,1)S(1)}, u32[]{:S(2)}, u32[]{:S(2)}) %collective-permute-start.5) | collective-permute-done | bytes 262176 | tf_op jit(solution)/shard_map/ppermute | solution.py:127
  112.4 1.6 %add_update.1 = bf16[64,2048]{1,0:T(8,128)(2,1)} custom-call(s32[4]{0:T(128)S(1)} %and_select_fusion.own_row_ref, s32[4]{0:T(128)S(1)} %copy-done.2, bf16[64,2048]{1,0:T(8,128)(2,1)S(1)} %copy-done.1, bf16[64,2048]{1,0:T(8,128)(2,1)S(1)} %collective-permute-done.5.refs_1_, bf16[64,2048]{1,0:T(8,128)(2,1)S(1)} %collective-permute-done.8.refs_2_, ...), custom_call_target="tpu_custom_call" | custom-call | flops 16777216 | bytes 1310720 | tf_op jit(solution)/shard_map/add_update/pallas_call | solution.py:261
  (40 shorter events, 5.5 us)
Async XLA Ops:
  0.0 22.4 %collective-permute-start = (bf16[2048,512]{1,0:T(8,128)(2,1)}, bf16[2048,512]{1,0:T(8,128)(2,1)S(1)}, u32[]{:S(2)}, u32[]{:S(2)}) collective-permute-start(bf16[2048,512]{1,0:T(8,128)(2,1)} %hidden_ref.3), channel_id=1, source_target_pairs={{0,1},{1,0},{2,3},{3,2},{4,5},{5,4},{6,7},{7,6},{8,9},{9,8},{10,11... | collective-permute-start | bytes 6291464 | tf_op jit(solution)/shard_map/ppermute | solution.py:127
  10.9 5.6 %copy-start.7 = (s32[4]{0:T(128)S(1)}, s32[4]{0:T(128)}, u32[]{:S(2)}) copy-start(s32[4]{0:T(128)} %param.12) | copy-start | bytes 52
  10.9 11.3 %copy-start.9 = (s32[64]{0:T(128)S(1)}, s32[64]{0:T(128)}, u32[]{:S(2)}) copy-start(s32[64]{0:T(128)} %param.11) | copy-start | bytes 772
  10.9 35.6 %all-to-all-start = ((bf16[8,144,512]{2,1,0:T(8,128)(2,1)}), bf16[8,144,512]{2,1,0:T(8,128)(2,1)S(1)}, u32[]{:S(2)}, u32[]{:S(2)}) async-start(bf16[8,144,512]{2,1,0:T(8,128)(2,1)} %factor_copies.1), calls=%async_computation | async-start | bytes 2359296 | tf_op jit(solution)/shard_map/all_to_all | solution.py:286
  14.5 7.9 %collective-permute-start.1 = (bf16[512,1024]{1,0:T(8,128)(2,1)}, bf16[512,1024]{1,0:T(8,128)(2,1)}, u32[]{:S(2)}, u32[]{:S(2)}) collective-permute-start(bf16[512,1024]{1,0:T(8,128)(2,1)} %matrix_ref.1), channel_id=1, source_target_pairs={{0,1},{1,0},{2,3},{3,2},{4,5},{5,4},{6,7},{7,6},{8,9},{9,8},{10,11... | collective-permute-start | bytes 3145736 | tf_op jit(solution)/shard_map/ppermute | solution.py:127
  22.4 1.3 %copy-start.8 = (bf16[2048,512]{1,0:T(8,128)(2,1)}, bf16[2048,512]{1,0:T(8,128)(2,1)S(1)}, u32[]{:S(2)}) copy-start(bf16[2048,512]{1,0:T(8,128)(2,1)S(1)} %collective-permute-done.other_ref) | copy-start | bytes 6291460
  30.6 30.4 %collective-permute-start.2 = (bf16[64,2048]{1,0:T(8,128)(2,1)}, bf16[64,2048]{1,0:T(8,128)(2,1)}, u32[]{:S(2)}, u32[]{:S(2)}) collective-permute-start(bf16[64,2048]{1,0:T(8,128)(2,1)} %get-tuple-element.17), channel_id=1, source_target_pairs={{0,2},{2,4},{4,6},{6,8},{8,10},{10,12},{12,14},{14,0},{1,3},{3,5},... | collective-permute-start | bytes 786440 | tf_op jit(solution)/shard_map/ppermute | solution.py:127
  48.3 17.9 %copy-start.6 = (bf16[64,2048]{1,0:T(8,128)(2,1)S(1)}, bf16[64,2048]{1,0:T(8,128)(2,1)}, u32[]{:S(2)}) copy-start(bf16[64,2048]{1,0:T(8,128)(2,1)} %get-tuple-element.22) | copy-start | bytes 786436
  48.3 24.1 %copy-start = (bf16[2048,512]{1,0:T(8,128)(2,1)S(1)}, bf16[2048,512]{1,0:T(8,128)(2,1)}, u32[]{:S(2)}) copy-start(bf16[2048,512]{1,0:T(8,128)(2,1)} %hidden_ref.3) | copy-start | bytes 6291460
  48.3 24.1 %all-to-all-start.1 = ((bf16[4,288,512]{2,1,0:T(8,128)(2,1)}), bf16[4,288,512]{2,1,0:T(8,128)(2,1)S(1)}, u32[]{:S(2)}, u32[]{:S(2)}) async-start(bf16[4,288,512]{2,1,0:T(8,128)(2,1)} %pick_factors.1), calls=%async_computation.1 | async-start | bytes 2359296 | tf_op jit(solution)/shard_map/all_to_all | solution.py:312
  51.9 14.3 %collective-permute-start.6 = (bf16[64,2048]{1,0:T(8,128)(2,1)}, bf16[64,2048]{1,0:T(8,128)(2,1)S(1)}, u32[]{:S(2)}, u32[]{:S(2)}) collective-permute-start(bf16[64,2048]{1,0:T(8,128)(2,1)} %get-tuple-element.21), channel_id=1, source_target_pairs={{0,14},{2,0},{4,2},{6,4},{8,6},{10,8},{12,10},{14,12},{1,15},{3,1}... | collective-permute-start | bytes 786440 | tf_op jit(solution)/shard_map/ppermute | solution.py:127
  62.8 17.5 %collective-permute-start.3 = (bf16[64,2048]{1,0:T(8,128)(2,1)}, bf16[64,2048]{1,0:T(8,128)(2,1)}, u32[]{:S(2)}, u32[]{:S(2)}) collective-permute-start(bf16[64,2048]{1,0:T(8,128)(2,1)} %add_convert_fusion.4), channel_id=1, source_target_pairs={{0,2},{2,4},{4,6},{6,8},{8,10},{10,12},{12,14},{14,0},{1,3},{3,5},... | collective-permute-start | bytes 786440 | tf_op jit(solution)/shard_map/ppermute | solution.py:127
  67.0 13.3 %copy-start.5 = (bf16[64,2048]{1,0:T(8,128)(2,1)S(1)}, bf16[64,2048]{1,0:T(8,128)(2,1)}, u32[]{:S(2)}) copy-start(bf16[64,2048]{1,0:T(8,128)(2,1)} %get-tuple-element.19) | copy-start | bytes 786436
  67.0 17.7 %collective-permute-start.7 = (bf16[64,2048]{1,0:T(8,128)(2,1)}, bf16[64,2048]{1,0:T(8,128)(2,1)}, u32[]{:S(2)}, u32[]{:S(2)}) collective-permute-start(bf16[64,2048]{1,0:T(8,128)(2,1)} %add_convert_fusion.1), channel_id=1, source_target_pairs={{0,14},{2,0},{4,2},{6,4},{8,6},{10,8},{12,10},{14,12},{1,15},{3,1}... | collective-permute-start | bytes 786440 | tf_op jit(solution)/shard_map/ppermute | solution.py:127
  74.4 10.3 %copy-start.4 = (bf16[64,2048]{1,0:T(8,128)(2,1)S(1)}, bf16[64,2048]{1,0:T(8,128)(2,1)}, u32[]{:S(2)}) copy-start(bf16[64,2048]{1,0:T(8,128)(2,1)} %get-tuple-element.23) | copy-start | bytes 786436
  74.4 17.9 %all-to-all-start.2 = ((bf16[16,64,128]{2,1,0:T(8,128)(2,1)}), bf16[16,64,128]{2,1,0:T(8,128)(2,1)S(1)}, u32[]{:S(2)}, u32[]{:S(2)}) async-start(bf16[16,64,128]{2,1,0:T(8,128)(2,1)} %down_projection.1), calls=%async_computation.2 | async-start | bytes 524288 | tf_op jit(solution)/shard_map/all_to_all | solution.py:314
  80.3 17.3 %copy-start.3 = (bf16[64,2048]{1,0:T(8,128)(2,1)S(1)}, bf16[64,2048]{1,0:T(8,128)(2,1)}, u32[]{:S(2)}) copy-start(bf16[64,2048]{1,0:T(8,128)(2,1)} %get-tuple-element.20) | copy-start | bytes 786436
  81.4 16.2 %collective-permute-start.4 = (bf16[64,2048]{1,0:T(8,128)(2,1)S(1)}, bf16[64,2048]{1,0:T(8,128)(2,1)S(1)}, u32[]{:S(2)}, u32[]{:S(2)}) collective-permute-start(bf16[64,2048]{1,0:T(8,128)(2,1)S(1)} %add_convert_fusion.3), channel_id=1, source_target_pairs={{0,2},{2,4},{4,6},{6,8},{8,10},{10,12},{12,14},{14,0},{1,3},{3,5},... | collective-permute-start | bytes 786440 | tf_op jit(solution)/shard_map/ppermute | solution.py:127
  84.7 27.7 %copy-start.1 = (bf16[64,2048]{1,0:T(8,128)(2,1)S(1)}, bf16[64,2048]{1,0:T(8,128)(2,1)}, u32[]{:S(2)}) copy-start(bf16[64,2048]{1,0:T(8,128)(2,1)} %get-tuple-element.16.refs_0_) | copy-start | bytes 786436
  84.7 27.6 %copy-start.2 = (s32[4]{0:T(128)S(1)}, s32[4]{0:T(128)}, u32[]{:S(2)}) copy-start(s32[4]{0:T(128)} %lengths_ref.1) | copy-start | bytes 52
  85.8 15.2 %collective-permute-start.8 = (bf16[64,2048]{1,0:T(8,128)(2,1)S(1)}, bf16[64,2048]{1,0:T(8,128)(2,1)S(1)}, u32[]{:S(2)}, u32[]{:S(2)}) collective-permute-start(bf16[64,2048]{1,0:T(8,128)(2,1)S(1)} %add_convert_fusion), channel_id=1, source_target_pairs={{0,14},{2,0},{4,2},{6,4},{8,6},{10,8},{12,10},{14,12},{1,15},{3,1}... | collective-permute-start | bytes 786440 | tf_op jit(solution)/shard_map/ppermute | solution.py:127
  93.0 19.4 %all-to-all-start.3 = ((bf16[16,64,128]{2,1,0:T(8,128)(2,1)}), bf16[16,64,128]{2,1,0:T(8,128)(2,1)S(1)}, u32[]{:S(2)}, u32[]{:S(2)}) async-start(bf16[16,64,128]{2,1,0:T(8,128)(2,1)} %sum_parts.1), calls=%async_computation.3 | async-start | bytes 524288 | tf_op jit(solution)/shard_map/all_to_all | solution.py:316
  97.6 14.7 %collective-permute-start.5 = (bf16[64,2048]{1,0:T(8,128)(2,1)S(1)}, bf16[64,2048]{1,0:T(8,128)(2,1)S(1)}, u32[]{:S(2)}, u32[]{:S(2)}) collective-permute-start(bf16[64,2048]{1,0:T(8,128)(2,1)S(1)} %add_convert_fusion.2), channel_id=1, source_target_pairs={{0,2},{2,4},{4,6},{6,8},{8,10},{10,12},{12,14},{14,0},{1,3},{3,5},... | collective-permute-start | bytes 786440 | tf_op jit(solution)/shard_map/ppermute | solution.py:127

commit v3 on v2

--- a/solution.py
+++ b/solution.py
@@ -12,6 +12,7 @@
 X, CORES = 4, 2
 DP, TENSOR = ("x", "y"), ("z", "core")
 LANES = 128
+AHEAD_WEIGHTS, BEHIND_WEIGHTS, LAST_WEIGHT = (1, 50000, 1), (50000, 1), 50000
 KERNEL_VMEM = 8 << 20
 PROJECT_VMEM, PROJECT_ROWS, PROJECT_CHIPS = 60 << 20, 1024, 4
 
@@ -118,8 +119,25 @@
     )(hidden, other, matrix, other_matrix)
 
 
-def add(a, b):
-    return (a.astype(jnp.float32) + b.astype(jnp.float32)).astype(a.dtype)
+def add_kernel(*refs):
+    *in_refs, out_ref = refs
+    total = in_refs[0][...].astype(jnp.float32)
+    for ref in in_refs[1:]:
+        total += ref[...].astype(jnp.float32)
+    out_ref[...] = total.astype(out_ref.dtype)
+
+
+def add(*parts, weight):
+    size = parts[0].size
+    return pl.pallas_call(
+        add_kernel,
+        out_shape=jax.ShapeDtypeStruct(parts[0].shape, parts[0].dtype),
+        in_specs=[pl.BlockSpec(memory_space=pltpu.VMEM)] * len(parts),
+        out_specs=pl.BlockSpec(memory_space=pltpu.VMEM),
+        cost_estimate=cost(weight * size, (len(parts) + 1) * size),
+        compiler_params=pltpu.CompilerParams(vmem_limit_bytes=KERNEL_VMEM),
+        name="add_parts",
+    )(*parts)
 
 
 def along(axis, value, step):
@@ -286,17 +304,18 @@
     row = lax.all_to_all(copies, "y", 0, 0)
 
     parts = project(hidden, other, value_matrix, other_matrix, adapter_up_store.shape[2])
+    *parts, rollout_adapter = lax.optimization_barrier((*parts, rollout_adapter))
     far = len(parts) // 2
     ahead, behind = parts[far], parts[far + 1]
     for k in range(far - 1, -1, -1):
         ahead = along("z", ahead, 1)
         if k:
-            ahead = add(ahead, parts[k])
+            ahead = add(ahead, parts[k], weight=AHEAD_WEIGHTS[far - 1 - k])
     for k in range(far + 2, len(parts) + 1):
         behind = along("z", behind, -1)
         if k < len(parts):
-            behind = add(behind, parts[k])
-    base = (parts[0], ahead, behind)
+            behind = add(behind, parts[k], weight=BEHIND_WEIGHTS[k - far - 2])
+    base = (add(parts[0], ahead, behind, weight=LAST_WEIGHT),)
 
     here = lax.axis_index("x")
     mine = jnp.arange(X, dtype=jnp.int32)[:, None] == here

time: 115 us -> 110 us (0.957)
  waiting for transfers between devices: 27.9 us -> 21.4 us
  other arithmetic: 5.13 us -> 0.35 us
  Pallas kernels: 15.1 us -> 18.8 us
  blocking collectives: 5.59 us -> 7.48 us
  starting transfers between devices: 58.5 us -> 59.7 us
    all_to_all x1, waiting for transfers between devices: 11.8 us -> 0.53 us  [on_device(): row = lax.all_to_all(copies, 'y', 0, 0)]
    all_to_all x2, waiting for transfers between devices: 3.22 us -> 13.8 us  [on_device(): down = lax.all_to_all(down, TENSOR, 0, 0)]
    ppermute x9, waiting for transfers between devices: 12.9 us -> 7.14 us  [along(): return lax.ppermute(value, axis, [(i, (i + step) % n) for i in range(n)])]
    convert_element_type x5 -> x0, other arithmetic: 4.77 us -> none  [add(): return (a.astype(jnp.float32) + b.astype(jnp.float32)).astype(a.dtype)]
    pallas_call x0 -> x6, Pallas kernels: none -> 3.78 us  [add(): pl.pallas_call(add_kernel, out_shape=jax.ShapeDtypeStruct(parts[0].shape,...]
    psum x1, blocking collectives: 5.59 us -> 7.48 us  [on_device(): lax.psum(jnp.where(mine, rollout_adapter[None, :], 0), 'x').reshape(-1)]
    all_to_all x2, starting transfers between devices: 10.5 us -> 11.7 us  [on_device(): down = lax.all_to_all(down, TENSOR, 0, 0)]
  transfers between devices with their start and end apart: 13 -> 13, of which waited for: 4 -> 6; matrix products, arithmetic and copies ran while one was open for 5% -> 0% of each run, Pallas kernels for 12% -> 16%
where the time goes in v3:
time: 110 us
  starting transfers between devices  59.7 us (54%)
  waiting for transfers between devices  21.4 us (19%)
  Pallas kernels  18.8 us (17%)
  blocking collectives  7.48 us (7%)
  local copies, waits for them, and re-layouts  1.45 us (1%)
    ppermute x9, starting transfers between devices, along(): return lax.ppermute(value, axis, [(i, (i + step) % n) for i in range(n)])  40.7 us
    all_to_all x2, waiting for transfers between devices, on_device(): down = lax.all_to_all(down, TENSOR, 0, 0)  13.8 us
    all_to_all x2, starting transfers between devices, on_device(): down = lax.all_to_all(down, TENSOR, 0, 0)  11.7 us
    psum x1, blocking collectives, on_device(): lax.psum(jnp.where(mine, rollout_adapter[None, :], 0), 'x').reshape(-1)  7.48 us
    ppermute x9, waiting for transfers between devices, along(): return lax.ppermute(value, axis, [(i, (i + step) % n) for i in range(n)])  7.14 us
    pallas_call x1, Pallas kernels, project(): pl.pallas_call(project_kernel, grid=(tokens // rows,), out_shape=[jax.Sha...  6.87 us
    pallas_call x6, Pallas kernels, add(): pl.pallas_call(add_kernel, out_shape=jax.ShapeDtypeStruct(parts[0].shape,...  3.78 us
    all_to_all x1, starting transfers between devices, on_device(): factors = lax.all_to_all(sent, 'x', 0, 0)  3.66 us
  transfers between devices with their start and end apart: 13, of which 6 were waited for; matrix products, arithmetic and copies ran while one was open for 0% of the time, Pallas kernels for 16%

profile of v3, /device:TPU:1, one launch (start us, length us, event | category | flops | bytes accessed | tf_op | source)
XLA Modules:
  0.0 109.5 jit_solution(5825079529456113032)
XLA Ops:
  0.0 8.8 %collective-permute-start = (bf16[2048,512]{1,0:T(8,128)(2,1)}, bf16[2048,512]{1,0:T(8,128)(2,1)S(1)}, u32[]{:S(2)}, u32[]{:S(2)}) collective-permute-start(bf16[2048,512]{1,0:T(8,128)(2,1)} %hidden_ref.3), channel_id=1, source_target_pairs={{0,1},{1,0},{2,3},{3,2},{4,5},{5,4},{6,7},{7,6},{8,9},{9,8},{10,11... | collective-permute-start | bytes 6291464 | tf_op jit(solution)/shard_map/ppermute | solution.py:145
  8.8 2.1 %factor_copies.1 = bf16[8,144,512]{2,1,0:T(8,128)(2,1)} custom-call(bf16[2,64,512]{2,1,0:T(8,128)(2,1)} %bitcast.2, bf16[2,64,64]{2,1,0:T(8,128)(2,1)} %up_ref.1), custom_call_target="tpu_custom_call" | custom-call | bytes 1179648 | tf_op jit(solution)/shard_map/factor_copies/pallas_call | solution.py:52
  10.9 3.6 %all-to-all-start = ((bf16[8,144,512]{2,1,0:T(8,128)(2,1)}), bf16[8,144,512]{2,1,0:T(8,128)(2,1)S(1)}, u32[]{:S(2)}, u32[]{:S(2)}) async-start(bf16[8,144,512]{2,1,0:T(8,128)(2,1)} %factor_copies.1), calls=%async_computation | async-start | bytes 2359296 | tf_op jit(solution)/shard_map/all_to_all | solution.py:304
  14.5 1.9 %collective-permute-start.1 = (bf16[512,1024]{1,0:T(8,128)(2,1)}, bf16[512,1024]{1,0:T(8,128)(2,1)}, u32[]{:S(2)}, u32[]{:S(2)}) collective-permute-start(bf16[512,1024]{1,0:T(8,128)(2,1)} %matrix_ref.1), channel_id=1, source_target_pairs={{0,1},{1,0},{2,3},{3,2},{4,5},{5,4},{6,7},{7,6},{8,9},{9,8},{10,11... | collective-permute-start | bytes 3145736 | tf_op jit(solution)/shard_map/ppermute | solution.py:145
  16.4 2.9 %collective-permute-done.1.other_matrix_ref = bf16[512,1024]{1,0:T(8,128)(2,1)} collective-permute-done((bf16[512,1024]{1,0:T(8,128)(2,1)}, bf16[512,1024]{1,0:T(8,128)(2,1)}, u32[]{:S(2)}, u32[]{:S(2)}) %collective-permute-start.1) | collective-permute-done | bytes 1048608 | tf_op jit(solution)/shard_map/ppermute | solution.py:145
  19.4 1.3 %copy-done.9 = bf16[2048,512]{1,0:T(8,128)(2,1)} copy-done((bf16[2048,512]{1,0:T(8,128)(2,1)}, bf16[2048,512]{1,0:T(8,128)(2,1)S(1)}, u32[]{:S(2)}) %copy-start.9) | copy-done | bytes 2097176
  20.7 6.9 %project.1 = (bf16[64,2048]{1,0:T(8,128)(2,1)}, bf16[64,2048]{1,0:T(8,128)(2,1)}, bf16[64,2048]{1,0:T(8,128)(2,1)}, bf16[64,2048]{1,0:T(8,128)(2,1)}, bf16[64,20...) custom-call(bf16[2048,512]{1,0:T(8,128)(2,1)} %hidden_ref.3, ...), custom_call_target="tpu_custom_call" | custom-call | flops 2147483648 | bytes 8388608 | tf_op jit(solution)/shard_map/project/pallas_call | solution.py:106
  27.7 8.5 %collective-permute-start.6 = (bf16[64,2048]{1,0:T(8,128)(2,1)}, bf16[64,2048]{1,0:T(8,128)(2,1)S(1)}, u32[]{:S(2)}, u32[]{:S(2)}) collective-permute-start(bf16[64,2048]{1,0:T(8,128)(2,1)} %get-tuple-element.39), channel_id=1, source_target_pairs={{0,14},{2,0},{4,2},{6,4},{8,6},{10,8},{12,10},{14,12},{1,15},{3,1}... | collective-permute-start | bytes 786440 | tf_op jit(solution)/shard_map/ppermute | solution.py:145
  36.3 1.9 %collective-permute-start.2 = (bf16[64,2048]{1,0:T(8,128)(2,1)}, bf16[64,2048]{1,0:T(8,128)(2,1)S(1)}, u32[]{:S(2)}, u32[]{:S(2)}) collective-permute-start(bf16[64,2048]{1,0:T(8,128)(2,1)} %get-tuple-element.35), channel_id=1, source_target_pairs={{0,2},{2,4},{4,6},{6,8},{8,10},{10,12},{12,14},{14,0},{1,3},{3,5},... | collective-permute-start | bytes 786440 | tf_op jit(solution)/shard_map/ppermute | solution.py:145
  38.2 7.5 %psum.7 = s32[16]{0:T(128)S(1)} all-reduce(s32[16]{0:T(128)S(1)} %eq.28), channel_id=1, replica_groups=mesh['x'=4,'y'=8,'z'=8,'core'=2] {'x'}, use_global_device_ids=true, to_apply=%region_0.1 | all-reduce | flops 16 | bytes 128 | tf_op jit(solution)/shard_map/psum | solution.py:322
  46.5 1.8 %pick_factors.1 = bf16[4,288,512]{2,1,0:T(8,128)(2,1)} custom-call(s32[16]{0:T(128)S(1)} %subtract_clamp_fusion.index_ref, bf16[8,144,512]{2,1,0:T(8,128)(2,1)S(1)} %all-to-all-done.row_ref), custom_call_target="tpu_custom_call" | custom-call | bytes 2359296 | tf_op jit(solution)/shard_map/pick_factors/pallas_call | solution.py:180
  48.3 3.7 %all-to-all-start.1 = ((bf16[4,288,512]{2,1,0:T(8,128)(2,1)}), bf16[4,288,512]{2,1,0:T(8,128)(2,1)S(1)}, u32[]{:S(2)}, u32[]{:S(2)}) async-start(bf16[4,288,512]{2,1,0:T(8,128)(2,1)} %pick_factors.1), calls=%async_computation.1 | async-start | bytes 2359296 | tf_op jit(solution)/shard_map/all_to_all | solution.py:331
  52.0 2.5 %collective-permute-start.3 = (bf16[64,2048]{1,0:T(8,128)(2,1)S(1)}, bf16[64,2048]{1,0:T(8,128)(2,1)S(1)}, u32[]{:S(2)}, u32[]{:S(2)}) collective-permute-start(bf16[64,2048]{1,0:T(8,128)(2,1)S(1)} %add_parts.6), channel_id=1, source_target_pairs={{0,2},{2,4},{4,6},{6,8},{8,10},{10,12},{12,14},{14,0},{1,3},{3,5},... | collective-permute-start | bytes 786440 | tf_op jit(solution)/shard_map/ppermute | solution.py:145
  55.3 8.6 %collective-permute-start.7 = (bf16[64,2048]{1,0:T(8,128)(2,1)}, bf16[64,2048]{1,0:T(8,128)(2,1)}, u32[]{:S(2)}, u32[]{:S(2)}) collective-permute-start(bf16[64,2048]{1,0:T(8,128)(2,1)} %add_parts.9), channel_id=1, source_target_pairs={{0,14},{2,0},{4,2},{6,4},{8,6},{10,8},{12,10},{14,12},{1,15},{3,1}... | collective-permute-start | bytes 786440 | tf_op jit(solution)/shard_map/ppermute | solution.py:145
  63.9 3.2 %collective-permute-done.3.refs_0_ = bf16[64,2048]{1,0:T(8,128)(2,1)S(1)} collective-permute-done((bf16[64,2048]{1,0:T(8,128)(2,1)S(1)}, bf16[64,2048]{1,0:T(8,128)(2,1)S(1)}, u32[]{:S(2)}, u32[]{:S(2)}) %collective-permute-start.3) | collective-permute-done | bytes 262176 | tf_op jit(solution)/shard_map/ppermute | solution.py:145
  68.0 2.0 %collective-permute-start.4 = (bf16[64,2048]{1,0:T(8,128)(2,1)}, bf16[64,2048]{1,0:T(8,128)(2,1)}, u32[]{:S(2)}, u32[]{:S(2)}) collective-permute-start(bf16[64,2048]{1,0:T(8,128)(2,1)} %add_parts.7), channel_id=1, source_target_pairs={{0,2},{2,4},{4,6},{6,8},{8,10},{10,12},{12,14},{14,0},{1,3},{3,5},... | collective-permute-start | bytes 786440 | tf_op jit(solution)/shard_map/ppermute | solution.py:145
  70.0 2.0 %down_projection.1 = bf16[16,64,128]{2,1,0:T(8,128)(2,1)} custom-call(s32[4]{0:T(128)S(1)} %and_select_fusion.own_row_ref, bf16[2048,512]{1,0:T(8,128)(2,1)S(1)} %copy-done, bf16[4,288,512]{2,1,0:T(8,128)(2,1)S(1)} %all-to-all-done.1.factor_ref.refs_2_), custom_call_target="tpu_custom_call" | custom-call | flops 134217728 | bytes 2359296 | tf_op jit(solution)/shard_map/down_projection/pallas_call | solution.py:212
  72.0 8.2 %all-to-all-start.2 = ((bf16[16,64,128]{2,1,0:T(8,128)(2,1)}), bf16[16,64,128]{2,1,0:T(8,128)(2,1)S(1)}, u32[]{:S(2)}, u32[]{:S(2)}) async-start(bf16[16,64,128]{2,1,0:T(8,128)(2,1)} %down_projection.1), calls=%async_computation.2 | async-start | bytes 524288 | tf_op jit(solution)/shard_map/all_to_all | solution.py:333
  81.4 4.5 %collective-permute-start.8 = (bf16[64,2048]{1,0:T(8,128)(2,1)S(1)}, bf16[64,2048]{1,0:T(8,128)(2,1)S(1)}, u32[]{:S(2)}, u32[]{:S(2)}) collective-permute-start(bf16[64,2048]{1,0:T(8,128)(2,1)S(1)} %add_parts.10), channel_id=1, source_target_pairs={{0,14},{2,0},{4,2},{6,4},{8,6},{10,8},{12,10},{14,12},{1,15},{3,1}... | collective-permute-start | bytes 786440 | tf_op jit(solution)/shard_map/ppermute | solution.py:145
  86.9 1.9 %collective-permute-start.5 = (bf16[64,2048]{1,0:T(8,128)(2,1)S(1)}, bf16[64,2048]{1,0:T(8,128)(2,1)S(1)}, u32[]{:S(2)}, u32[]{:S(2)}) collective-permute-start(bf16[64,2048]{1,0:T(8,128)(2,1)S(1)} %add_parts.8), channel_id=1, source_target_pairs={{0,2},{2,4},{4,6},{6,8},{8,10},{10,12},{12,14},{14,0},{1,3},{3,5},... | collective-permute-start | bytes 786440 | tf_op jit(solution)/shard_map/ppermute | solution.py:145
  88.8 3.1 %all-to-all-done.2.parts_ref = bf16[16,64,128]{2,1,0:T(8,128)(2,1)S(1)} async-done(((bf16[16,64,128]{2,1,0:T(8,128)(2,1)}), bf16[16,64,128]{2,1,0:T(8,128)(2,1)S(1)}, u32[]{:S(2)}, u32[]{:S(2)}) %all-to-all-start.2) | async-done | bytes 262176 | tf_op jit(solution)/shard_map/all_to_all | solution.py:333
  92.7 3.5 %all-to-all-start.3 = ((bf16[16,64,128]{2,1,0:T(8,128)(2,1)}), bf16[16,64,128]{2,1,0:T(8,128)(2,1)S(1)}, u32[]{:S(2)}, u32[]{:S(2)}) async-start(bf16[16,64,128]{2,1,0:T(8,128)(2,1)} %sum_parts.1), calls=%async_computation.3 | async-start | bytes 524288 | tf_op jit(solution)/shard_map/all_to_all | solution.py:335
  97.3 10.6 %all-to-all-done.3.refs_1_ = bf16[16,64,128]{2,1,0:T(8,128)(2,1)S(1)} async-done(((bf16[16,64,128]{2,1,0:T(8,128)(2,1)}), bf16[16,64,128]{2,1,0:T(8,128)(2,1)S(1)}, u32[]{:S(2)}, u32[]{:S(2)}) %all-to-all-start.3) | async-done | bytes 262176 | tf_op jit(solution)/shard_map/all_to_all | solution.py:335
  107.9 1.6 %add_update.1 = bf16[64,2048]{1,0:T(8,128)(2,1)} custom-call(s32[4]{0:T(128)S(1)} %and_select_fusion.own_row_ref, s32[4]{0:T(128)S(1)} %copy-done.4, bf16[64,2048]{1,0:T(8,128)(2,1)S(1)} %add_parts.11.refs_0_, bf16[16,64,128]{2,1,0:T(8,128)(2,1)S(1)} %all-to-all-done.3.refs_1_, bf16[4,288,512]{2,1,0:T(8,128)(2,1)S(1)} %all-to-all-done.1.factor_ref.refs_2_), custom_call_target="tpu_custom_call" | custom-call | flops 16777216 | bytes 1310720 | tf_op jit(solution)/shard_map/add_update/pallas_call | solution.py:279
  (43 shorter events, 6.5 us)
Async XLA Ops:
  0.0 19.4 %collective-permute-start = (bf16[2048,512]{1,0:T(8,128)(2,1)}, bf16[2048,512]{1,0:T(8,128)(2,1)S(1)}, u32[]{:S(2)}, u32[]{:S(2)}) collective-permute-start(bf16[2048,512]{1,0:T(8,128)(2,1)} %hidden_ref.3), channel_id=1, source_target_pairs={{0,1},{1,0},{2,3},{3,2},{4,5},{5,4},{6,7},{7,6},{8,9},{9,8},{10,11... | collective-permute-start | bytes 6291464 | tf_op jit(solution)/shard_map/ppermute | solution.py:145
  10.9 35.6 %all-to-all-start = ((bf16[8,144,512]{2,1,0:T(8,128)(2,1)}), bf16[8,144,512]{2,1,0:T(8,128)(2,1)S(1)}, u32[]{:S(2)}, u32[]{:S(2)}) async-start(bf16[8,144,512]{2,1,0:T(8,128)(2,1)} %factor_copies.1), calls=%async_computation | async-start | bytes 2359296 | tf_op jit(solution)/shard_map/all_to_all | solution.py:304
  14.5 4.9 %collective-permute-start.1 = (bf16[512,1024]{1,0:T(8,128)(2,1)}, bf16[512,1024]{1,0:T(8,128)(2,1)}, u32[]{:S(2)}, u32[]{:S(2)}) collective-permute-start(bf16[512,1024]{1,0:T(8,128)(2,1)} %matrix_ref.1), channel_id=1, source_target_pairs={{0,1},{1,0},{2,3},{3,2},{4,5},{5,4},{6,7},{7,6},{8,9},{9,8},{10,11... | collective-permute-start | bytes 3145736 | tf_op jit(solution)/shard_map/ppermute | solution.py:145
  16.4 11.2 %copy-start.8 = (s32[4]{0:T(128)S(1)}, s32[4]{0:T(128)}, u32[]{:S(2)}) copy-start(s32[4]{0:T(128)} %param.12) | copy-start | bytes 52
  16.4 29.3 %copy-start.10 = (s32[64]{0:T(128)S(1)}, s32[64]{0:T(128)}, u32[]{:S(2)}) copy-start(s32[64]{0:T(128)} %param.11) | copy-start | bytes 772
  19.4 1.3 %copy-start.9 = (bf16[2048,512]{1,0:T(8,128)(2,1)}, bf16[2048,512]{1,0:T(8,128)(2,1)S(1)}, u32[]{:S(2)}) copy-start(bf16[2048,512]{1,0:T(8,128)(2,1)S(1)} %collective-permute-done.other_ref) | copy-start | bytes 6291460
  27.7 26.8 %collective-permute-start.6 = (bf16[64,2048]{1,0:T(8,128)(2,1)}, bf16[64,2048]{1,0:T(8,128)(2,1)S(1)}, u32[]{:S(2)}, u32[]{:S(2)}) collective-permute-start(bf16[64,2048]{1,0:T(8,128)(2,1)} %get-tuple-element.39), channel_id=1, source_target_pairs={{0,14},{2,0},{4,2},{6,4},{8,6},{10,8},{12,10},{14,12},{1,15},{3,1}... | collective-permute-start | bytes 786440 | tf_op jit(solution)/shard_map/ppermute | solution.py:145
  36.3 15.7 %collective-permute-start.2 = (bf16[64,2048]{1,0:T(8,128)(2,1)}, bf16[64,2048]{1,0:T(8,128)(2,1)S(1)}, u32[]{:S(2)}, u32[]{:S(2)}) collective-permute-start(bf16[64,2048]{1,0:T(8,128)(2,1)} %get-tuple-element.35), channel_id=1, source_target_pairs={{0,2},{2,4},{4,6},{6,8},{8,10},{10,12},{12,14},{14,0},{1,3},{3,5},... | collective-permute-start | bytes 786440 | tf_op jit(solution)/shard_map/ppermute | solution.py:145
  48.2 3.7 %copy-start.3 = (bf16[64,2048]{1,0:T(8,128)(2,1)S(1)}, bf16[64,2048]{1,0:T(8,128)(2,1)}, u32[]{:S(2)}) copy-start(bf16[64,2048]{1,0:T(8,128)(2,1)} %get-tuple-element.36.refs_1_) | copy-start | bytes 786436
  48.3 6.3 %copy-start.7 = (bf16[64,2048]{1,0:T(8,128)(2,1)S(1)}, bf16[64,2048]{1,0:T(8,128)(2,1)}, u32[]{:S(2)}) copy-start(bf16[64,2048]{1,0:T(8,128)(2,1)} %get-tuple-element.40.refs_1_) | copy-start | bytes 786436
  48.3 21.8 %all-to-all-start.1 = ((bf16[4,288,512]{2,1,0:T(8,128)(2,1)}), bf16[4,288,512]{2,1,0:T(8,128)(2,1)S(1)}, u32[]{:S(2)}, u32[]{:S(2)}) async-start(bf16[4,288,512]{2,1,0:T(8,128)(2,1)} %pick_factors.1), calls=%async_computation.1 | async-start | bytes 2359296 | tf_op jit(solution)/shard_map/all_to_all | solution.py:331
  52.0 15.2 %copy-start.6 = (bf16[64,2048]{1,0:T(8,128)(2,1)S(1)}, bf16[64,2048]{1,0:T(8,128)(2,1)}, u32[]{:S(2)}) copy-start(bf16[64,2048]{1,0:T(8,128)(2,1)} %get-tuple-element.37.refs_1_) | copy-start | bytes 786436
  52.0 15.1 %collective-permute-start.3 = (bf16[64,2048]{1,0:T(8,128)(2,1)S(1)}, bf16[64,2048]{1,0:T(8,128)(2,1)S(1)}, u32[]{:S(2)}, u32[]{:S(2)}) collective-permute-start(bf16[64,2048]{1,0:T(8,128)(2,1)S(1)} %add_parts.6), channel_id=1, source_target_pairs={{0,2},{2,4},{4,6},{6,8},{8,10},{10,12},{12,14},{14,0},{1,3},{3,5},... | collective-permute-start | bytes 786440 | tf_op jit(solution)/shard_map/ppermute | solution.py:145
  55.3 24.9 %collective-permute-start.7 = (bf16[64,2048]{1,0:T(8,128)(2,1)}, bf16[64,2048]{1,0:T(8,128)(2,1)}, u32[]{:S(2)}, u32[]{:S(2)}) collective-permute-start(bf16[64,2048]{1,0:T(8,128)(2,1)} %add_parts.9), channel_id=1, source_target_pairs={{0,14},{2,0},{4,2},{6,4},{8,6},{10,8},{12,10},{14,12},{1,15},{3,1}... | collective-permute-start | bytes 786440 | tf_op jit(solution)/shard_map/ppermute | solution.py:145
  67.2 2.9 %copy-start = (bf16[2048,512]{1,0:T(8,128)(2,1)S(1)}, bf16[2048,512]{1,0:T(8,128)(2,1)}, u32[]{:S(2)}) copy-start(bf16[2048,512]{1,0:T(8,128)(2,1)} %hidden_ref.3) | copy-start | bytes 6291460
  68.0 12.3 %copy-start.2 = (bf16[64,2048]{1,0:T(8,128)(2,1)S(1)}, bf16[64,2048]{1,0:T(8,128)(2,1)}, u32[]{:S(2)}) copy-start(bf16[64,2048]{1,0:T(8,128)(2,1)} %get-tuple-element.41.refs_1_) | copy-start | bytes 786436
  68.0 17.9 %collective-permute-start.4 = (bf16[64,2048]{1,0:T(8,128)(2,1)}, bf16[64,2048]{1,0:T(8,128)(2,1)}, u32[]{:S(2)}, u32[]{:S(2)}) collective-permute-start(bf16[64,2048]{1,0:T(8,128)(2,1)} %add_parts.7), channel_id=1, source_target_pairs={{0,2},{2,4},{4,6},{6,8},{8,10},{10,12},{12,14},{14,0},{1,3},{3,5},... | collective-permute-start | bytes 786440 | tf_op jit(solution)/shard_map/ppermute | solution.py:145
  72.0 13.8 %copy-start.1 = (bf16[64,2048]{1,0:T(8,128)(2,1)S(1)}, bf16[64,2048]{1,0:T(8,128)(2,1)}, u32[]{:S(2)}) copy-start(bf16[64,2048]{1,0:T(8,128)(2,1)} %get-tuple-element.38.refs_1_) | copy-start | bytes 786436
  72.0 19.9 %all-to-all-start.2 = ((bf16[16,64,128]{2,1,0:T(8,128)(2,1)}), bf16[16,64,128]{2,1,0:T(8,128)(2,1)S(1)}, u32[]{:S(2)}, u32[]{:S(2)}) async-start(bf16[16,64,128]{2,1,0:T(8,128)(2,1)} %down_projection.1), calls=%async_computation.2 | async-start | bytes 524288 | tf_op jit(solution)/shard_map/all_to_all | solution.py:333
  80.3 17.0 %copy-start.5 = (bf16[64,2048]{1,0:T(8,128)(2,1)S(1)}, bf16[64,2048]{1,0:T(8,128)(2,1)}, u32[]{:S(2)}) copy-start(bf16[64,2048]{1,0:T(8,128)(2,1)} %get-tuple-element.34.refs_0_) | copy-start | bytes 786436
  81.4 14.9 %collective-permute-start.8 = (bf16[64,2048]{1,0:T(8,128)(2,1)S(1)}, bf16[64,2048]{1,0:T(8,128)(2,1)S(1)}, u32[]{:S(2)}, u32[]{:S(2)}) collective-permute-start(bf16[64,2048]{1,0:T(8,128)(2,1)S(1)} %add_parts.10), channel_id=1, source_target_pairs={{0,14},{2,0},{4,2},{6,4},{8,6},{10,8},{12,10},{14,12},{1,15},{3,1}... | collective-permute-start | bytes 786440 | tf_op jit(solution)/shard_map/ppermute | solution.py:145
  86.9 10.3 %collective-permute-start.5 = (bf16[64,2048]{1,0:T(8,128)(2,1)S(1)}, bf16[64,2048]{1,0:T(8,128)(2,1)S(1)}, u32[]{:S(2)}, u32[]{:S(2)}) collective-permute-start(bf16[64,2048]{1,0:T(8,128)(2,1)S(1)} %add_parts.8), channel_id=1, source_target_pairs={{0,2},{2,4},{4,6},{6,8},{8,10},{10,12},{12,14},{14,0},{1,3},{3,5},... | collective-permute-start | bytes 786440 | tf_op jit(solution)/shard_map/ppermute | solution.py:145
  92.7 15.2 %all-to-all-start.3 = ((bf16[16,64,128]{2,1,0:T(8,128)(2,1)}), bf16[16,64,128]{2,1,0:T(8,128)(2,1)S(1)}, u32[]{:S(2)}, u32[]{:S(2)}) async-start(bf16[16,64,128]{2,1,0:T(8,128)(2,1)} %sum_parts.1), calls=%async_computation.3 | async-start | bytes 524288 | tf_op jit(solution)/shard_map/all_to_all | solution.py:335
  96.2 11.7 %copy-start.4 = (s32[4]{0:T(128)S(1)}, s32[4]{0:T(128)}, u32[]{:S(2)}) copy-start(s32[4]{0:T(128)} %lengths_ref.1) | copy-start | bytes 52

commit v4 on v2

--- a/solution.py
+++ b/solution.py
@@ -12,8 +12,9 @@
 X, CORES = 4, 2
 DP, TENSOR = ("x", "y"), ("z", "core")
 LANES = 128
+WEIGHTS = (1, 1, 50000, 1)
 KERNEL_VMEM = 8 << 20
-PROJECT_VMEM, PROJECT_ROWS, PROJECT_CHIPS = 60 << 20, 1024, 4
+PROJECT_VMEM, PROJECT_ROWS = 60 << 20, 1024
 
 
 def cost(flops, size):
@@ -66,60 +67,121 @@
 
 
 def project_kernel(hidden_ref, other_ref, matrix_ref, other_matrix_ref, *refs):
-    *out_refs, own, own_other = refs
-    columns = out_refs[0].shape[0]
-    chips, span = len(out_refs), CORES * columns
+    *out_refs, own_ref, far_ref, chosen, chosen_other = refs
+    columns, span = own_ref.shape[0], out_refs[0].shape[0]
+    chips = matrix_ref.shape[1] // span
+    last = len(out_refs) * span
 
     @pl.when(pl.program_id(0) == 0)
     def _():
         here, upper = lax.axis_index("z"), lax.axis_index("core") == 1
         low = lax.broadcasted_iota(jnp.int32, (matrix_ref.shape[0], span), 1) < columns
-        for source, chosen in ((matrix_ref, own), (other_matrix_ref, own_other)):
-            for k in range(0, chips, 2):
-                pair = []
-                for i in range(2):
-                    start = pl.multiple_of(lax.rem(here + k + i, chips) * span, span)
-                    block = source[:, pl.ds(start, span)]
-                    turned = jnp.concatenate([block[:, columns:], block[:, :columns]], axis=1)
-                    pair.append(jnp.where(upper == (i == 1), block, turned))
-                chosen[:, k * columns : (k + 2) * columns] = jnp.where(low, pair[0], pair[1])
-
-    for first in range(0, chips, PROJECT_CHIPS):
-        last = min(first + PROJECT_CHIPS, chips)
-        lanes = slice(first * columns, last * columns)
+
+        def block(source, chip):
+            start = pl.multiple_of(lax.rem(chip + chips, chips) * span, span)
+            return source[:, pl.ds(start, span)]
+
+        def turned(value):
+            return jnp.concatenate([value[:, columns:], value[:, :columns]], axis=1)
+
+        for source, to in ((matrix_ref, chosen), (other_matrix_ref, chosen_other)):
+            for i in range(len(out_refs)):
+                hops = len(out_refs) - i
+                chip = here + jnp.where(upper, -hops, hops)
+                to[:, i * span : (i + 1) * span] = block(source, chip)
+            own, far = block(source, here), block(source, here + chips // 2)
+            own = jnp.where(upper, turned(own), own)
+            far = jnp.where(upper, far, turned(far))
+            to[:, last:] = jnp.where(low, own, far)
+
+    for first in range(0, last + span, 2 * span):
+        lanes = slice(first, first + 2 * span)
         product = jnp.dot(
-            hidden_ref[...], own[:, lanes], preferred_element_type=jnp.float32
-        ) + jnp.dot(other_ref[...], own_other[:, lanes], preferred_element_type=jnp.float32)
-        product = product.astype(out_refs[0].dtype).T
-        for k in range(first, last):
-            out_refs[k][...] = product[(k - first) * columns : (k - first + 1) * columns]
+            hidden_ref[...], chosen[:, lanes], preferred_element_type=jnp.float32
+        ) + jnp.dot(other_ref[...], chosen_other[:, lanes], preferred_element_type=jnp.float32)
+        product = product.astype(own_ref.dtype).T
+        for i in range(2):
+            block = product[i * span : (i + 1) * span]
+            if first + i * span < last:
+                out_refs[first // span + i][...] = block
+            else:
+                own_ref[...] = block[:columns]
+                far_ref[...] = block[columns:]
 
 
 def project(hidden, other, matrix, other_matrix, columns):
     tokens, features = hidden.shape
     width = matrix.shape[1]
-    chips = width // (CORES * columns)
+    span = CORES * columns
+    hops = width // span // 2 - 1
     rows = min(PROJECT_ROWS, tokens)
     row_spec = pl.BlockSpec((rows, features), lambda t: (t, 0))
     matrix_spec = pl.BlockSpec(matrix.shape, lambda t: (0, 0))
+    heights = [span] * hops + [columns] * 2
     return pl.pallas_call(
         project_kernel,
         grid=(tokens // rows,),
-        out_shape=[jax.ShapeDtypeStruct((columns, tokens), hidden.dtype)] * chips,
+        out_shape=[jax.ShapeDtypeStruct((height, tokens), hidden.dtype) for height in heights],
         in_specs=[row_spec] * 2 + [matrix_spec] * 2,
-        out_specs=[pl.BlockSpec((columns, rows), lambda t: (0, t))] * chips,
-        scratch_shapes=[pltpu.VMEM((features, chips * columns), matrix.dtype)] * 2,
-        cost_estimate=cost(
-            2 * tokens * features * width,
-            2 * hidden.size + 2 * matrix.size + tokens * chips * columns,
-        ),
+        out_specs=[pl.BlockSpec((height, rows), lambda t: (0, t)) for height in heights],
+        scratch_shapes=[pltpu.VMEM((features, sum(heights)), matrix.dtype)] * 2,
+        cost_estimate=cost(0, 0),
         compiler_params=pltpu.CompilerParams(vmem_limit_bytes=PROJECT_VMEM),
         name="project",
     )(hidden, other, matrix, other_matrix)
 
 
-def add(a, b):
+def vmem_call(kernel, name, weight, out_shape, *operands):
+    size = operands[0].size
+    several = isinstance(out_shape, list)
+    spec = pl.BlockSpec(memory_space=pltpu.VMEM)
+    return pl.pallas_call(
+        kernel,
+        out_shape=out_shape,
+        in_specs=[spec] * len(operands),
+        out_specs=[spec] * len(out_shape) if several else spec,
+        cost_estimate=cost(weight * size, 3 * size),
+        compiler_params=pltpu.CompilerParams(vmem_limit_bytes=KERNEL_VMEM),
+        name=name,
+    )(*operands)
+
+
+def like(value, rows=None):
+    return jax.ShapeDtypeStruct((rows or value.shape[0], *value.shape[1:]), value.dtype)
+
+
+def sum_refs(a, b):
     return (a.astype(jnp.float32) + b.astype(jnp.float32)).astype(a.dtype)
+
+
+def add_kernel(part_ref, came_ref, out_ref):
+    out_ref[...] = sum_refs(part_ref[...], came_ref[...])
+
+
+def add_own_kernel(part_ref, came_ref, out_ref):
+    columns = came_ref.shape[0]
+    mine = pl.ds(pl.multiple_of(lax.axis_index("core") * columns, columns), columns)
+    out_ref[...] = part_ref[...]
+    out_ref[mine] = sum_refs(part_ref[mine], came_ref[...])
+
+
+def split_kernel(chain_ref, own_ref, kept_ref, sent_ref):
+    columns = own_ref.shape[0]
+    core = lax.axis_index("core")
+    mine = pl.ds(pl.multiple_of(core * columns, columns), columns)
+    theirs = pl.ds(pl.multiple_of((1 - core) * columns, columns), columns)
+    kept_ref[...] = sum_refs(own_ref[...], chain_ref[mine])
+    sent_ref[...] = chain_ref[theirs]
+
+
+def hop(value):
+    n = lax.axis_size("z")
+    pairs = [
+        (z * CORES + core, (z + (1 - 2 * core)) % n * CORES + core)
+        for z in range(n)
+        for core in range(CORES)
+    ]
+    return lax.ppermute(value, TENSOR, pairs)
 
 
 def along(axis, value, step):
@@ -286,17 +348,15 @@
     row = lax.all_to_all(copies, "y", 0, 0)
 
     parts = project(hidden, other, value_matrix, other_matrix, adapter_up_store.shape[2])
-    far = len(parts) // 2
-    ahead, behind = parts[far], parts[far + 1]
-    for k in range(far - 1, -1, -1):
-        ahead = along("z", ahead, 1)
-        if k:
-            ahead = add(ahead, parts[k])
-    for k in range(far + 2, len(parts) + 1):
-        behind = along("z", behind, -1)
-        if k < len(parts):
-            behind = add(behind, parts[k])
-    base = (parts[0], ahead, behind)
+    *parts, rollout_adapter = lax.optimization_barrier((*parts, rollout_adapter))
+    *parts, own, far = parts
+    chain = vmem_call(add_own_kernel, "add_own", WEIGHTS[0], like(parts[0]), parts[0], hop(far))
+    for i, part in enumerate(parts[1:], 1):
+        chain = vmem_call(add_kernel, "add_parts", WEIGHTS[i], like(part), part, hop(chain))
+    kept, sent = vmem_call(
+        split_kernel, "split", WEIGHTS[-1], [like(own), like(own)], hop(chain), own
+    )
+    base = (kept, along("core", sent, 1))
 
     here = lax.axis_index("x")
     mine = jnp.arange(X, dtype=jnp.int32)[:, None] == here

time: 115 us -> 110 us (0.957)
  starting transfers between devices: 58.5 us -> 52 us
  other arithmetic: 5.13 us -> 0.36 us
  local copies, waits for them, and re-layouts: 1.45 us -> 5.59 us
  Pallas kernels: 15.1 us -> 17.6 us
  waiting for transfers between devices: 27.9 us -> 25.6 us
  blocking collectives: 5.59 us -> 7.44 us
    ppermute x9 -> x3, starting transfers between devices: 40.8 us -> 12.6 us  [along(): return lax.ppermute(value, axis, [(i, (i + step) % n) for i in range(n)])]
    ppermute x0 -> x4, starting transfers between devices: none -> 20.4 us  [hop(): return lax.ppermute(value, TENSOR, pairs)]
    all_to_all x1, waiting for transfers between devices: 11.8 us -> 0.01 us  [on_device(): row = lax.all_to_all(copies, 'y', 0, 0)]
    all_to_all x2, waiting for transfers between devices: 3.22 us -> 13.9 us  [on_device(): down = lax.all_to_all(down, TENSOR, 0, 0)]
    ppermute x9 -> x3, waiting for transfers between devices: 12.9 us -> 2.93 us  [along(): return lax.ppermute(value, axis, [(i, (i + step) % n) for i in range(n)])]
    all_to_all x1, waiting for transfers between devices: 0.01 us -> 5.8 us  [on_device(): factors = lax.all_to_all(sent, 'x', 0, 0)]
    convert_element_type x5 -> x0, other arithmetic: 4.77 us -> none  [add(): return (a.astype(jnp.float32) + b.astype(jnp.float32)).astype(a.dtype)]
    unnamed x20, local copies, waits for them, and re-layouts: 1.36 us -> 5.51 us
  transfers between devices with their start and end apart: 13 -> 11, of which waited for: 4 -> 5; matrix products, arithmetic and copies ran while one was open for 5% -> 0% of each run, Pallas kernels for 12% -> 15%
where the time goes in v4:
time: 110 us; the launch traced here: 109 us
  starting transfers between devices  52 us (47%)
  waiting for transfers between devices  25.6 us (23%)
  Pallas kernels  17.6 us (16%)
  blocking collectives  7.44 us (7%)
  local copies, waits for them, and re-layouts  5.59 us (5%)
    ppermute x4, starting transfers between devices, hop(): return lax.ppermute(value, TENSOR, pairs)  20.4 us
    all_to_all x2, waiting for transfers between devices, on_device(): down = lax.all_to_all(down, TENSOR, 0, 0)  13.9 us
    ppermute x3, starting transfers between devices, along(): return lax.ppermute(value, axis, [(i, (i + step) % n) for i in range(n)])  12.6 us
    all_to_all x2, starting transfers between devices, on_device(): down = lax.all_to_all(down, TENSOR, 0, 0)  11.7 us
    psum x1, blocking collectives, on_device(): lax.psum(jnp.where(mine, rollout_adapter[None, :], 0), 'x').reshape(-1)  7.44 us
    pallas_call x1, Pallas kernels, project(): pl.pallas_call(project_kernel, grid=(tokens // rows,), out_shape=[jax.Sha...  6.3 us
    all_to_all x1, waiting for transfers between devices, on_device(): factors = lax.all_to_all(sent, 'x', 0, 0)  5.8 us
    unnamed x20, local copies, waits for them, and re-layouts  5.51 us
  transfers between devices with their start and end apart: 11, of which 5 were waited for; matrix products, arithmetic and copies ran while one was open for 0% of the time, Pallas kernels for 15%

profile of v4, /device:TPU:1, one launch (start us, length us, event | category | flops | bytes accessed | tf_op | source)
XLA Modules:
  0.0 108.8 jit_solution(1064382132608452395)
XLA Ops:
  0.0 8.8 %collective-permute-start = (bf16[2048,512]{1,0:T(8,128)(2,1)}, bf16[2048,512]{1,0:T(8,128)(2,1)S(1)}, u32[]{:S(2)}, u32[]{:S(2)}) collective-permute-start(bf16[2048,512]{1,0:T(8,128)(2,1)} %hidden_ref.3), channel_id=1, source_target_pairs={{0,1},{1,0},{2,3},{3,2},{4,5},{5,4},{6,7},{7,6},{8,9},{9,8},{10,11... | collective-permute-start | bytes 6291464 | tf_op jit(solution)/shard_map/ppermute | solution.py:189
  8.8 2.1 %factor_copies.1 = bf16[8,144,512]{2,1,0:T(8,128)(2,1)} custom-call(bf16[2,64,512]{2,1,0:T(8,128)(2,1)} %bitcast.2, bf16[2,64,64]{2,1,0:T(8,128)(2,1)} %up_ref.1), custom_call_target="tpu_custom_call" | custom-call | bytes 1179648 | tf_op jit(solution)/shard_map/factor_copies/pallas_call | solution.py:52
  10.9 3.6 %all-to-all-start = ((bf16[8,144,512]{2,1,0:T(8,128)(2,1)}), bf16[8,144,512]{2,1,0:T(8,128)(2,1)S(1)}, u32[]{:S(2)}, u32[]{:S(2)}) async-start(bf16[8,144,512]{2,1,0:T(8,128)(2,1)} %factor_copies.1), calls=%async_computation | async-start | bytes 2359296 | tf_op jit(solution)/shard_map/all_to_all | solution.py:348
  14.4 1.9 %collective-permute-start.1 = (bf16[512,1024]{1,0:T(8,128)(2,1)}, bf16[512,1024]{1,0:T(8,128)(2,1)}, u32[]{:S(2)}, u32[]{:S(2)}) collective-permute-start(bf16[512,1024]{1,0:T(8,128)(2,1)} %matrix_ref.1), channel_id=1, source_target_pairs={{0,1},{1,0},{2,3},{3,2},{4,5},{5,4},{6,7},{7,6},{8,9},{9,8},{10,11... | collective-permute-start | bytes 3145736 | tf_op jit(solution)/shard_map/ppermute | solution.py:189
  16.4 2.9 %collective-permute-done.1.other_matrix_ref = bf16[512,1024]{1,0:T(8,128)(2,1)} collective-permute-done((bf16[512,1024]{1,0:T(8,128)(2,1)}, bf16[512,1024]{1,0:T(8,128)(2,1)}, u32[]{:S(2)}, u32[]{:S(2)}) %collective-permute-start.1) | collective-permute-done | bytes 1048608 | tf_op jit(solution)/shard_map/ppermute | solution.py:189
  19.3 1.3 %copy-done.7 = bf16[2048,512]{1,0:T(8,128)(2,1)} copy-done((bf16[2048,512]{1,0:T(8,128)(2,1)}, bf16[2048,512]{1,0:T(8,128)(2,1)S(1)}, u32[]{:S(2)}) %copy-start.7) | copy-done | bytes 2097176
  20.7 6.3 %project.1 = (bf16[128,2048]{1,0:T(8,128)(2,1)}, bf16[128,2048]{1,0:T(8,128)(2,1)}, bf16[128,2048]{1,0:T(8,128)(2,1)}, bf16[64,2048]{1,0:T(8,128)(2,1)}, bf16[64,2048]{1,0:T(8,128)(2,1)}) custom-call(bf16[2048,512]{1,0:T(8,128)(2,1)} %hidden_ref.3, bf16[2048,512]{1,0:T(8,128)(2,1)} %copy-done.7, bf16[512,1024]{1,0:T(8,128)(2,1)} %matrix_ref.1, ...), custom_call_target="tpu_custom_call" | custom-call | tf_op jit(solution)/shard_map/project/pallas_call | solution.py:121
  27.0 8.5 %collective-permute-start.2 = (bf16[64,2048]{1,0:T(8,128)(2,1)}, bf16[64,2048]{1,0:T(8,128)(2,1)S(1)}, u32[]{:S(2)}, u32[]{:S(2)}) collective-permute-start(bf16[64,2048]{1,0:T(8,128)(2,1)} %get-tuple-element.30), channel_id=1, source_target_pairs={{0,2},{1,15},{2,4},{3,1},{4,6},{5,3},{6,8},{7,5},{8,10},{9,7},{10,... | collective-permute-start | bytes 786440 | tf_op jit(solution)/shard_map/ppermute | solution.py:184
  35.7 7.4 %psum.7 = s32[16]{0:T(128)S(1)} all-reduce(s32[16]{0:T(128)S(1)} %eq.28), channel_id=1, replica_groups=mesh['x'=4,'y'=8,'z'=8,'core'=2] {'x'}, use_global_device_ids=true, to_apply=%region_0.1 | all-reduce | flops 16 | bytes 128 | tf_op jit(solution)/shard_map/psum | solution.py:363
  45.3 2.0 %collective-permute-start.3 = (bf16[128,2048]{1,0:T(8,128)(2,1)}, bf16[128,2048]{1,0:T(8,128)(2,1)}, u32[]{:S(2)}, u32[]{:S(2)}) collective-permute-start(bf16[128,2048]{1,0:T(8,128)(2,1)} %add_own.1), channel_id=1, source_target_pairs={{0,2},{1,15},{2,4},{3,1},{4,6},{5,3},{6,8},{7,5},{8,10},{9,7},{10,... | collective-permute-start | bytes 1572872 | tf_op jit(solution)/shard_map/ppermute | solution.py:184
  49.2 3.7 %all-to-all-start.1 = ((bf16[4,288,512]{2,1,0:T(8,128)(2,1)}), bf16[4,288,512]{2,1,0:T(8,128)(2,1)S(1)}, u32[]{:S(2)}, u32[]{:S(2)}) async-start(bf16[4,288,512]{2,1,0:T(8,128)(2,1)} %copy-done.1), calls=%async_computation.1 | async-start | bytes 2359296 | tf_op jit(solution)/shard_map/all_to_all | solution.py:372
  52.9 2.9 %collective-permute-done.3.came_ref = bf16[128,2048]{1,0:T(8,128)(2,1)} collective-permute-done((bf16[128,2048]{1,0:T(8,128)(2,1)}, bf16[128,2048]{1,0:T(8,128)(2,1)}, u32[]{:S(2)}, u32[]{:S(2)}) %collective-permute-start.3) | collective-permute-done | bytes 524320 | tf_op jit(solution)/shard_map/ppermute | solution.py:184
  56.8 2.0 %add_parts.2 = bf16[128,2048]{1,0:T(8,128)(2,1)} custom-call(bf16[128,2048]{1,0:T(8,128)(2,1)S(1)} %copy-done.2, bf16[128,2048]{1,0:T(8,128)(2,1)} %collective-permute-done.3.came_ref), custom_call_target="tpu_custom_call" | custom-call | flops 262144 | bytes 1572864 | tf_op jit(solution)/shard_map/add_parts/pallas_call | solution.py:138
  58.8 5.2 %collective-permute-start.4 = (bf16[128,2048]{1,0:T(8,128)(2,1)}, bf16[128,2048]{1,0:T(8,128)(2,1)}, u32[]{:S(2)}, u32[]{:S(2)}) collective-permute-start(bf16[128,2048]{1,0:T(8,128)(2,1)} %add_parts.2), channel_id=1, source_target_pairs={{0,2},{1,15},{2,4},{3,1},{4,6},{5,3},{6,8},{7,5},{8,10},{9,7},{10,... | collective-permute-start | bytes 1572872 | tf_op jit(solution)/shard_map/ppermute | solution.py:184
  64.0 5.8 %all-to-all-done.1.factor_ref.refs_3_ = bf16[4,288,512]{2,1,0:T(8,128)(2,1)S(1)} async-done(((bf16[4,288,512]{2,1,0:T(8,128)(2,1)}), bf16[4,288,512]{2,1,0:T(8,128)(2,1)S(1)}, u32[]{:S(2)}, u32[]{:S(2)}) %all-to-all-start.1) | async-done | bytes 1179680 | tf_op jit(solution)/shard_map/all_to_all | solution.py:372
  69.8 2.0 %down_projection.1 = bf16[16,64,128]{2,1,0:T(8,128)(2,1)} custom-call(s32[4]{0:T(128)S(1)} %and_select_fusion.own_row_ref, bf16[2048,512]{1,0:T(8,128)(2,1)S(1)} %copy-done, bf16[4,288,512]{2,1,0:T(8,128)(2,1)S(1)} %all-to-all-done.1.factor_ref.refs_3_), custom_call_target="tpu_custom_call" | custom-call | flops 134217728 | bytes 2359296 | tf_op jit(solution)/shard_map/down_projection/pallas_call | solution.py:256
  71.8 8.3 %all-to-all-start.2 = ((bf16[16,64,128]{2,1,0:T(8,128)(2,1)}), bf16[16,64,128]{2,1,0:T(8,128)(2,1)S(1)}, u32[]{:S(2)}, u32[]{:S(2)}) async-start(bf16[16,64,128]{2,1,0:T(8,128)(2,1)} %down_projection.1), calls=%async_computation.2 | async-start | bytes 524288 | tf_op jit(solution)/shard_map/all_to_all | solution.py:374
  81.2 1.2 %add_parts.3 = bf16[128,2048]{1,0:T(8,128)(2,1)S(1)} custom-call(bf16[128,2048]{1,0:T(8,128)(2,1)S(1)} %copy-done.6, bf16[128,2048]{1,0:T(8,128)(2,1)} %collective-permute-done.4.came_ref), custom_call_target="tpu_custom_call" | custom-call | flops 13107200000 | bytes 1572864 | tf_op jit(solution)/shard_map/add_parts/pallas_call | solution.py:138
  82.4 4.6 %collective-permute-start.5 = (bf16[128,2048]{1,0:T(8,128)(2,1)S(1)}, bf16[128,2048]{1,0:T(8,128)(2,1)S(1)}, u32[]{:S(2)}, u32[]{:S(2)}) collective-permute-start(bf16[128,2048]{1,0:T(8,128)(2,1)S(1)} %add_parts.3), channel_id=1, source_target_pairs={{0,2},{1,15},{2,4},{3,1},{4,6},{5,3},{6,8},{7,5},{8,10},{9,7},{10,... | collective-permute-start | bytes 1572872 | tf_op jit(solution)/shard_map/ppermute | solution.py:184
  87.0 4.8 %all-to-all-done.2.parts_ref = bf16[16,64,128]{2,1,0:T(8,128)(2,1)S(1)} async-done(((bf16[16,64,128]{2,1,0:T(8,128)(2,1)}), bf16[16,64,128]{2,1,0:T(8,128)(2,1)S(1)}, u32[]{:S(2)}, u32[]{:S(2)}) %all-to-all-start.2) | async-done | bytes 262176 | tf_op jit(solution)/shard_map/all_to_all | solution.py:374
  92.6 3.4 %all-to-all-start.3 = ((bf16[16,64,128]{2,1,0:T(8,128)(2,1)}), bf16[16,64,128]{2,1,0:T(8,128)(2,1)S(1)}, u32[]{:S(2)}, u32[]{:S(2)}) async-start(bf16[16,64,128]{2,1,0:T(8,128)(2,1)} %sum_parts.1), calls=%async_computation.3 | async-start | bytes 524288 | tf_op jit(solution)/shard_map/all_to_all | solution.py:376
  96.2 1.9 %collective-permute-start.6 = (bf16[64,2048]{1,0:T(8,128)(2,1)S(1)}, bf16[64,2048]{1,0:T(8,128)(2,1)S(1)}, u32[]{:S(2)}, u32[]{:S(2)}) collective-permute-start(bf16[64,2048]{1,0:T(8,128)(2,1)S(1)} %get-tuple-element.33), channel_id=1, source_target_pairs={{0,1},{1,0},{2,3},{3,2},{4,5},{5,4},{6,7},{7,6},{8,9},{9,8},{10,11... | collective-permute-start | bytes 786440 | tf_op jit(solution)/shard_map/ppermute | solution.py:189
  98.1 9.1 %all-to-all-done.3.refs_2_ = bf16[16,64,128]{2,1,0:T(8,128)(2,1)S(1)} async-done(((bf16[16,64,128]{2,1,0:T(8,128)(2,1)}), bf16[16,64,128]{2,1,0:T(8,128)(2,1)S(1)}, u32[]{:S(2)}, u32[]{:S(2)}) %all-to-all-start.3) | async-done | bytes 262176 | tf_op jit(solution)/shard_map/all_to_all | solution.py:376
  107.2 1.6 %add_update.1 = bf16[64,2048]{1,0:T(8,128)(2,1)} custom-call(s32[4]{0:T(128)S(1)} %and_select_fusion.own_row_ref, s32[4]{0:T(128)S(1)} %copy-done.5, bf16[64,2048]{1,0:T(8,128)(2,1)S(1)} %get-tuple-element.32.refs_0_, bf16[64,2048]{1,0:T(8,128)(2,1)S(1)} %collective-permute-done.6.refs_1_, bf16[16,64,128]{2,1,0:T(8,128)(2,1)S(1)} %all-to-all-done.3.refs_2_, ...), custom_call_target="tpu_custom_call" | custom-call | flops 16777216 | bytes 1310720 | tf_op jit(solution)/shard_map/add_update/pallas_call | solution.py:323
  (35 shorter events, 7.1 us)
Async XLA Ops:
  0.0 19.3 %collective-permute-start = (bf16[2048,512]{1,0:T(8,128)(2,1)}, bf16[2048,512]{1,0:T(8,128)(2,1)S(1)}, u32[]{:S(2)}, u32[]{:S(2)}) collective-permute-start(bf16[2048,512]{1,0:T(8,128)(2,1)} %hidden_ref.3), channel_id=1, source_target_pairs={{0,1},{1,0},{2,3},{3,2},{4,5},{5,4},{6,7},{7,6},{8,9},{9,8},{10,11... | collective-permute-start | bytes 6291464 | tf_op jit(solution)/shard_map/ppermute | solution.py:189
  10.9 36.5 %all-to-all-start = ((bf16[8,144,512]{2,1,0:T(8,128)(2,1)}), bf16[8,144,512]{2,1,0:T(8,128)(2,1)S(1)}, u32[]{:S(2)}, u32[]{:S(2)}) async-start(bf16[8,144,512]{2,1,0:T(8,128)(2,1)} %factor_copies.1), calls=%async_computation | async-start | bytes 2359296 | tf_op jit(solution)/shard_map/all_to_all | solution.py:348
  14.4 4.9 %collective-permute-start.1 = (bf16[512,1024]{1,0:T(8,128)(2,1)}, bf16[512,1024]{1,0:T(8,128)(2,1)}, u32[]{:S(2)}, u32[]{:S(2)}) collective-permute-start(bf16[512,1024]{1,0:T(8,128)(2,1)} %matrix_ref.1), channel_id=1, source_target_pairs={{0,1},{1,0},{2,3},{3,2},{4,5},{5,4},{6,7},{7,6},{8,9},{9,8},{10,11... | collective-permute-start | bytes 3145736 | tf_op jit(solution)/shard_map/ppermute | solution.py:189
  16.4 19.1 %copy-start.8 = (s32[4]{0:T(128)S(1)}, s32[4]{0:T(128)}, u32[]{:S(2)}) copy-start(s32[4]{0:T(128)} %param.12) | copy-start | bytes 52
  16.4 26.7 %copy-start.9 = (s32[64]{0:T(128)S(1)}, s32[64]{0:T(128)}, u32[]{:S(2)}) copy-start(s32[64]{0:T(128)} %param.11) | copy-start | bytes 772
  19.3 1.3 %copy-start.7 = (bf16[2048,512]{1,0:T(8,128)(2,1)}, bf16[2048,512]{1,0:T(8,128)(2,1)S(1)}, u32[]{:S(2)}) copy-start(bf16[2048,512]{1,0:T(8,128)(2,1)S(1)} %collective-permute-done.other_ref) | copy-start | bytes 6291460
  27.0 16.3 %collective-permute-start.2 = (bf16[64,2048]{1,0:T(8,128)(2,1)}, bf16[64,2048]{1,0:T(8,128)(2,1)S(1)}, u32[]{:S(2)}, u32[]{:S(2)}) collective-permute-start(bf16[64,2048]{1,0:T(8,128)(2,1)} %get-tuple-element.30), channel_id=1, source_target_pairs={{0,2},{1,15},{2,4},{3,1},{4,6},{5,3},{6,8},{7,5},{8,10},{9,7},{10,... | collective-permute-start | bytes 786440 | tf_op jit(solution)/shard_map/ppermute | solution.py:184
  43.3 1.0 copy-start.3
  45.3 10.5 %collective-permute-start.3 = (bf16[128,2048]{1,0:T(8,128)(2,1)}, bf16[128,2048]{1,0:T(8,128)(2,1)}, u32[]{:S(2)}, u32[]{:S(2)}) collective-permute-start(bf16[128,2048]{1,0:T(8,128)(2,1)} %add_own.1), channel_id=1, source_target_pairs={{0,2},{1,15},{2,4},{3,1},{4,6},{5,3},{6,8},{7,5},{8,10},{9,7},{10,... | collective-permute-start | bytes 1572872 | tf_op jit(solution)/shard_map/ppermute | solution.py:184
  48.1 1.0 copy-start.1
  49.2 20.6 %copy-start = (bf16[2048,512]{1,0:T(8,128)(2,1)S(1)}, bf16[2048,512]{1,0:T(8,128)(2,1)}, u32[]{:S(2)}) copy-start(bf16[2048,512]{1,0:T(8,128)(2,1)} %hidden_ref.3) | copy-start | bytes 6291460
  49.2 20.6 %all-to-all-start.1 = ((bf16[4,288,512]{2,1,0:T(8,128)(2,1)}), bf16[4,288,512]{2,1,0:T(8,128)(2,1)S(1)}, u32[]{:S(2)}, u32[]{:S(2)}) async-start(bf16[4,288,512]{2,1,0:T(8,128)(2,1)} %copy-done.1), calls=%async_computation.1 | async-start | bytes 2359296 | tf_op jit(solution)/shard_map/all_to_all | solution.py:372
  55.8 1.0 copy-start.2
  58.8 21.4 %collective-permute-start.4 = (bf16[128,2048]{1,0:T(8,128)(2,1)}, bf16[128,2048]{1,0:T(8,128)(2,1)}, u32[]{:S(2)}, u32[]{:S(2)}) collective-permute-start(bf16[128,2048]{1,0:T(8,128)(2,1)} %add_parts.2), channel_id=1, source_target_pairs={{0,2},{1,15},{2,4},{3,1},{4,6},{5,3},{6,8},{7,5},{8,10},{9,7},{10,... | collective-permute-start | bytes 1572872 | tf_op jit(solution)/shard_map/ppermute | solution.py:184
  71.8 20.0 %all-to-all-start.2 = ((bf16[16,64,128]{2,1,0:T(8,128)(2,1)}), bf16[16,64,128]{2,1,0:T(8,128)(2,1)S(1)}, u32[]{:S(2)}, u32[]{:S(2)}) async-start(bf16[16,64,128]{2,1,0:T(8,128)(2,1)} %down_projection.1), calls=%async_computation.2 | async-start | bytes 524288 | tf_op jit(solution)/shard_map/all_to_all | solution.py:374
  80.1 1.0 copy-start.6
  82.4 13.7 %copy-start.4 = (bf16[64,2048]{1,0:T(8,128)(2,1)S(1)}, bf16[64,2048]{1,0:T(8,128)(2,1)}, u32[]{:S(2)}) copy-start(bf16[64,2048]{1,0:T(8,128)(2,1)} %get-tuple-element.31.own_ref) | copy-start | bytes 786436
  82.4 24.8 %copy-start.5 = (s32[4]{0:T(128)S(1)}, s32[4]{0:T(128)}, u32[]{:S(2)}) copy-start(s32[4]{0:T(128)} %lengths_ref.1) | copy-start | bytes 52
  82.4 13.7 %collective-permute-start.5 = (bf16[128,2048]{1,0:T(8,128)(2,1)S(1)}, bf16[128,2048]{1,0:T(8,128)(2,1)S(1)}, u32[]{:S(2)}, u32[]{:S(2)}) collective-permute-start(bf16[128,2048]{1,0:T(8,128)(2,1)S(1)} %add_parts.3), channel_id=1, source_target_pairs={{0,2},{1,15},{2,4},{3,1},{4,6},{5,3},{6,8},{7,5},{8,10},{9,7},{10,... | collective-permute-start | bytes 1572872 | tf_op jit(solution)/shard_map/ppermute | solution.py:184
  92.6 14.6 %all-to-all-start.3 = ((bf16[16,64,128]{2,1,0:T(8,128)(2,1)}), bf16[16,64,128]{2,1,0:T(8,128)(2,1)S(1)}, u32[]{:S(2)}, u32[]{:S(2)}) async-start(bf16[16,64,128]{2,1,0:T(8,128)(2,1)} %sum_parts.1), calls=%async_computation.3 | async-start | bytes 524288 | tf_op jit(solution)/shard_map/all_to_all | solution.py:376
  96.2 11.0 %collective-permute-start.6 = (bf16[64,2048]{1,0:T(8,128)(2,1)S(1)}, bf16[64,2048]{1,0:T(8,128)(2,1)S(1)}, u32[]{:S(2)}, u32[]{:S(2)}) collective-permute-start(bf16[64,2048]{1,0:T(8,128)(2,1)S(1)} %get-tuple-element.33), channel_id=1, source_target_pairs={{0,1},{1,0},{2,3},{3,2},{4,5},{5,4},{6,7},{7,6},{8,9},{9,8},{10,11... | collective-permute-start | bytes 786440 | tf_op jit(solution)/shard_map/ppermute | solution.py:189

commit v5 on v4

--- a/solution.py
+++ b/solution.py
@@ -12,9 +12,9 @@
 X, CORES = 4, 2
 DP, TENSOR = ("x", "y"), ("z", "core")
 LANES = 128
-WEIGHTS = (1, 1, 50000, 1)
+WEIGHTS = (1, 1, 1, 50000, 1)
 KERNEL_VMEM = 8 << 20
-PROJECT_VMEM, PROJECT_ROWS = 60 << 20, 1024
+PROJECT_VMEM, PROJECT_PARTS = 60 << 20, 2
 
 
 def cost(flops, size):
@@ -66,69 +66,92 @@
     )(down, up)
 
 
-def project_kernel(hidden_ref, other_ref, matrix_ref, other_matrix_ref, *refs):
-    *out_refs, own_ref, far_ref, chosen, chosen_other = refs
-    columns, span = own_ref.shape[0], out_refs[0].shape[0]
-    chips = matrix_ref.shape[1] // span
-    last = len(out_refs) * span
-
-    @pl.when(pl.program_id(0) == 0)
-    def _():
-        here, upper = lax.axis_index("z"), lax.axis_index("core") == 1
-        low = lax.broadcasted_iota(jnp.int32, (matrix_ref.shape[0], span), 1) < columns
-
-        def block(source, chip):
-            start = pl.multiple_of(lax.rem(chip + chips, chips) * span, span)
-            return source[:, pl.ds(start, span)]
-
-        def turned(value):
-            return jnp.concatenate([value[:, columns:], value[:, :columns]], axis=1)
-
-        for source, to in ((matrix_ref, chosen), (other_matrix_ref, chosen_other)):
-            for i in range(len(out_refs)):
-                hops = len(out_refs) - i
-                chip = here + jnp.where(upper, -hops, hops)
-                to[:, i * span : (i + 1) * span] = block(source, chip)
-            own, far = block(source, here), block(source, here + chips // 2)
-            own = jnp.where(upper, turned(own), own)
-            far = jnp.where(upper, far, turned(far))
-            to[:, last:] = jnp.where(low, own, far)
-
-    for first in range(0, last + span, 2 * span):
-        lanes = slice(first, first + 2 * span)
-        product = jnp.dot(
-            hidden_ref[...], chosen[:, lanes], preferred_element_type=jnp.float32
-        ) + jnp.dot(other_ref[...], chosen_other[:, lanes], preferred_element_type=jnp.float32)
-        product = product.astype(own_ref.dtype).T
-        for i in range(2):
-            block = product[i * span : (i + 1) * span]
-            if first + i * span < last:
-                out_refs[first // span + i][...] = block
-            else:
-                own_ref[...] = block[:columns]
-                far_ref[...] = block[columns:]
-
-
-def project(hidden, other, matrix, other_matrix, columns):
+def project_kernel(hidden_ref, matrix_ref, *refs):
+    *out_refs, mine, whole, chosen, stage, in_sems, out_sems = refs
+    near_ref, middle_ref = out_refs[:2]
+    span = middle_ref.shape[0] // 2
+    columns = span // CORES
+    chips = whole.shape[1] // span
+    tokens = mine.shape[0]
+    rows = tokens // PROJECT_PARTS
+
+    take = [pltpu.make_async_copy(matrix_ref, whole, in_sems.at[0])] + [
+        pltpu.make_async_copy(
+            hidden_ref.at[pl.ds(i * rows, rows)], mine.at[pl.ds(i * rows, rows)], in_sems.at[1 + i]
+        )
+        for i in range(PROJECT_PARTS)
+    ]
+    for copy in take:
+        copy.start()
+
+    here = lax.axis_index("z")
+    low = lax.broadcasted_iota(jnp.int32, (whole.shape[0], span), 1) < columns
+
+    def block(chip):
+        start = pl.multiple_of(lax.rem(chip + chips, chips) * span, span)
+        return whole[:, pl.ds(start, span)]
+
+    def turned(value):
+        return jnp.concatenate([value[:, columns:], value[:, :columns]], axis=1)
+
+    take[0].wait()
+    for core, flip in enumerate((True, False)):
+        upper = (lax.axis_index("core") == 1) != flip
+        own, far = block(here), block(here + chips // 2)
+        own = jnp.where(upper, turned(own), own)
+        far = jnp.where(upper, far, turned(far))
+        chosen[2 * core, :, :span] = block(here + jnp.where(upper, -3, 3))
+        chosen[2 * core, :, span:] = jnp.where(low, own, far)
+        chosen[2 * core + 1, :, :span] = block(here + jnp.where(upper, -2, 2))
+        chosen[2 * core + 1, :, span:] = block(here + jnp.where(upper, -1, 1))
+
+    places = [
+        [(near_ref, 0)],
+        [(middle_ref, 0)],
+        [(out_refs[2], 0), (out_refs[5], span), (out_refs[6], span + columns)],
+        [(out_refs[3], 0), (out_refs[4], span)],
+    ]
+    leave = []
+    for g, group in enumerate(places):
+        for i in range(PROJECT_PARTS):
+            if g == 0:
+                take[1 + i].wait()
+            part = slice(i * rows, (i + 1) * rows)
+            product = jnp.dot(mine[part], chosen[g], preferred_element_type=jnp.float32)
+            stage[g, :, part] = product.astype(stage.dtype).T
+        for ref, start in group:
+            copy = pltpu.make_async_copy(
+                stage.at[g, pl.ds(start, ref.shape[0])], ref, out_sems.at[len(leave)]
+            )
+            copy.start()
+            leave.append(copy)
+    for copy in leave:
+        copy.wait()
+
+
+def project(hidden, matrix, columns):
     tokens, features = hidden.shape
-    width = matrix.shape[1]
+    kind = hidden.dtype
     span = CORES * columns
-    hops = width // span // 2 - 1
-    rows = min(PROJECT_ROWS, tokens)
-    row_spec = pl.BlockSpec((rows, features), lambda t: (t, 0))
-    matrix_spec = pl.BlockSpec(matrix.shape, lambda t: (0, 0))
-    heights = [span] * hops + [columns] * 2
+    heights = [2 * span] * 2 + [span] * 3 + [columns] * 2
+    anywhere = pl.BlockSpec(memory_space=pl.ANY)
     return pl.pallas_call(
         project_kernel,
-        grid=(tokens // rows,),
-        out_shape=[jax.ShapeDtypeStruct((height, tokens), hidden.dtype) for height in heights],
-        in_specs=[row_spec] * 2 + [matrix_spec] * 2,
-        out_specs=[pl.BlockSpec((height, rows), lambda t: (0, t)) for height in heights],
-        scratch_shapes=[pltpu.VMEM((features, sum(heights)), matrix.dtype)] * 2,
+        out_shape=[jax.ShapeDtypeStruct((height, tokens), kind) for height in heights],
+        in_specs=[anywhere] * 2,
+        out_specs=[anywhere] * len(heights),
+        scratch_shapes=[
+            pltpu.VMEM(hidden.shape, kind),
+            pltpu.VMEM(matrix.shape, kind),
+            pltpu.VMEM((4, features, 2 * span), kind),
+            pltpu.VMEM((4, 2 * span, tokens), kind),
+            pltpu.SemaphoreType.DMA((1 + PROJECT_PARTS,)),
+            pltpu.SemaphoreType.DMA((len(heights),)),
+        ],
         cost_estimate=cost(0, 0),
         compiler_params=pltpu.CompilerParams(vmem_limit_bytes=PROJECT_VMEM),
         name="project",
-    )(hidden, other, matrix, other_matrix)
+    )(hidden, matrix)
 
 
 def vmem_call(kernel, name, weight, out_shape, *operands):
@@ -150,27 +173,37 @@
     return jax.ShapeDtypeStruct((rows or value.shape[0], *value.shape[1:]), value.dtype)
 
 
-def sum_refs(a, b):
-    return (a.astype(jnp.float32) + b.astype(jnp.float32)).astype(a.dtype)
-
-
-def add_kernel(part_ref, came_ref, out_ref):
-    out_ref[...] = sum_refs(part_ref[...], came_ref[...])
-
-
-def add_own_kernel(part_ref, came_ref, out_ref):
+def sum_refs(*values):
+    total = values[0].astype(jnp.float32)
+    for value in values[1:]:
+        total += value.astype(jnp.float32)
+    return total.astype(values[0].dtype)
+
+
+def add_kernel(first, part_ref, other_ref, came_ref, out_ref):
+    other = other_ref[first : first + part_ref.shape[0]]
+    out_ref[...] = sum_refs(part_ref[...], other, came_ref[...])
+
+
+def add_far_kernel(first, part_ref, other_ref, out_ref):
+    out_ref[...] = sum_refs(part_ref[...], other_ref[first : first + part_ref.shape[0]])
+
+
+def add_own_kernel(first, part_ref, other_ref, came_ref, out_ref):
     columns = came_ref.shape[0]
-    mine = pl.ds(pl.multiple_of(lax.axis_index("core") * columns, columns), columns)
-    out_ref[...] = part_ref[...]
-    out_ref[mine] = sum_refs(part_ref[mine], came_ref[...])
-
-
-def split_kernel(chain_ref, own_ref, kept_ref, sent_ref):
+    core = lax.axis_index("core")
+    mine = pl.ds(pl.multiple_of(core * columns, columns), columns)
+    out_ref[...] = sum_refs(part_ref[...], other_ref[first : first + part_ref.shape[0]])
+    out_ref[mine] = sum_refs(out_ref[mine], came_ref[...])
+
+
+def split_kernel(first, own_ref, other_ref, chain_ref, kept_ref, sent_ref):
     columns = own_ref.shape[0]
     core = lax.axis_index("core")
     mine = pl.ds(pl.multiple_of(core * columns, columns), columns)
     theirs = pl.ds(pl.multiple_of((1 - core) * columns, columns), columns)
-    kept_ref[...] = sum_refs(own_ref[...], chain_ref[mine])
+    other = other_ref[first : first + columns]
+    kept_ref[...] = sum_refs(own_ref[...], other, chain_ref[mine])
     sent_ref[...] = chain_ref[theirs]
 
 
@@ -235,8 +268,9 @@
     )(index, row)
 
 
-def down_kernel(own_row_ref, hidden_ref, factor_ref, out_ref):
+def down_kernel(own_row_ref, hidden_ref, factor_ref, out_ref, up_ref):
     members, rank, chunk = out_ref.shape
+    packed = up_ref.shape[1]
     count = own_row_ref.shape[0]
     per = members // count
     length = per * chunk
@@ -249,16 +283,22 @@
         ).T.astype(out_ref.dtype)
         for i in range(per):
             out_ref[r * per + i] = product[:, i * chunk : (i + 1) * chunk]
+        at = count * rank + r // 2 * packed
+        up_ref[r] = factor_ref[own_row_ref[r], at : at + packed]
 
 
 def down_projection(own_row, hidden, factors, members, rank):
     tokens, features = hidden.shape
+    packed = rank * LANES // features
     return pl.pallas_call(
         down_kernel,
-        out_shape=jax.ShapeDtypeStruct((members, rank, tokens // members), hidden.dtype),
+        out_shape=[
+            jax.ShapeDtypeStruct((members, rank, tokens // members), hidden.dtype),
+            jax.ShapeDtypeStruct((own_row.shape[0], packed, features), factors.dtype),
+        ],
         in_specs=[pl.BlockSpec(memory_space=pltpu.SMEM)]
         + [pl.BlockSpec(memory_space=pltpu.VMEM)] * 2,
-        out_specs=pl.BlockSpec(memory_space=pltpu.VMEM),
+        out_specs=[pl.BlockSpec(memory_space=pltpu.VMEM)] * 2,
         cost_estimate=cost(2 * tokens * features * rank, hidden.size + tokens * rank),
         compiler_params=pltpu.CompilerParams(vmem_limit_bytes=KERNEL_VMEM),
         name="down_projection",
@@ -286,17 +326,14 @@
     )(parts)
 
 
-def final_kernel(own_row_ref, lengths_ref, *refs):
-    *base_refs, down_ref, factor_ref, out_ref = refs
+def final_kernel(lengths_ref, *refs):
+    *base_refs, down_ref, up_ref, out_ref = refs
     columns, tokens = out_ref.shape
     members, rank, chunk = down_ref.shape
-    features = factor_ref.shape[2]
-    packed = rank * LANES // features
-    count = own_row_ref.shape[0]
+    count, _, features = up_ref.shape
     per, length = members // count, tokens // count
     for r in range(count):
-        at = count * rank + r // 2 * packed
-        block = factor_ref[own_row_ref[r], at : at + packed, :]
+        block = up_ref[r]
         first = r % 2 * columns
         up = jnp.concatenate(
             [
@@ -317,19 +354,19 @@
         out_ref[:, span] = jnp.where(position < lengths_ref[r], total, 0.0).astype(out_ref.dtype)
 
 
-def final(own_row, lengths, base, down, factors):
+def final(lengths, base, down, ups):
     columns, tokens = base[0].shape
     rank = down.shape[1]
     return pl.pallas_call(
         final_kernel,
         out_shape=jax.ShapeDtypeStruct(base[0].shape, base[0].dtype),
-        in_specs=[pl.BlockSpec(memory_space=pltpu.SMEM)] * 2
+        in_specs=[pl.BlockSpec(memory_space=pltpu.SMEM)]
         + [pl.BlockSpec(memory_space=pltpu.VMEM)] * (len(base) + 2),
         out_specs=pl.BlockSpec(memory_space=pltpu.VMEM),
         cost_estimate=cost(2 * tokens * columns * rank, 4 * base[0].size + down.size),
         compiler_params=pltpu.CompilerParams(vmem_limit_bytes=KERNEL_VMEM),
         name="add_update",
-    )(own_row, lengths, *base, down, factors)
+    )(lengths, *base, down, ups)
 
 
 def on_device(
@@ -340,21 +377,32 @@
     slots_here, rank, _ = adapter_up_store.shape
     row_slots = slots_here * lax.axis_size("y")
 
-    other = along("core", hidden, 1)
-    other_matrix = along("core", value_matrix, 1)
     copies = factor_copies(
         jnp.swapaxes(adapter_down_store, 1, 2), adapter_up_store, lax.axis_size("y")
     )
     row = lax.all_to_all(copies, "y", 0, 0)
 
-    parts = project(hidden, other, value_matrix, other_matrix, adapter_up_store.shape[2])
-    *parts, rollout_adapter = lax.optimization_barrier((*parts, rollout_adapter))
-    *parts, own, far = parts
-    chain = vmem_call(add_own_kernel, "add_own", WEIGHTS[0], like(parts[0]), parts[0], hop(far))
-    for i, part in enumerate(parts[1:], 1):
-        chain = vmem_call(add_kernel, "add_parts", WEIGHTS[i], like(part), part, hop(chain))
+    columns = adapter_up_store.shape[2]
+    span = CORES * columns
+    near, middle, *parts, own, far = project(hidden, value_matrix, columns)
+    near, middle = along("core", near, 1), along("core", middle, 1)
+    *parts, own, far, rollout_adapter = lax.optimization_barrier((*parts, own, far, rollout_adapter))
+
+    def add(kernel, first, weight, name, part, *others):
+        return vmem_call(functools.partial(kernel, first), name, weight, like(part), part, *others)
+
+    chain = add(add_far_kernel, span + columns, WEIGHTS[0], "add_far", far, near)
+    chain = add(add_own_kernel, 0, WEIGHTS[1], "add_own", parts[0], near, hop(chain))
+    chain = add(add_kernel, 0, WEIGHTS[2], "add_parts", parts[1], middle, hop(chain))
+    chain = add(add_kernel, span, WEIGHTS[3], "add_parts", parts[2], middle, hop(chain))
     kept, sent = vmem_call(
-        split_kernel, "split", WEIGHTS[-1], [like(own), like(own)], hop(chain), own
+        functools.partial(split_kernel, span),
+        "split",
+        WEIGHTS[4],
+        [like(own), like(own)],
+        own,
+        near,
+        hop(chain),
     )
     base = (kept, along("core", sent, 1))
 
@@ -370,11 +418,11 @@
 
     sent = pick(local, row, X, slots_here, rank)
     factors = lax.all_to_all(sent, "x", 0, 0)
-    down = down_projection(own_row, hidden, factors, members, rank)
+    down, ups = down_projection(own_row, hidden, factors, members, rank)
     down = lax.all_to_all(down, TENSOR, 0, 0)
     down = sum_copies(down)
     down = lax.all_to_all(down, TENSOR, 0, 0)
-    return final(own_row, lengths, base, down, factors).T
+    return final(lengths, base, down, ups).T
 
 
 def solution(mesh):

time: 110 us -> 108 us (0.982)
  waiting for transfers between devices: 25.6 us -> 20 us
  starting transfers between devices: 52 us -> 55.9 us
  Pallas kernels: 17.6 us -> 20.1 us
  local copies, waits for them, and re-layouts: 5.59 us -> 3.14 us
    all_to_all x1, starting transfers between devices: 3.58 us -> 7.66 us  [on_device(): row = lax.all_to_all(copies, 'y', 0, 0)]
    ppermute x3, starting transfers between devices: 12.6 us -> 8.69 us  [along(): return lax.ppermute(value, axis, [(i, (i + step) % n) for i in range(n)])]
    unnamed x20 -> x18, local copies, waits for them, and re-layouts: 5.51 us -> 3.06 us
    all_to_all x1, waiting for transfers between devices: 5.8 us -> 3.6 us  [on_device(): factors = lax.all_to_all(sent, 'x', 0, 0)]
    all_to_all x2, waiting for transfers between devices: 13.9 us -> 12 us  [on_device(): down = lax.all_to_all(down, TENSOR, 0, 0)]
    all_to_all x2, starting transfers between devices: 11.7 us -> 13.6 us  [on_device(): down = lax.all_to_all(down, TENSOR, 0, 0)]
    ppermute x4, starting transfers between devices: 20.4 us -> 21.7 us  [hop(): return lax.ppermute(value, TENSOR, pairs)]
    pallas_call x4 -> x5, Pallas kernels: 4.09 us -> 5.24 us  [vmem_call(): pl.pallas_call(kernel, out_shape=out_shape, in_specs=[spec] * len(operand...]
  transfers between devices with their start and end apart: 11 -> 11, of which waited for: 5 -> 6; matrix products, arithmetic and copies ran while one was open for 0% -> 0% of each run, Pallas kernels for 15% -> 15%
where the time goes in v5:
time: 108 us; the launch traced here: 107 us
  starting transfers between devices  55.9 us (52%)
  Pallas kernels  20.1 us (19%)
  waiting for transfers between devices  20 us (19%)
  blocking collectives  7.46 us (7%)
  local copies, waits for them, and re-layouts  3.14 us (3%)
    ppermute x4, starting transfers between devices, hop(): return lax.ppermute(value, TENSOR, pairs)  21.7 us
    all_to_all x2, starting transfers between devices, on_device(): down = lax.all_to_all(down, TENSOR, 0, 0)  13.6 us
    all_to_all x2, waiting for transfers between devices, on_device(): down = lax.all_to_all(down, TENSOR, 0, 0)  12 us
    ppermute x3, starting transfers between devices, along(): return lax.ppermute(value, axis, [(i, (i + step) % n) for i in range(n)])  8.69 us
    all_to_all x1, starting transfers between devices, on_device(): row = lax.all_to_all(copies, 'y', 0, 0)  7.66 us
    psum x1, blocking collectives, on_device(): lax.psum(jnp.where(mine, rollout_adapter[None, :], 0), 'x').reshape(-1)  7.46 us
    pallas_call x1, Pallas kernels, project(): pl.pallas_call(project_kernel, out_shape=[jax.ShapeDtypeStruct((height, t...  5.96 us
    pallas_call x5, Pallas kernels, vmem_call(): pl.pallas_call(kernel, out_shape=out_shape, in_specs=[spec] * len(operand...  5.24 us
  transfers between devices with their start and end apart: 11, of which 6 were waited for; matrix products, arithmetic and copies ran while one was open for 0% of the time, Pallas kernels for 15%

profile of v5, /device:TPU:1, one launch (start us, length us, event | category | flops | bytes accessed | tf_op | source)
XLA Modules:
  0.0 107.2 jit_solution(5079737703880734024)
XLA Ops:
  0.0 2.1 %factor_copies.1 = bf16[8,144,512]{2,1,0:T(8,128)(2,1)} custom-call(bf16[2,64,512]{2,1,0:T(8,128)(2,1)} %bitcast.2, bf16[2,64,64]{2,1,0:T(8,128)(2,1)} %up_ref.1), custom_call_target="tpu_custom_call" | custom-call | bytes 1179648 | tf_op jit(solution)/shard_map/factor_copies/pallas_call | solution.py:52
  2.1 7.7 %all-to-all-start = ((bf16[8,144,512]{2,1,0:T(8,128)(2,1)}), bf16[8,144,512]{2,1,0:T(8,128)(2,1)S(1)}, u32[]{:S(2)}, u32[]{:S(2)}) async-start(bf16[8,144,512]{2,1,0:T(8,128)(2,1)} %factor_copies.1), calls=%async_computation | async-start | bytes 2359296 | tf_op jit(solution)/shard_map/all_to_all | solution.py:383
  9.8 6.0 %project.1 = (bf16[256,2048]{1,0:T(8,128)(2,1)}, bf16[256,2048]{1,0:T(8,128)(2,1)}, bf16[128,2048]{1,0:T(8,128)(2,1)}, bf16[128,2048]{1,0:T(8,128)(2,1)}, bf16[1...) custom-call(bf16[2048,512]{1,0:T(8,128)(2,1)} %hidden_ref.3, bf16[512,1024]{1,0:T(8,128)(2,1)} %matrix_ref.1), custom_call_target="tpu_custom_call" | custom-call | tf_op jit(solution)/shard_map/project/pallas_call | solution.py:138
  15.7 4.8 %collective-permute-start = (bf16[256,2048]{1,0:T(8,128)(2,1)}, bf16[256,2048]{1,0:T(8,128)(2,1)S(1)}, u32[]{:S(2)}, u32[]{:S(2)}) collective-permute-start(bf16[256,2048]{1,0:T(8,128)(2,1)} %get-tuple-element.30), channel_id=1, source_target_pairs={{0,1},{1,0},{2,3},{3,2},{4,5},{5,4},{6,7},{7,6},{8,9},{9,8},{10,11... | collective-permute-start | bytes 3145736 | tf_op jit(solution)/shard_map/ppermute | solution.py:222
  20.6 1.9 %collective-permute-start.1 = (bf16[256,2048]{1,0:T(8,128)(2,1)}, bf16[256,2048]{1,0:T(8,128)(2,1)}, u32[]{:S(2)}, u32[]{:S(2)}) collective-permute-start(bf16[256,2048]{1,0:T(8,128)(2,1)} %get-tuple-element.32), channel_id=1, source_target_pairs={{0,1},{1,0},{2,3},{3,2},{4,5},{5,4},{6,7},{7,6},{8,9},{9,8},{10,11... | collective-permute-start | bytes 3145736 | tf_op jit(solution)/shard_map/ppermute | solution.py:222
  24.1 8.8 %collective-permute-start.2 = (bf16[64,2048]{1,0:T(8,128)(2,1)S(1)}, bf16[64,2048]{1,0:T(8,128)(2,1)S(1)}, u32[]{:S(2)}, u32[]{:S(2)}) collective-permute-start(bf16[64,2048]{1,0:T(8,128)(2,1)S(1)} %add_far.1), channel_id=1, source_target_pairs={{0,2},{1,15},{2,4},{3,1},{4,6},{5,3},{6,8},{7,5},{8,10},{9,7},{10,... | collective-permute-start | bytes 786440 | tf_op jit(solution)/shard_map/ppermute | solution.py:217
  33.1 7.5 %psum.7 = s32[16]{0:T(128)S(1)} all-reduce(s32[16]{0:T(128)S(1)} %eq.28), channel_id=1, replica_groups=mesh['x'=4,'y'=8,'z'=8,'core'=2] {'x'}, use_global_device_ids=true, to_apply=%region_0.1 | all-reduce | flops 16 | bytes 128 | tf_op jit(solution)/shard_map/psum | solution.py:411
  41.9 2.0 %collective-permute-start.3 = (bf16[128,2048]{1,0:T(8,128)(2,1)}, bf16[128,2048]{1,0:T(8,128)(2,1)}, u32[]{:S(2)}, u32[]{:S(2)}) collective-permute-start(bf16[128,2048]{1,0:T(8,128)(2,1)} %add_own.1), channel_id=1, source_target_pairs={{0,2},{1,15},{2,4},{3,1},{4,6},{5,3},{6,8},{7,5},{8,10},{9,7},{10,... | collective-permute-start | bytes 1572872 | tf_op jit(solution)/shard_map/ppermute | solution.py:217
  44.0 1.8 %pick_factors.1 = bf16[4,288,512]{2,1,0:T(8,128)(2,1)} custom-call(s32[16]{0:T(128)S(1)} %subtract_clamp_fusion.index_ref, bf16[8,144,512]{2,1,0:T(8,128)(2,1)S(1)} %all-to-all-done.row_ref), custom_call_target="tpu_custom_call" | custom-call | bytes 2359296 | tf_op jit(solution)/shard_map/pick_factors/pallas_call | solution.py:257
  45.8 4.3 %all-to-all-start.1 = ((bf16[4,288,512]{2,1,0:T(8,128)(2,1)}), bf16[4,288,512]{2,1,0:T(8,128)(2,1)}, u32[]{:S(2)}, u32[]{:S(2)}) async-start(bf16[4,288,512]{2,1,0:T(8,128)(2,1)} %pick_factors.1), calls=%async_computation.1 | async-start | bytes 2359296 | tf_op jit(solution)/shard_map/all_to_all | solution.py:420
  50.1 2.3 %collective-permute-done.3.came_ref = bf16[128,2048]{1,0:T(8,128)(2,1)} collective-permute-done((bf16[128,2048]{1,0:T(8,128)(2,1)}, bf16[128,2048]{1,0:T(8,128)(2,1)}, u32[]{:S(2)}, u32[]{:S(2)}) %collective-permute-start.3) | collective-permute-done | bytes 524320 | tf_op jit(solution)/shard_map/ppermute | solution.py:217
  53.5 2.4 %add_parts.2 = bf16[128,2048]{1,0:T(8,128)(2,1)} custom-call(bf16[128,2048]{1,0:T(8,128)(2,1)S(1)} %copy-done.1, bf16[256,2048]{1,0:T(8,128)(2,1)} %collective-permute-done.1.other_ref, bf16[128,2048]{1,0:T(8,128)(2,1)} %collective-permute-done.3.came_ref), custom_call_target="tpu_custom_call" | custom-call | flops 262144 | bytes 1572864 | tf_op jit(solution)/shard_map/add_parts/pallas_call | solution.py:161
  55.8 6.2 %collective-permute-start.4 = (bf16[128,2048]{1,0:T(8,128)(2,1)}, bf16[128,2048]{1,0:T(8,128)(2,1)}, u32[]{:S(2)}, u32[]{:S(2)}) collective-permute-start(bf16[128,2048]{1,0:T(8,128)(2,1)} %add_parts.2), channel_id=1, source_target_pairs={{0,2},{1,15},{2,4},{3,1},{4,6},{5,3},{6,8},{7,5},{8,10},{9,7},{10,... | collective-permute-start | bytes 1572872 | tf_op jit(solution)/shard_map/ppermute | solution.py:217
  62.1 3.6 %all-to-all-done.1.factor_ref = bf16[4,288,512]{2,1,0:T(8,128)(2,1)} async-done(((bf16[4,288,512]{2,1,0:T(8,128)(2,1)}), bf16[4,288,512]{2,1,0:T(8,128)(2,1)}, u32[]{:S(2)}, u32[]{:S(2)}) %all-to-all-start.1) | async-done | bytes 1179680 | tf_op jit(solution)/shard_map/all_to_all | solution.py:420
  65.7 2.8 %down_projection.1 = (bf16[16,64,128]{2,1,0:T(8,128)(2,1)}, bf16[4,16,512]{2,1,0:T(8,128)(2,1)S(1)}) custom-call(s32[4]{0:T(128)S(1)} %and_select_fusion.own_row_ref, bf16[2048,512]{1,0:T(8,128)(2,1)S(1)} %copy-done, bf16[4,288,512]{2,1,0:T(8,128)(2,1)} %all-to-all-done.1.factor_ref), custom_call_target="tpu_custom_call" | custom-call | flops 134217728 | bytes 2359296 | tf_op jit(solution)/shard_map/down_projection/pallas_call | solution.py:293
  68.4 10.0 %all-to-all-start.2 = ((bf16[16,64,128]{2,1,0:T(8,128)(2,1)}), bf16[16,64,128]{2,1,0:T(8,128)(2,1)S(1)}, u32[]{:S(2)}, u32[]{:S(2)}) async-start(bf16[16,64,128]{2,1,0:T(8,128)(2,1)} %get-tuple-element.41), calls=%async_computation.2 | async-start | bytes 524288 | tf_op jit(solution)/shard_map/all_to_all | solution.py:422
  79.5 1.5 %add_parts.3 = bf16[128,2048]{1,0:T(8,128)(2,1)S(1)} custom-call(bf16[128,2048]{1,0:T(8,128)(2,1)S(1)} %copy-done.6, bf16[256,2048]{1,0:T(8,128)(2,1)} %collective-permute-done.1.other_ref, bf16[128,2048]{1,0:T(8,128)(2,1)} %collective-permute-done.4.came_ref), custom_call_target="tpu_custom_call" | custom-call | flops 13107200000 | bytes 1572864 | tf_op jit(solution)/shard_map/add_parts/pallas_call | solution.py:161
  81.0 4.6 %collective-permute-start.5 = (bf16[128,2048]{1,0:T(8,128)(2,1)S(1)}, bf16[128,2048]{1,0:T(8,128)(2,1)S(1)}, u32[]{:S(2)}, u32[]{:S(2)}) collective-permute-start(bf16[128,2048]{1,0:T(8,128)(2,1)S(1)} %add_parts.3), channel_id=1, source_target_pairs={{0,2},{1,15},{2,4},{3,1},{4,6},{5,3},{6,8},{7,5},{8,10},{9,7},{10,... | collective-permute-start | bytes 1572872 | tf_op jit(solution)/shard_map/ppermute | solution.py:217
  85.7 4.5 %all-to-all-done.2.parts_ref = bf16[16,64,128]{2,1,0:T(8,128)(2,1)S(1)} async-done(((bf16[16,64,128]{2,1,0:T(8,128)(2,1)}), bf16[16,64,128]{2,1,0:T(8,128)(2,1)S(1)}, u32[]{:S(2)}, u32[]{:S(2)}) %all-to-all-start.2) | async-done | bytes 262176 | tf_op jit(solution)/shard_map/all_to_all | solution.py:422
  90.9 3.6 %all-to-all-start.3 = ((bf16[16,64,128]{2,1,0:T(8,128)(2,1)}), bf16[16,64,128]{2,1,0:T(8,128)(2,1)S(1)}, u32[]{:S(2)}, u32[]{:S(2)}) async-start(bf16[16,64,128]{2,1,0:T(8,128)(2,1)} %sum_parts.1), calls=%async_computation.3 | async-start | bytes 524288 | tf_op jit(solution)/shard_map/all_to_all | solution.py:424
  94.6 1.9 %collective-permute-start.6 = (bf16[64,2048]{1,0:T(8,128)(2,1)S(1)}, bf16[64,2048]{1,0:T(8,128)(2,1)S(1)}, u32[]{:S(2)}, u32[]{:S(2)}) collective-permute-start(bf16[64,2048]{1,0:T(8,128)(2,1)S(1)} %get-tuple-element.37), channel_id=1, source_target_pairs={{0,1},{1,0},{2,3},{3,2},{4,5},{5,4},{6,7},{7,6},{8,9},{9,8},{10,11... | collective-permute-start | bytes 786440 | tf_op jit(solution)/shard_map/ppermute | solution.py:222
  96.5 1.5 %collective-permute-done.6.refs_1_ = bf16[64,2048]{1,0:T(8,128)(2,1)S(1)} collective-permute-done((bf16[64,2048]{1,0:T(8,128)(2,1)S(1)}, bf16[64,2048]{1,0:T(8,128)(2,1)S(1)}, u32[]{:S(2)}, u32[]{:S(2)}) %collective-permute-start.6) | collective-permute-done | bytes 262176 | tf_op jit(solution)/shard_map/ppermute | solution.py:222
  98.0 7.6 %all-to-all-done.3.refs_2_ = bf16[16,64,128]{2,1,0:T(8,128)(2,1)S(1)} async-done(((bf16[16,64,128]{2,1,0:T(8,128)(2,1)}), bf16[16,64,128]{2,1,0:T(8,128)(2,1)S(1)}, u32[]{:S(2)}, u32[]{:S(2)}) %all-to-all-start.3) | async-done | bytes 262176 | tf_op jit(solution)/shard_map/all_to_all | solution.py:424
  105.6 1.6 %add_update.1 = bf16[64,2048]{1,0:T(8,128)(2,1)} custom-call(s32[4]{0:T(128)S(1)} %copy-done.5, bf16[64,2048]{1,0:T(8,128)(2,1)S(1)} %get-tuple-element.36.refs_0_, bf16[64,2048]{1,0:T(8,128)(2,1)S(1)} %collective-permute-done.6.refs_1_, bf16[16,64,128]{2,1,0:T(8,128)(2,1)S(1)} %all-to-all-done.3.refs_2_, bf16[4,16,512]{2,1,0:T(8,128)(2,1)S(1)} %get-tuple-element.42.refs_3_), custom_call_target="tpu_custom_call" | custom-call | flops 16777216 | bytes 1310720 | tf_op jit(solution)/shard_map/add_update/pallas_call | solution.py:360
  (34 shorter events, 6.1 us)
Async XLA Ops:
  2.1 42.0 %all-to-all-start = ((bf16[8,144,512]{2,1,0:T(8,128)(2,1)}), bf16[8,144,512]{2,1,0:T(8,128)(2,1)S(1)}, u32[]{:S(2)}, u32[]{:S(2)}) async-start(bf16[8,144,512]{2,1,0:T(8,128)(2,1)} %factor_copies.1), calls=%async_computation | async-start | bytes 2359296 | tf_op jit(solution)/shard_map/all_to_all | solution.py:383
  9.8 23.2 %copy-start.7 = (s32[4]{0:T(128)S(1)}, s32[4]{0:T(128)}, u32[]{:S(2)}) copy-start(s32[4]{0:T(128)} %param.12) | copy-start | bytes 52
  9.8 30.8 %copy-start.8 = (s32[64]{0:T(128)S(1)}, s32[64]{0:T(128)}, u32[]{:S(2)}) copy-start(s32[64]{0:T(128)} %param.11) | copy-start | bytes 772
  15.7 25.0 %copy-start.2 = (bf16[128,2048]{1,0:T(8,128)(2,1)S(1)}, bf16[128,2048]{1,0:T(8,128)(2,1)}, u32[]{:S(2)}) copy-start(bf16[128,2048]{1,0:T(8,128)(2,1)} %get-tuple-element.34.part_ref) | copy-start | bytes 1572868
  15.7 7.3 %collective-permute-start = (bf16[256,2048]{1,0:T(8,128)(2,1)}, bf16[256,2048]{1,0:T(8,128)(2,1)S(1)}, u32[]{:S(2)}, u32[]{:S(2)}) collective-permute-start(bf16[256,2048]{1,0:T(8,128)(2,1)} %get-tuple-element.30), channel_id=1, source_target_pairs={{0,1},{1,0},{2,3},{3,2},{4,5},{5,4},{6,7},{7,6},{8,9},{9,8},{10,11... | collective-permute-start | bytes 3145736 | tf_op jit(solution)/shard_map/ppermute | solution.py:222
  20.6 29.5 %collective-permute-start.1 = (bf16[256,2048]{1,0:T(8,128)(2,1)}, bf16[256,2048]{1,0:T(8,128)(2,1)}, u32[]{:S(2)}, u32[]{:S(2)}) collective-permute-start(bf16[256,2048]{1,0:T(8,128)(2,1)} %get-tuple-element.32), channel_id=1, source_target_pairs={{0,1},{1,0},{2,3},{3,2},{4,5},{5,4},{6,7},{7,6},{8,9},{9,8},{10,11... | collective-permute-start | bytes 3145736 | tf_op jit(solution)/shard_map/ppermute | solution.py:222
  23.1 0.9 copy-start.4
  24.1 16.6 %collective-permute-start.2 = (bf16[64,2048]{1,0:T(8,128)(2,1)S(1)}, bf16[64,2048]{1,0:T(8,128)(2,1)S(1)}, u32[]{:S(2)}, u32[]{:S(2)}) collective-permute-start(bf16[64,2048]{1,0:T(8,128)(2,1)S(1)} %add_far.1), channel_id=1, source_target_pairs={{0,2},{1,15},{2,4},{3,1},{4,6},{5,3},{6,8},{7,5},{8,10},{9,7},{10,... | collective-permute-start | bytes 786440 | tf_op jit(solution)/shard_map/ppermute | solution.py:217
  41.9 10.5 %collective-permute-start.3 = (bf16[128,2048]{1,0:T(8,128)(2,1)}, bf16[128,2048]{1,0:T(8,128)(2,1)}, u32[]{:S(2)}, u32[]{:S(2)}) collective-permute-start(bf16[128,2048]{1,0:T(8,128)(2,1)} %add_own.1), channel_id=1, source_target_pairs={{0,2},{1,15},{2,4},{3,1},{4,6},{5,3},{6,8},{7,5},{8,10},{9,7},{10,... | collective-permute-start | bytes 1572872 | tf_op jit(solution)/shard_map/ppermute | solution.py:217
  45.8 19.9 %all-to-all-start.1 = ((bf16[4,288,512]{2,1,0:T(8,128)(2,1)}), bf16[4,288,512]{2,1,0:T(8,128)(2,1)}, u32[]{:S(2)}, u32[]{:S(2)}) async-start(bf16[4,288,512]{2,1,0:T(8,128)(2,1)} %pick_factors.1), calls=%async_computation.1 | async-start | bytes 2359296 | tf_op jit(solution)/shard_map/all_to_all | solution.py:420
  50.1 15.6 %copy-start = (bf16[2048,512]{1,0:T(8,128)(2,1)S(1)}, bf16[2048,512]{1,0:T(8,128)(2,1)}, u32[]{:S(2)}) copy-start(bf16[2048,512]{1,0:T(8,128)(2,1)} %hidden_ref.3) | copy-start | bytes 6291460
  52.4 1.0 copy-start.1
  55.8 22.6 %collective-permute-start.4 = (bf16[128,2048]{1,0:T(8,128)(2,1)}, bf16[128,2048]{1,0:T(8,128)(2,1)}, u32[]{:S(2)}, u32[]{:S(2)}) collective-permute-start(bf16[128,2048]{1,0:T(8,128)(2,1)} %add_parts.2), channel_id=1, source_target_pairs={{0,2},{1,15},{2,4},{3,1},{4,6},{5,3},{6,8},{7,5},{8,10},{9,7},{10,... | collective-permute-start | bytes 1572872 | tf_op jit(solution)/shard_map/ppermute | solution.py:217
  68.4 21.7 %all-to-all-start.2 = ((bf16[16,64,128]{2,1,0:T(8,128)(2,1)}), bf16[16,64,128]{2,1,0:T(8,128)(2,1)S(1)}, u32[]{:S(2)}, u32[]{:S(2)}) async-start(bf16[16,64,128]{2,1,0:T(8,128)(2,1)} %get-tuple-element.41), calls=%async_computation.2 | async-start | bytes 524288 | tf_op jit(solution)/shard_map/all_to_all | solution.py:422
  78.4 1.0 copy-start.6
  81.0 13.5 %copy-start.3 = (bf16[64,2048]{1,0:T(8,128)(2,1)S(1)}, bf16[64,2048]{1,0:T(8,128)(2,1)}, u32[]{:S(2)}) copy-start(bf16[64,2048]{1,0:T(8,128)(2,1)} %get-tuple-element.29.own_ref) | copy-start | bytes 786436
  81.0 13.4 %collective-permute-start.5 = (bf16[128,2048]{1,0:T(8,128)(2,1)S(1)}, bf16[128,2048]{1,0:T(8,128)(2,1)S(1)}, u32[]{:S(2)}, u32[]{:S(2)}) collective-permute-start(bf16[128,2048]{1,0:T(8,128)(2,1)S(1)} %add_parts.3), channel_id=1, source_target_pairs={{0,2},{1,15},{2,4},{3,1},{4,6},{5,3},{6,8},{7,5},{8,10},{9,7},{10,... | collective-permute-start | bytes 1572872 | tf_op jit(solution)/shard_map/ppermute | solution.py:217
  90.9 14.7 %copy-start.5 = (s32[4]{0:T(128)S(1)}, s32[4]{0:T(128)}, u32[]{:S(2)}) copy-start(s32[4]{0:T(128)} %lengths_ref.1) | copy-start | bytes 52
  90.9 14.7 %all-to-all-start.3 = ((bf16[16,64,128]{2,1,0:T(8,128)(2,1)}), bf16[16,64,128]{2,1,0:T(8,128)(2,1)S(1)}, u32[]{:S(2)}, u32[]{:S(2)}) async-start(bf16[16,64,128]{2,1,0:T(8,128)(2,1)} %sum_parts.1), calls=%async_computation.3 | async-start | bytes 524288 | tf_op jit(solution)/shard_map/all_to_all | solution.py:424
  94.6 3.4 %collective-permute-start.6 = (bf16[64,2048]{1,0:T(8,128)(2,1)S(1)}, bf16[64,2048]{1,0:T(8,128)(2,1)S(1)}, u32[]{:S(2)}, u32[]{:S(2)}) collective-permute-start(bf16[64,2048]{1,0:T(8,128)(2,1)S(1)} %get-tuple-element.37), channel_id=1, source_target_pairs={{0,1},{1,0},{2,3},{3,2},{4,5},{5,4},{6,7},{7,6},{8,9},{9,8},{10,11... | collective-permute-start | bytes 786440 | tf_op jit(solution)/shard_map/ppermute | solution.py:222

commit v6 on v5

--- a/solution.py
+++ b/solution.py
@@ -13,7 +13,7 @@
 DP, TENSOR = ("x", "y"), ("z", "core")
 LANES = 128
 WEIGHTS = (1, 1, 1, 50000, 1)
-KERNEL_VMEM = 8 << 20
+KERNEL_VMEM, COPIES_VMEM = 8 << 20, 60 << 20
 PROJECT_VMEM, PROJECT_PARTS = 60 << 20, 2
 
 
@@ -164,7 +164,7 @@
         in_specs=[spec] * len(operands),
         out_specs=[spec] * len(out_shape) if several else spec,
         cost_estimate=cost(weight * size, 3 * size),
-        compiler_params=pltpu.CompilerParams(vmem_limit_bytes=KERNEL_VMEM),
+        compiler_params=pltpu.CompilerParams(vmem_limit_bytes=COPIES_VMEM if name == "add_parts" else KERNEL_VMEM),
         name=name,
     )(*operands)
 
@@ -185,8 +185,10 @@
     out_ref[...] = sum_refs(part_ref[...], other, came_ref[...])
 
 
-def add_far_kernel(first, part_ref, other_ref, out_ref):
-    out_ref[...] = sum_refs(part_ref[...], other_ref[first : first + part_ref.shape[0]])
+def add_far_kernel(first, far_ref, own_ref, other_ref, far_out_ref, own_out_ref):
+    columns = own_ref.shape[0]
+    own_out_ref[...] = sum_refs(own_ref[...], other_ref[first : first + columns])
+    far_out_ref[...] = sum_refs(far_ref[...], other_ref[first + columns : first + 2 * columns])
 
 
 def add_own_kernel(first, part_ref, other_ref, came_ref, out_ref):
@@ -197,13 +199,12 @@
     out_ref[mine] = sum_refs(out_ref[mine], came_ref[...])
 
 
-def split_kernel(first, own_ref, other_ref, chain_ref, kept_ref, sent_ref):
+def split_kernel(own_ref, chain_ref, kept_ref, sent_ref):
     columns = own_ref.shape[0]
     core = lax.axis_index("core")
     mine = pl.ds(pl.multiple_of(core * columns, columns), columns)
     theirs = pl.ds(pl.multiple_of((1 - core) * columns, columns), columns)
-    other = other_ref[first : first + columns]
-    kept_ref[...] = sum_refs(own_ref[...], other, chain_ref[mine])
+    kept_ref[...] = sum_refs(own_ref[...], chain_ref[mine])
     sent_ref[...] = chain_ref[theirs]
 
 
@@ -391,18 +392,20 @@
     def add(kernel, first, weight, name, part, *others):
         return vmem_call(functools.partial(kernel, first), name, weight, like(part), part, *others)
 
-    chain = add(add_far_kernel, span + columns, WEIGHTS[0], "add_far", far, near)
+    chain, own = vmem_call(
+        functools.partial(add_far_kernel, span),
+        "add_far",
+        WEIGHTS[0],
+        [like(far), like(own)],
+        far,
+        own,
+        near,
+    )
     chain = add(add_own_kernel, 0, WEIGHTS[1], "add_own", parts[0], near, hop(chain))
     chain = add(add_kernel, 0, WEIGHTS[2], "add_parts", parts[1], middle, hop(chain))
     chain = add(add_kernel, span, WEIGHTS[3], "add_parts", parts[2], middle, hop(chain))
     kept, sent = vmem_call(
-        functools.partial(split_kernel, span),
-        "split",
-        WEIGHTS[4],
-        [like(own), like(own)],
-        own,
-        near,
-        hop(chain),
+        split_kernel, "split", WEIGHTS[4], [like(own), like(own)], own, hop(chain)
     )
     base = (kept, along("core", sent, 1))
 

time: 108 us -> 107 us (level)
  starting transfers between devices: 55.9 us -> 53.6 us
  waiting for transfers between devices: 20 us -> 21.8 us
    pallas_call x1, Pallas kernels: 2.76 us -> 1.32 us  [down_projection(): pl.pallas_call(down_kernel, out_shape=[jax.ShapeDtypeStruct((members, ran...]
    ppermute x4, starting transfers between devices: 21.7 us -> 20.5 us  [hop(): return lax.ppermute(value, TENSOR, pairs)]
    pallas_call x5, Pallas kernels: 5.24 us -> 6.36 us  [vmem_call(): pl.pallas_call(kernel, out_shape=out_shape, in_specs=[spec] * len(operand...]
    all_to_all x1, waiting for transfers between devices: 3.6 us -> 4.68 us  [on_device(): factors = lax.all_to_all(sent, 'x', 0, 0)]
    unnamed x18 -> x20, local copies, waits for them, and re-layouts: 3.06 us -> 3.24 us
where the time goes in v6:
time: 107 us
  starting transfers between devices  53.6 us (50%)
  waiting for transfers between devices  21.8 us (20%)
  Pallas kernels  19.8 us (19%)
  blocking collectives  7.44 us (7%)
  local copies, waits for them, and re-layouts  3.33 us (3%)
    ppermute x4, starting transfers between devices, hop(): return lax.ppermute(value, TENSOR, pairs)  20.5 us
    all_to_all x2, starting transfers between devices, on_device(): down = lax.all_to_all(down, TENSOR, 0, 0)  13.2 us
    all_to_all x2, waiting for transfers between devices, on_device(): down = lax.all_to_all(down, TENSOR, 0, 0)  12.2 us
    ppermute x3, starting transfers between devices, along(): return lax.ppermute(value, axis, [(i, (i + step) % n) for i in range(n)])  8.76 us
    all_to_all x1, starting transfers between devices, on_device(): row = lax.all_to_all(copies, 'y', 0, 0)  7.66 us
    psum x1, blocking collectives, on_device(): lax.psum(jnp.where(mine, rollout_adapter[None, :], 0), 'x').reshape(-1)  7.44 us
    pallas_call x5, Pallas kernels, vmem_call(): pl.pallas_call(kernel, out_shape=out_shape, in_specs=[spec] * len(operand...  6.36 us
    pallas_call x1, Pallas kernels, project(): pl.pallas_call(project_kernel, out_shape=[jax.ShapeDtypeStruct((height, t...  5.97 us
  transfers between devices with their start and end apart: 11, of which 6 were waited for; matrix products, arithmetic and copies ran while one was open for 0% of the time, Pallas kernels for 15%

profile of v6, /device:TPU:1, one launch (start us, length us, event | category | flops | bytes accessed | tf_op | source)
XLA Modules:
  0.0 106.6 jit_solution(12210515607022889139)
XLA Ops:
  0.0 2.1 %factor_copies.1 = bf16[8,144,512]{2,1,0:T(8,128)(2,1)} custom-call(bf16[2,64,512]{2,1,0:T(8,128)(2,1)} %bitcast.2, bf16[2,64,64]{2,1,0:T(8,128)(2,1)} %up_ref.1), custom_call_target="tpu_custom_call" | custom-call | bytes 1179648 | tf_op jit(solution)/shard_map/factor_copies/pallas_call | solution.py:52
  2.1 7.7 %all-to-all-start = ((bf16[8,144,512]{2,1,0:T(8,128)(2,1)}), bf16[8,144,512]{2,1,0:T(8,128)(2,1)S(1)}, u32[]{:S(2)}, u32[]{:S(2)}) async-start(bf16[8,144,512]{2,1,0:T(8,128)(2,1)} %factor_copies.1), calls=%async_computation | async-start | bytes 2359296 | tf_op jit(solution)/shard_map/all_to_all | solution.py:384
  9.8 6.0 %project.1 = (bf16[256,2048]{1,0:T(8,128)(2,1)}, bf16[256,2048]{1,0:T(8,128)(2,1)}, bf16[128,2048]{1,0:T(8,128)(2,1)}, bf16[128,2048]{1,0:T(8,128)(2,1)}, bf16[1...) custom-call(bf16[2048,512]{1,0:T(8,128)(2,1)} %hidden_ref.3, bf16[512,1024]{1,0:T(8,128)(2,1)} %matrix_ref.1), custom_call_target="tpu_custom_call" | custom-call | tf_op jit(solution)/shard_map/project/pallas_call | solution.py:138
  15.7 4.8 %collective-permute-start = (bf16[256,2048]{1,0:T(8,128)(2,1)}, bf16[256,2048]{1,0:T(8,128)(2,1)S(1)}, u32[]{:S(2)}, u32[]{:S(2)}) collective-permute-start(bf16[256,2048]{1,0:T(8,128)(2,1)} %get-tuple-element.33), channel_id=1, source_target_pairs={{0,1},{1,0},{2,3},{3,2},{4,5},{5,4},{6,7},{7,6},{8,9},{9,8},{10,11... | collective-permute-start | bytes 3145736 | tf_op jit(solution)/shard_map/ppermute | solution.py:223
  20.6 1.9 %collective-permute-start.1 = (bf16[256,2048]{1,0:T(8,128)(2,1)}, bf16[256,2048]{1,0:T(8,128)(2,1)}, u32[]{:S(2)}, u32[]{:S(2)}) collective-permute-start(bf16[256,2048]{1,0:T(8,128)(2,1)} %get-tuple-element.36), channel_id=1, source_target_pairs={{0,1},{1,0},{2,3},{3,2},{4,5},{5,4},{6,7},{7,6},{8,9},{9,8},{10,11... | collective-permute-start | bytes 3145736 | tf_op jit(solution)/shard_map/ppermute | solution.py:223
  25.1 8.8 %collective-permute-start.2 = (bf16[64,2048]{1,0:T(8,128)(2,1)S(1)}, bf16[64,2048]{1,0:T(8,128)(2,1)S(1)}, u32[]{:S(2)}, u32[]{:S(2)}) collective-permute-start(bf16[64,2048]{1,0:T(8,128)(2,1)S(1)} %get-tuple-element.39), channel_id=1, source_target_pairs={{0,2},{1,15},{2,4},{3,1},{4,6},{5,3},{6,8},{7,5},{8,10},{9,7},{10,... | collective-permute-start | bytes 786440 | tf_op jit(solution)/shard_map/ppermute | solution.py:218
  34.1 7.4 %psum.7 = s32[16]{0:T(128)S(1)} all-reduce(s32[16]{0:T(128)S(1)} %eq.28), channel_id=1, replica_groups=mesh['x'=4,'y'=8,'z'=8,'core'=2] {'x'}, use_global_device_ids=true, to_apply=%region_0.1 | all-reduce | flops 16 | bytes 128 | tf_op jit(solution)/shard_map/psum | solution.py:414
  42.9 2.0 %collective-permute-start.3 = (bf16[128,2048]{1,0:T(8,128)(2,1)}, bf16[128,2048]{1,0:T(8,128)(2,1)}, u32[]{:S(2)}, u32[]{:S(2)}) collective-permute-start(bf16[128,2048]{1,0:T(8,128)(2,1)} %add_own.1), channel_id=1, source_target_pairs={{0,2},{1,15},{2,4},{3,1},{4,6},{5,3},{6,8},{7,5},{8,10},{9,7},{10,... | collective-permute-start | bytes 1572872 | tf_op jit(solution)/shard_map/ppermute | solution.py:218
  45.1 1.8 %pick_factors.1 = bf16[4,288,512]{2,1,0:T(8,128)(2,1)} custom-call(s32[16]{0:T(128)S(1)} %subtract_clamp_fusion.index_ref, bf16[8,144,512]{2,1,0:T(8,128)(2,1)S(1)} %all-to-all-done.row_ref), custom_call_target="tpu_custom_call" | custom-call | bytes 2359296 | tf_op jit(solution)/shard_map/pick_factors/pallas_call | solution.py:258
  46.9 3.5 %all-to-all-start.1 = ((bf16[4,288,512]{2,1,0:T(8,128)(2,1)}), bf16[4,288,512]{2,1,0:T(8,128)(2,1)S(1)}, u32[]{:S(2)}, u32[]{:S(2)}) async-start(bf16[4,288,512]{2,1,0:T(8,128)(2,1)} %pick_factors.1), calls=%async_computation.1 | async-start | bytes 2359296 | tf_op jit(solution)/shard_map/all_to_all | solution.py:423
  50.4 3.0 %collective-permute-done.3.came_ref = bf16[128,2048]{1,0:T(8,128)(2,1)} collective-permute-done((bf16[128,2048]{1,0:T(8,128)(2,1)}, bf16[128,2048]{1,0:T(8,128)(2,1)}, u32[]{:S(2)}, u32[]{:S(2)}) %collective-permute-start.3) | collective-permute-done | bytes 524320 | tf_op jit(solution)/shard_map/ppermute | solution.py:218
  53.4 2.5 %add_parts.2 = bf16[128,2048]{1,0:T(8,128)(2,1)} custom-call(bf16[128,2048]{1,0:T(8,128)(2,1)} %get-tuple-element.37.part_ref, bf16[256,2048]{1,0:T(8,128)(2,1)} %collective-permute-done.1.other_ref, bf16[128,2048]{1,0:T(8,128)(2,1)} %collective-permute-done.3.came_ref), custom_call_target="tpu_custom_call" | custom-call | flops 262144 | bytes 1572864 | tf_op jit(solution)/shard_map/add_parts/pallas_call | solution.py:161
  55.9 5.0 %collective-permute-start.4 = (bf16[128,2048]{1,0:T(8,128)(2,1)}, bf16[128,2048]{1,0:T(8,128)(2,1)}, u32[]{:S(2)}, u32[]{:S(2)}) collective-permute-start(bf16[128,2048]{1,0:T(8,128)(2,1)} %add_parts.2), channel_id=1, source_target_pairs={{0,2},{1,15},{2,4},{3,1},{4,6},{5,3},{6,8},{7,5},{8,10},{9,7},{10,... | collective-permute-start | bytes 1572872 | tf_op jit(solution)/shard_map/ppermute | solution.py:218
  60.9 4.7 %all-to-all-done.1.factor_ref = bf16[4,288,512]{2,1,0:T(8,128)(2,1)S(1)} async-done(((bf16[4,288,512]{2,1,0:T(8,128)(2,1)}), bf16[4,288,512]{2,1,0:T(8,128)(2,1)S(1)}, u32[]{:S(2)}, u32[]{:S(2)}) %all-to-all-start.1) | async-done | bytes 1179680 | tf_op jit(solution)/shard_map/all_to_all | solution.py:423
  65.6 1.3 %down_projection.1 = (bf16[16,64,128]{2,1,0:T(8,128)(2,1)S(1)}, bf16[4,16,512]{2,1,0:T(8,128)(2,1)S(1)}) custom-call(s32[4]{0:T(128)S(1)} %and_select_fusion.own_row_ref, bf16[2048,512]{1,0:T(8,128)(2,1)S(1)} %copy-done, bf16[4,288,512]{2,1,0:T(8,128)(2,1)S(1)} %all-to-all-done.1.factor_ref), custom_call_target="tpu_custom_call" | custom-call | flops 134217728 | bytes 2359296 | tf_op jit(solution)/shard_map/down_projection/pallas_call | solution.py:294
  68.2 9.8 %all-to-all-start.2 = ((bf16[16,64,128]{2,1,0:T(8,128)(2,1)}), bf16[16,64,128]{2,1,0:T(8,128)(2,1)S(1)}, u32[]{:S(2)}, u32[]{:S(2)}) async-start(bf16[16,64,128]{2,1,0:T(8,128)(2,1)} %copy-done.2), calls=%async_computation.2 | async-start | bytes 524288 | tf_op jit(solution)/shard_map/all_to_all | solution.py:425
  78.0 2.5 %add_parts.3 = bf16[128,2048]{1,0:T(8,128)(2,1)} custom-call(bf16[128,2048]{1,0:T(8,128)(2,1)} %get-tuple-element.35.part_ref, bf16[256,2048]{1,0:T(8,128)(2,1)} %collective-permute-done.1.other_ref, bf16[128,2048]{1,0:T(8,128)(2,1)} %collective-permute-done.4.came_ref), custom_call_target="tpu_custom_call" | custom-call | flops 13107200000 | bytes 1572864 | tf_op jit(solution)/shard_map/add_parts/pallas_call | solution.py:161
  80.5 4.6 %collective-permute-start.5 = (bf16[128,2048]{1,0:T(8,128)(2,1)}, bf16[128,2048]{1,0:T(8,128)(2,1)S(1)}, u32[]{:S(2)}, u32[]{:S(2)}) collective-permute-start(bf16[128,2048]{1,0:T(8,128)(2,1)} %add_parts.3), channel_id=1, source_target_pairs={{0,2},{1,15},{2,4},{3,1},{4,6},{5,3},{6,8},{7,5},{8,10},{9,7},{10,... | collective-permute-start | bytes 1572872 | tf_op jit(solution)/shard_map/ppermute | solution.py:218
  85.2 4.6 %all-to-all-done.2.parts_ref = bf16[16,64,128]{2,1,0:T(8,128)(2,1)S(1)} async-done(((bf16[16,64,128]{2,1,0:T(8,128)(2,1)}), bf16[16,64,128]{2,1,0:T(8,128)(2,1)S(1)}, u32[]{:S(2)}, u32[]{:S(2)}) %all-to-all-start.2) | async-done | bytes 262176 | tf_op jit(solution)/shard_map/all_to_all | solution.py:425
  90.5 3.4 %all-to-all-start.3 = ((bf16[16,64,128]{2,1,0:T(8,128)(2,1)}), bf16[16,64,128]{2,1,0:T(8,128)(2,1)S(1)}, u32[]{:S(2)}, u32[]{:S(2)}) async-start(bf16[16,64,128]{2,1,0:T(8,128)(2,1)} %sum_parts.1), calls=%async_computation.3 | async-start | bytes 524288 | tf_op jit(solution)/shard_map/all_to_all | solution.py:427
  94.0 2.0 %collective-permute-start.6 = (bf16[64,2048]{1,0:T(8,128)(2,1)S(1)}, bf16[64,2048]{1,0:T(8,128)(2,1)S(1)}, u32[]{:S(2)}, u32[]{:S(2)}) collective-permute-start(bf16[64,2048]{1,0:T(8,128)(2,1)S(1)} %get-tuple-element.41), channel_id=1, source_target_pairs={{0,1},{1,0},{2,3},{3,2},{4,5},{5,4},{6,7},{7,6},{8,9},{9,8},{10,11... | collective-permute-start | bytes 786440 | tf_op jit(solution)/shard_map/ppermute | solution.py:223
  96.0 1.4 %collective-permute-done.6.refs_1_ = bf16[64,2048]{1,0:T(8,128)(2,1)S(1)} collective-permute-done((bf16[64,2048]{1,0:T(8,128)(2,1)S(1)}, bf16[64,2048]{1,0:T(8,128)(2,1)S(1)}, u32[]{:S(2)}, u32[]{:S(2)}) %collective-permute-start.6) | collective-permute-done | bytes 262176 | tf_op jit(solution)/shard_map/ppermute | solution.py:223
  97.5 7.6 %all-to-all-done.3.refs_2_ = bf16[16,64,128]{2,1,0:T(8,128)(2,1)S(1)} async-done(((bf16[16,64,128]{2,1,0:T(8,128)(2,1)}), bf16[16,64,128]{2,1,0:T(8,128)(2,1)S(1)}, u32[]{:S(2)}, u32[]{:S(2)}) %all-to-all-start.3) | async-done | bytes 262176 | tf_op jit(solution)/shard_map/all_to_all | solution.py:427
  105.1 1.6 %add_update.1 = bf16[64,2048]{1,0:T(8,128)(2,1)} custom-call(s32[4]{0:T(128)S(1)} %copy-done.7, bf16[64,2048]{1,0:T(8,128)(2,1)S(1)} %get-tuple-element.40.refs_0_, bf16[64,2048]{1,0:T(8,128)(2,1)S(1)} %collective-permute-done.6.refs_1_, bf16[16,64,128]{2,1,0:T(8,128)(2,1)S(1)} %all-to-all-done.3.refs_2_, bf16[4,16,512]{2,1,0:T(8,128)(2,1)S(1)} %copy-done.6), custom_call_target="tpu_custom_call" | custom-call | flops 16777216 | bytes 1310720 | tf_op jit(solution)/shard_map/add_update/pallas_call | solution.py:361
  (36 shorter events, 6.3 us)
Async XLA Ops:
  2.1 43.0 %all-to-all-start = ((bf16[8,144,512]{2,1,0:T(8,128)(2,1)}), bf16[8,144,512]{2,1,0:T(8,128)(2,1)S(1)}, u32[]{:S(2)}, u32[]{:S(2)}) async-start(bf16[8,144,512]{2,1,0:T(8,128)(2,1)} %factor_copies.1), calls=%async_computation | async-start | bytes 2359296 | tf_op jit(solution)/shard_map/all_to_all | solution.py:384
  9.7 24.2 %copy-start.8 = (s32[4]{0:T(128)S(1)}, s32[4]{0:T(128)}, u32[]{:S(2)}) copy-start(s32[4]{0:T(128)} %param.12) | copy-start | bytes 52
  9.7 31.8 %copy-start.9 = (s32[64]{0:T(128)S(1)}, s32[64]{0:T(128)}, u32[]{:S(2)}) copy-start(s32[64]{0:T(128)} %param.11) | copy-start | bytes 772
  15.7 26.0 %copy-start.1 = (bf16[128,2048]{1,0:T(8,128)(2,1)S(1)}, bf16[128,2048]{1,0:T(8,128)(2,1)}, u32[]{:S(2)}) copy-start(bf16[128,2048]{1,0:T(8,128)(2,1)} %get-tuple-element.38.part_ref) | copy-start | bytes 1572868
  15.7 7.3 %collective-permute-start = (bf16[256,2048]{1,0:T(8,128)(2,1)}, bf16[256,2048]{1,0:T(8,128)(2,1)S(1)}, u32[]{:S(2)}, u32[]{:S(2)}) collective-permute-start(bf16[256,2048]{1,0:T(8,128)(2,1)} %get-tuple-element.33), channel_id=1, source_target_pairs={{0,1},{1,0},{2,3},{3,2},{4,5},{5,4},{6,7},{7,6},{8,9},{9,8},{10,11... | collective-permute-start | bytes 3145736 | tf_op jit(solution)/shard_map/ppermute | solution.py:223
  20.6 29.8 %collective-permute-start.1 = (bf16[256,2048]{1,0:T(8,128)(2,1)}, bf16[256,2048]{1,0:T(8,128)(2,1)}, u32[]{:S(2)}, u32[]{:S(2)}) collective-permute-start(bf16[256,2048]{1,0:T(8,128)(2,1)} %get-tuple-element.36), channel_id=1, source_target_pairs={{0,1},{1,0},{2,3},{3,2},{4,5},{5,4},{6,7},{7,6},{8,9},{9,8},{10,11... | collective-permute-start | bytes 3145736 | tf_op jit(solution)/shard_map/ppermute | solution.py:223
  23.1 0.9 copy-start.3
  24.0 0.9 copy-start.4
  25.1 16.6 %collective-permute-start.2 = (bf16[64,2048]{1,0:T(8,128)(2,1)S(1)}, bf16[64,2048]{1,0:T(8,128)(2,1)S(1)}, u32[]{:S(2)}, u32[]{:S(2)}) collective-permute-start(bf16[64,2048]{1,0:T(8,128)(2,1)S(1)} %get-tuple-element.39), channel_id=1, source_target_pairs={{0,2},{1,15},{2,4},{3,1},{4,6},{5,3},{6,8},{7,5},{8,10},{9,7},{10,... | collective-permute-start | bytes 786440 | tf_op jit(solution)/shard_map/ppermute | solution.py:218
  42.9 10.5 %collective-permute-start.3 = (bf16[128,2048]{1,0:T(8,128)(2,1)}, bf16[128,2048]{1,0:T(8,128)(2,1)}, u32[]{:S(2)}, u32[]{:S(2)}) collective-permute-start(bf16[128,2048]{1,0:T(8,128)(2,1)} %add_own.1), channel_id=1, source_target_pairs={{0,2},{1,15},{2,4},{3,1},{4,6},{5,3},{6,8},{7,5},{8,10},{9,7},{10,... | collective-permute-start | bytes 1572872 | tf_op jit(solution)/shard_map/ppermute | solution.py:218
  46.9 18.7 %all-to-all-start.1 = ((bf16[4,288,512]{2,1,0:T(8,128)(2,1)}), bf16[4,288,512]{2,1,0:T(8,128)(2,1)S(1)}, u32[]{:S(2)}, u32[]{:S(2)}) async-start(bf16[4,288,512]{2,1,0:T(8,128)(2,1)} %pick_factors.1), calls=%async_computation.1 | async-start | bytes 2359296 | tf_op jit(solution)/shard_map/all_to_all | solution.py:423
  50.4 15.2 %copy-start = (bf16[2048,512]{1,0:T(8,128)(2,1)S(1)}, bf16[2048,512]{1,0:T(8,128)(2,1)}, u32[]{:S(2)}) copy-start(bf16[2048,512]{1,0:T(8,128)(2,1)} %hidden_ref.3) | copy-start | bytes 6291460
  55.9 22.1 %collective-permute-start.4 = (bf16[128,2048]{1,0:T(8,128)(2,1)}, bf16[128,2048]{1,0:T(8,128)(2,1)}, u32[]{:S(2)}, u32[]{:S(2)}) collective-permute-start(bf16[128,2048]{1,0:T(8,128)(2,1)} %add_parts.2), channel_id=1, source_target_pairs={{0,2},{1,15},{2,4},{3,1},{4,6},{5,3},{6,8},{7,5},{8,10},{9,7},{10,... | collective-permute-start | bytes 1572872 | tf_op jit(solution)/shard_map/ppermute | solution.py:218
  66.9 0.7 copy-start.2
  67.6 0.6 copy-start.5
  68.2 21.5 %all-to-all-start.2 = ((bf16[16,64,128]{2,1,0:T(8,128)(2,1)}), bf16[16,64,128]{2,1,0:T(8,128)(2,1)S(1)}, u32[]{:S(2)}, u32[]{:S(2)}) async-start(bf16[16,64,128]{2,1,0:T(8,128)(2,1)} %copy-done.2), calls=%async_computation.2 | async-start | bytes 524288 | tf_op jit(solution)/shard_map/all_to_all | solution.py:425
  80.5 24.5 %copy-start.6 = (bf16[4,16,512]{2,1,0:T(8,128)(2,1)S(1)}, bf16[4,16,512]{2,1,0:T(8,128)(2,1)}, u32[]{:S(2)}) copy-start(bf16[4,16,512]{2,1,0:T(8,128)(2,1)} %copy-done.5) | copy-start | bytes 196612
  80.5 24.5 %copy-start.7 = (s32[4]{0:T(128)S(1)}, s32[4]{0:T(128)}, u32[]{:S(2)}) copy-start(s32[4]{0:T(128)} %lengths_ref.1) | copy-start | bytes 52
  80.5 13.4 %collective-permute-start.5 = (bf16[128,2048]{1,0:T(8,128)(2,1)}, bf16[128,2048]{1,0:T(8,128)(2,1)S(1)}, u32[]{:S(2)}, u32[]{:S(2)}) collective-permute-start(bf16[128,2048]{1,0:T(8,128)(2,1)} %add_parts.3), channel_id=1, source_target_pairs={{0,2},{1,15},{2,4},{3,1},{4,6},{5,3},{6,8},{7,5},{8,10},{9,7},{10,... | collective-permute-start | bytes 1572872 | tf_op jit(solution)/shard_map/ppermute | solution.py:218
  90.5 14.6 %all-to-all-start.3 = ((bf16[16,64,128]{2,1,0:T(8,128)(2,1)}), bf16[16,64,128]{2,1,0:T(8,128)(2,1)S(1)}, u32[]{:S(2)}, u32[]{:S(2)}) async-start(bf16[16,64,128]{2,1,0:T(8,128)(2,1)} %sum_parts.1), calls=%async_computation.3 | async-start | bytes 524288 | tf_op jit(solution)/shard_map/all_to_all | solution.py:427
  94.0 3.4 %collective-permute-start.6 = (bf16[64,2048]{1,0:T(8,128)(2,1)S(1)}, bf16[64,2048]{1,0:T(8,128)(2,1)S(1)}, u32[]{:S(2)}, u32[]{:S(2)}) collective-permute-start(bf16[64,2048]{1,0:T(8,128)(2,1)S(1)} %get-tuple-element.41), channel_id=1, source_target_pairs={{0,1},{1,0},{2,3},{3,2},{4,5},{5,4},{6,7},{7,6},{8,9},{9,8},{10,11... | collective-permute-start | bytes 786440 | tf_op jit(solution)/shard_map/ppermute | solution.py:223

commit v7 on v6

--- a/solution.py
+++ b/solution.py
@@ -108,7 +108,7 @@
     places = [
         [(near_ref, 0)],
         [(middle_ref, 0)],
-        [(out_refs[2], 0), (out_refs[5], span), (out_refs[6], span + columns)],
+        [(out_refs[2], 0), (out_refs[5], span)],
         [(out_refs[3], 0), (out_refs[4], span)],
     ]
     leave = []
@@ -133,7 +133,7 @@
     tokens, features = hidden.shape
     kind = hidden.dtype
     span = CORES * columns
-    heights = [2 * span] * 2 + [span] * 3 + [columns] * 2
+    heights = [2 * span] * 2 + [span] * 4
     anywhere = pl.BlockSpec(memory_space=pl.ANY)
     return pl.pallas_call(
         project_kernel,
@@ -185,10 +185,11 @@
     out_ref[...] = sum_refs(part_ref[...], other, came_ref[...])
 
 
-def add_far_kernel(first, far_ref, own_ref, other_ref, far_out_ref, own_out_ref):
-    columns = own_ref.shape[0]
-    own_out_ref[...] = sum_refs(own_ref[...], other_ref[first : first + columns])
-    far_out_ref[...] = sum_refs(far_ref[...], other_ref[first + columns : first + 2 * columns])
+def add_far_kernel(first, tail_ref, other_ref, far_out_ref, own_out_ref):
+    total = sum_refs(tail_ref[...], other_ref[first : first + tail_ref.shape[0]])
+    columns = own_out_ref.shape[0]
+    own_out_ref[...] = total[:columns]
+    far_out_ref[...] = total[columns:]
 
 
 def add_own_kernel(first, part_ref, other_ref, came_ref, out_ref):
@@ -385,9 +386,9 @@
 
     columns = adapter_up_store.shape[2]
     span = CORES * columns
-    near, middle, *parts, own, far = project(hidden, value_matrix, columns)
+    near, middle, *parts, tail = project(hidden, value_matrix, columns)
     near, middle = along("core", near, 1), along("core", middle, 1)
-    *parts, own, far, rollout_adapter = lax.optimization_barrier((*parts, own, far, rollout_adapter))
+    *parts, tail, rollout_adapter = lax.optimization_barrier((*parts, tail, rollout_adapter))
 
     def add(kernel, first, weight, name, part, *others):
         return vmem_call(functools.partial(kernel, first), name, weight, like(part), part, *others)
@@ -396,9 +397,8 @@
         functools.partial(add_far_kernel, span),
         "add_far",
         WEIGHTS[0],
-        [like(far), like(own)],
-        far,
-        own,
+        [like(tail, columns)] * 2,
+        tail,
         near,
     )
     chain = add(add_own_kernel, 0, WEIGHTS[1], "add_own", parts[0], near, hop(chain))

time: 107 us -> 107 us (level)
    unnamed x20 -> x18, local copies, waits for them, and re-layouts: 3.24 us -> 2.39 us
where the time goes in v7:
time: 107 us
  starting transfers between devices  54.5 us (51%)
  waiting for transfers between devices  21.8 us (20%)
  Pallas kernels  19.9 us (19%)
  blocking collectives  7.44 us (7%)
  local copies, waits for them, and re-layouts  2.47 us (2%)
    ppermute x4, starting transfers between devices, hop(): return lax.ppermute(value, TENSOR, pairs)  21.4 us
    all_to_all x2, starting transfers between devices, on_device(): down = lax.all_to_all(down, TENSOR, 0, 0)  13.2 us
    all_to_all x2, waiting for transfers between devices, on_device(): down = lax.all_to_all(down, TENSOR, 0, 0)  12.2 us
    ppermute x3, starting transfers between devices, along(): return lax.ppermute(value, axis, [(i, (i + step) % n) for i in range(n)])  8.63 us
    all_to_all x1, starting transfers between devices, on_device(): row = lax.all_to_all(copies, 'y', 0, 0)  7.66 us
    psum x1, blocking collectives, on_device(): lax.psum(jnp.where(mine, rollout_adapter[None, :], 0), 'x').reshape(-1)  7.44 us
    pallas_call x5, Pallas kernels, vmem_call(): pl.pallas_call(kernel, out_shape=out_shape, in_specs=[spec] * len(operand...  6.38 us
    pallas_call x1, Pallas kernels, project(): pl.pallas_call(project_kernel, out_shape=[jax.ShapeDtypeStruct((height, t...  5.98 us
  transfers between devices with their start and end apart: 11, of which 6 were waited for; matrix products, arithmetic and copies ran while one was open for 0% of the time, Pallas kernels for 15%

profile of v7, /device:TPU:1, one launch (start us, length us, event | category | flops | bytes accessed | tf_op | source)
XLA Modules:
  0.0 106.7 jit_solution(5415721792881422194)
XLA Ops:
  0.0 2.1 %factor_copies.1 = bf16[8,144,512]{2,1,0:T(8,128)(2,1)} custom-call(bf16[2,64,512]{2,1,0:T(8,128)(2,1)} %bitcast.2, bf16[2,64,64]{2,1,0:T(8,128)(2,1)} %up_ref.1), custom_call_target="tpu_custom_call" | custom-call | bytes 1179648 | tf_op jit(solution)/shard_map/factor_copies/pallas_call | solution.py:52
  2.1 7.7 %all-to-all-start = ((bf16[8,144,512]{2,1,0:T(8,128)(2,1)}), bf16[8,144,512]{2,1,0:T(8,128)(2,1)S(1)}, u32[]{:S(2)}, u32[]{:S(2)}) async-start(bf16[8,144,512]{2,1,0:T(8,128)(2,1)} %factor_copies.1), calls=%async_computation | async-start | bytes 2359296 | tf_op jit(solution)/shard_map/all_to_all | solution.py:385
  9.7 6.0 %project.1 = (bf16[256,2048]{1,0:T(8,128)(2,1)}, bf16[256,2048]{1,0:T(8,128)(2,1)}, bf16[128,2048]{1,0:T(8,128)(2,1)}, bf16[128,2048]{1,0:T(8,128)(2,1)}, bf16[1...) custom-call(bf16[2048,512]{1,0:T(8,128)(2,1)} %hidden_ref.3, bf16[512,1024]{1,0:T(8,128)(2,1)} %matrix_ref.1), custom_call_target="tpu_custom_call" | custom-call | tf_op jit(solution)/shard_map/project/pallas_call | solution.py:138
  15.8 4.7 %collective-permute-start = (bf16[256,2048]{1,0:T(8,128)(2,1)}, bf16[256,2048]{1,0:T(8,128)(2,1)S(1)}, u32[]{:S(2)}, u32[]{:S(2)}) collective-permute-start(bf16[256,2048]{1,0:T(8,128)(2,1)} %get-tuple-element.29), channel_id=1, source_target_pairs={{0,1},{1,0},{2,3},{3,2},{4,5},{5,4},{6,7},{7,6},{8,9},{9,8},{10,11... | collective-permute-start | bytes 3145736 | tf_op jit(solution)/shard_map/ppermute | solution.py:224
  20.5 1.9 %collective-permute-start.1 = (bf16[256,2048]{1,0:T(8,128)(2,1)}, bf16[256,2048]{1,0:T(8,128)(2,1)}, u32[]{:S(2)}, u32[]{:S(2)}) collective-permute-start(bf16[256,2048]{1,0:T(8,128)(2,1)} %get-tuple-element.32), channel_id=1, source_target_pairs={{0,1},{1,0},{2,3},{3,2},{4,5},{5,4},{6,7},{7,6},{8,9},{9,8},{10,11... | collective-permute-start | bytes 3145736 | tf_op jit(solution)/shard_map/ppermute | solution.py:224
  24.1 9.0 %collective-permute-start.2 = (bf16[64,2048]{1,0:T(8,128)(2,1)S(1)}, bf16[64,2048]{1,0:T(8,128)(2,1)S(1)}, u32[]{:S(2)}, u32[]{:S(2)}) collective-permute-start(bf16[64,2048]{1,0:T(8,128)(2,1)S(1)} %get-tuple-element.35), channel_id=1, source_target_pairs={{0,2},{1,15},{2,4},{3,1},{4,6},{5,3},{6,8},{7,5},{8,10},{9,7},{10,... | collective-permute-start | bytes 786440 | tf_op jit(solution)/shard_map/ppermute | solution.py:219
  33.3 7.4 %psum.7 = s32[16]{0:T(128)S(1)} all-reduce(s32[16]{0:T(128)S(1)} %eq.28), channel_id=1, replica_groups=mesh['x'=4,'y'=8,'z'=8,'core'=2] {'x'}, use_global_device_ids=true, to_apply=%region_0.1 | all-reduce | flops 16 | bytes 128 | tf_op jit(solution)/shard_map/psum | solution.py:414
  42.1 2.0 %collective-permute-start.3 = (bf16[128,2048]{1,0:T(8,128)(2,1)}, bf16[128,2048]{1,0:T(8,128)(2,1)}, u32[]{:S(2)}, u32[]{:S(2)}) collective-permute-start(bf16[128,2048]{1,0:T(8,128)(2,1)} %add_own.1), channel_id=1, source_target_pairs={{0,2},{1,15},{2,4},{3,1},{4,6},{5,3},{6,8},{7,5},{8,10},{9,7},{10,... | collective-permute-start | bytes 1572872 | tf_op jit(solution)/shard_map/ppermute | solution.py:219
  44.2 1.8 %pick_factors.1 = bf16[4,288,512]{2,1,0:T(8,128)(2,1)} custom-call(s32[16]{0:T(128)S(1)} %subtract_clamp_fusion.index_ref, bf16[8,144,512]{2,1,0:T(8,128)(2,1)S(1)} %all-to-all-done.row_ref), custom_call_target="tpu_custom_call" | custom-call | bytes 2359296 | tf_op jit(solution)/shard_map/pick_factors/pallas_call | solution.py:259
  46.0 3.5 %all-to-all-start.1 = ((bf16[4,288,512]{2,1,0:T(8,128)(2,1)}), bf16[4,288,512]{2,1,0:T(8,128)(2,1)S(1)}, u32[]{:S(2)}, u32[]{:S(2)}) async-start(bf16[4,288,512]{2,1,0:T(8,128)(2,1)} %pick_factors.1), calls=%async_computation.1 | async-start | bytes 2359296 | tf_op jit(solution)/shard_map/all_to_all | solution.py:423
  49.6 3.0 %collective-permute-done.3.came_ref = bf16[128,2048]{1,0:T(8,128)(2,1)} collective-permute-done((bf16[128,2048]{1,0:T(8,128)(2,1)}, bf16[128,2048]{1,0:T(8,128)(2,1)}, u32[]{:S(2)}, u32[]{:S(2)}) %collective-permute-start.3) | collective-permute-done | bytes 524320 | tf_op jit(solution)/shard_map/ppermute | solution.py:219
  52.6 2.5 %add_parts.2 = bf16[128,2048]{1,0:T(8,128)(2,1)} custom-call(bf16[128,2048]{1,0:T(8,128)(2,1)} %get-tuple-element.33.part_ref, bf16[256,2048]{1,0:T(8,128)(2,1)} %collective-permute-done.1.other_ref, bf16[128,2048]{1,0:T(8,128)(2,1)} %collective-permute-done.3.came_ref), custom_call_target="tpu_custom_call" | custom-call | flops 262144 | bytes 1572864 | tf_op jit(solution)/shard_map/add_parts/pallas_call | solution.py:161
  55.1 5.8 %collective-permute-start.4 = (bf16[128,2048]{1,0:T(8,128)(2,1)}, bf16[128,2048]{1,0:T(8,128)(2,1)}, u32[]{:S(2)}, u32[]{:S(2)}) collective-permute-start(bf16[128,2048]{1,0:T(8,128)(2,1)} %add_parts.2), channel_id=1, source_target_pairs={{0,2},{1,15},{2,4},{3,1},{4,6},{5,3},{6,8},{7,5},{8,10},{9,7},{10,... | collective-permute-start | bytes 1572872 | tf_op jit(solution)/shard_map/ppermute | solution.py:219
  60.9 4.7 %all-to-all-done.1.factor_ref = bf16[4,288,512]{2,1,0:T(8,128)(2,1)S(1)} async-done(((bf16[4,288,512]{2,1,0:T(8,128)(2,1)}), bf16[4,288,512]{2,1,0:T(8,128)(2,1)S(1)}, u32[]{:S(2)}, u32[]{:S(2)}) %all-to-all-start.1) | async-done | bytes 1179680 | tf_op jit(solution)/shard_map/all_to_all | solution.py:423
  65.6 1.3 %down_projection.1 = (bf16[16,64,128]{2,1,0:T(8,128)(2,1)S(1)}, bf16[4,16,512]{2,1,0:T(8,128)(2,1)S(1)}) custom-call(s32[4]{0:T(128)S(1)} %and_select_fusion.own_row_ref, bf16[2048,512]{1,0:T(8,128)(2,1)S(1)} %copy-done, bf16[4,288,512]{2,1,0:T(8,128)(2,1)S(1)} %all-to-all-done.1.factor_ref), custom_call_target="tpu_custom_call" | custom-call | flops 134217728 | bytes 2359296 | tf_op jit(solution)/shard_map/down_projection/pallas_call | solution.py:295
  68.2 9.8 %all-to-all-start.2 = ((bf16[16,64,128]{2,1,0:T(8,128)(2,1)}), bf16[16,64,128]{2,1,0:T(8,128)(2,1)S(1)}, u32[]{:S(2)}, u32[]{:S(2)}) async-start(bf16[16,64,128]{2,1,0:T(8,128)(2,1)} %copy-done.3), calls=%async_computation.2 | async-start | bytes 524288 | tf_op jit(solution)/shard_map/all_to_all | solution.py:425
  78.0 2.5 %add_parts.3 = bf16[128,2048]{1,0:T(8,128)(2,1)} custom-call(bf16[128,2048]{1,0:T(8,128)(2,1)} %get-tuple-element.31.part_ref, bf16[256,2048]{1,0:T(8,128)(2,1)} %collective-permute-done.1.other_ref, bf16[128,2048]{1,0:T(8,128)(2,1)} %collective-permute-done.4.came_ref), custom_call_target="tpu_custom_call" | custom-call | flops 13107200000 | bytes 1572864 | tf_op jit(solution)/shard_map/add_parts/pallas_call | solution.py:161
  80.6 4.6 %collective-permute-start.5 = (bf16[128,2048]{1,0:T(8,128)(2,1)}, bf16[128,2048]{1,0:T(8,128)(2,1)S(1)}, u32[]{:S(2)}, u32[]{:S(2)}) collective-permute-start(bf16[128,2048]{1,0:T(8,128)(2,1)} %add_parts.3), channel_id=1, source_target_pairs={{0,2},{1,15},{2,4},{3,1},{4,6},{5,3},{6,8},{7,5},{8,10},{9,7},{10,... | collective-permute-start | bytes 1572872 | tf_op jit(solution)/shard_map/ppermute | solution.py:219
  85.2 4.6 %all-to-all-done.2.parts_ref = bf16[16,64,128]{2,1,0:T(8,128)(2,1)S(1)} async-done(((bf16[16,64,128]{2,1,0:T(8,128)(2,1)}), bf16[16,64,128]{2,1,0:T(8,128)(2,1)S(1)}, u32[]{:S(2)}, u32[]{:S(2)}) %all-to-all-start.2) | async-done | bytes 262176 | tf_op jit(solution)/shard_map/all_to_all | solution.py:425
  90.5 3.4 %all-to-all-start.3 = ((bf16[16,64,128]{2,1,0:T(8,128)(2,1)}), bf16[16,64,128]{2,1,0:T(8,128)(2,1)S(1)}, u32[]{:S(2)}, u32[]{:S(2)}) async-start(bf16[16,64,128]{2,1,0:T(8,128)(2,1)} %sum_parts.1), calls=%async_computation.3 | async-start | bytes 524288 | tf_op jit(solution)/shard_map/all_to_all | solution.py:427
  94.1 2.0 %collective-permute-start.6 = (bf16[64,2048]{1,0:T(8,128)(2,1)S(1)}, bf16[64,2048]{1,0:T(8,128)(2,1)S(1)}, u32[]{:S(2)}, u32[]{:S(2)}) collective-permute-start(bf16[64,2048]{1,0:T(8,128)(2,1)S(1)} %get-tuple-element.37), channel_id=1, source_target_pairs={{0,1},{1,0},{2,3},{3,2},{4,5},{5,4},{6,7},{7,6},{8,9},{9,8},{10,11... | collective-permute-start | bytes 786440 | tf_op jit(solution)/shard_map/ppermute | solution.py:224
  96.1 1.4 %collective-permute-done.6.refs_1_ = bf16[64,2048]{1,0:T(8,128)(2,1)S(1)} collective-permute-done((bf16[64,2048]{1,0:T(8,128)(2,1)S(1)}, bf16[64,2048]{1,0:T(8,128)(2,1)S(1)}, u32[]{:S(2)}, u32[]{:S(2)}) %collective-permute-start.6) | collective-permute-done | bytes 262176 | tf_op jit(solution)/shard_map/ppermute | solution.py:224
  97.5 7.6 %all-to-all-done.3.refs_2_ = bf16[16,64,128]{2,1,0:T(8,128)(2,1)S(1)} async-done(((bf16[16,64,128]{2,1,0:T(8,128)(2,1)}), bf16[16,64,128]{2,1,0:T(8,128)(2,1)S(1)}, u32[]{:S(2)}, u32[]{:S(2)}) %all-to-all-start.3) | async-done | bytes 262176 | tf_op jit(solution)/shard_map/all_to_all | solution.py:427
  105.1 1.6 %add_update.1 = bf16[64,2048]{1,0:T(8,128)(2,1)} custom-call(s32[4]{0:T(128)S(1)} %copy-done.6, bf16[64,2048]{1,0:T(8,128)(2,1)S(1)} %get-tuple-element.36.refs_0_, bf16[64,2048]{1,0:T(8,128)(2,1)S(1)} %collective-permute-done.6.refs_1_, bf16[16,64,128]{2,1,0:T(8,128)(2,1)S(1)} %all-to-all-done.3.refs_2_, bf16[4,16,512]{2,1,0:T(8,128)(2,1)S(1)} %copy-done.5), custom_call_target="tpu_custom_call" | custom-call | flops 16777216 | bytes 1310720 | tf_op jit(solution)/shard_map/add_update/pallas_call | solution.py:362
  (34 shorter events, 5.5 us)
Async XLA Ops:
  2.1 42.1 %all-to-all-start = ((bf16[8,144,512]{2,1,0:T(8,128)(2,1)}), bf16[8,144,512]{2,1,0:T(8,128)(2,1)S(1)}, u32[]{:S(2)}, u32[]{:S(2)}) async-start(bf16[8,144,512]{2,1,0:T(8,128)(2,1)} %factor_copies.1), calls=%async_computation | async-start | bytes 2359296 | tf_op jit(solution)/shard_map/all_to_all | solution.py:385
  15.7 17.4 %copy-start.7 = (s32[4]{0:T(128)S(1)}, s32[4]{0:T(128)}, u32[]{:S(2)}) copy-start(s32[4]{0:T(128)} %param.12) | copy-start | bytes 52
  15.7 25.0 %copy-start.8 = (s32[64]{0:T(128)S(1)}, s32[64]{0:T(128)}, u32[]{:S(2)}) copy-start(s32[64]{0:T(128)} %param.11) | copy-start | bytes 772
  15.8 7.2 %collective-permute-start = (bf16[256,2048]{1,0:T(8,128)(2,1)}, bf16[256,2048]{1,0:T(8,128)(2,1)S(1)}, u32[]{:S(2)}, u32[]{:S(2)}) collective-permute-start(bf16[256,2048]{1,0:T(8,128)(2,1)} %get-tuple-element.29), channel_id=1, source_target_pairs={{0,1},{1,0},{2,3},{3,2},{4,5},{5,4},{6,7},{7,6},{8,9},{9,8},{10,11... | collective-permute-start | bytes 3145736 | tf_op jit(solution)/shard_map/ppermute | solution.py:224
  20.5 29.1 %collective-permute-start.1 = (bf16[256,2048]{1,0:T(8,128)(2,1)}, bf16[256,2048]{1,0:T(8,128)(2,1)}, u32[]{:S(2)}, u32[]{:S(2)}) collective-permute-start(bf16[256,2048]{1,0:T(8,128)(2,1)} %get-tuple-element.32), channel_id=1, source_target_pairs={{0,1},{1,0},{2,3},{3,2},{4,5},{5,4},{6,7},{7,6},{8,9},{9,8},{10,11... | collective-permute-start | bytes 3145736 | tf_op jit(solution)/shard_map/ppermute | solution.py:224
  23.0 1.0 copy-start.1
  24.0 16.9 %copy-start.2 = (bf16[128,2048]{1,0:T(8,128)(2,1)S(1)}, bf16[128,2048]{1,0:T(8,128)(2,1)}, u32[]{:S(2)}) copy-start(bf16[128,2048]{1,0:T(8,128)(2,1)} %get-tuple-element.34.part_ref) | copy-start | bytes 1572868
  24.1 16.8 %collective-permute-start.2 = (bf16[64,2048]{1,0:T(8,128)(2,1)S(1)}, bf16[64,2048]{1,0:T(8,128)(2,1)S(1)}, u32[]{:S(2)}, u32[]{:S(2)}) collective-permute-start(bf16[64,2048]{1,0:T(8,128)(2,1)S(1)} %get-tuple-element.35), channel_id=1, source_target_pairs={{0,2},{1,15},{2,4},{3,1},{4,6},{5,3},{6,8},{7,5},{8,10},{9,7},{10,... | collective-permute-start | bytes 786440 | tf_op jit(solution)/shard_map/ppermute | solution.py:219
  42.1 10.5 %collective-permute-start.3 = (bf16[128,2048]{1,0:T(8,128)(2,1)}, bf16[128,2048]{1,0:T(8,128)(2,1)}, u32[]{:S(2)}, u32[]{:S(2)}) collective-permute-start(bf16[128,2048]{1,0:T(8,128)(2,1)} %add_own.1), channel_id=1, source_target_pairs={{0,2},{1,15},{2,4},{3,1},{4,6},{5,3},{6,8},{7,5},{8,10},{9,7},{10,... | collective-permute-start | bytes 1572872 | tf_op jit(solution)/shard_map/ppermute | solution.py:219
  46.0 19.6 %all-to-all-start.1 = ((bf16[4,288,512]{2,1,0:T(8,128)(2,1)}), bf16[4,288,512]{2,1,0:T(8,128)(2,1)S(1)}, u32[]{:S(2)}, u32[]{:S(2)}) async-start(bf16[4,288,512]{2,1,0:T(8,128)(2,1)} %pick_factors.1), calls=%async_computation.1 | async-start | bytes 2359296 | tf_op jit(solution)/shard_map/all_to_all | solution.py:423
  49.6 16.0 %copy-start = (bf16[2048,512]{1,0:T(8,128)(2,1)S(1)}, bf16[2048,512]{1,0:T(8,128)(2,1)}, u32[]{:S(2)}) copy-start(bf16[2048,512]{1,0:T(8,128)(2,1)} %hidden_ref.3) | copy-start | bytes 6291460
  55.1 22.9 %collective-permute-start.4 = (bf16[128,2048]{1,0:T(8,128)(2,1)}, bf16[128,2048]{1,0:T(8,128)(2,1)}, u32[]{:S(2)}, u32[]{:S(2)}) collective-permute-start(bf16[128,2048]{1,0:T(8,128)(2,1)} %add_parts.2), channel_id=1, source_target_pairs={{0,2},{1,15},{2,4},{3,1},{4,6},{5,3},{6,8},{7,5},{8,10},{9,7},{10,... | collective-permute-start | bytes 1572872 | tf_op jit(solution)/shard_map/ppermute | solution.py:219
  66.9 0.7 copy-start.3
  67.6 0.6 copy-start.4
  68.2 21.5 %all-to-all-start.2 = ((bf16[16,64,128]{2,1,0:T(8,128)(2,1)}), bf16[16,64,128]{2,1,0:T(8,128)(2,1)S(1)}, u32[]{:S(2)}, u32[]{:S(2)}) async-start(bf16[16,64,128]{2,1,0:T(8,128)(2,1)} %copy-done.3), calls=%async_computation.2 | async-start | bytes 524288 | tf_op jit(solution)/shard_map/all_to_all | solution.py:425
  80.6 24.5 %copy-start.5 = (bf16[4,16,512]{2,1,0:T(8,128)(2,1)S(1)}, bf16[4,16,512]{2,1,0:T(8,128)(2,1)}, u32[]{:S(2)}) copy-start(bf16[4,16,512]{2,1,0:T(8,128)(2,1)} %copy-done.4) | copy-start | bytes 196612
  80.6 24.5 %copy-start.6 = (s32[4]{0:T(128)S(1)}, s32[4]{0:T(128)}, u32[]{:S(2)}) copy-start(s32[4]{0:T(128)} %lengths_ref.1) | copy-start | bytes 52
  80.6 13.4 %collective-permute-start.5 = (bf16[128,2048]{1,0:T(8,128)(2,1)}, bf16[128,2048]{1,0:T(8,128)(2,1)S(1)}, u32[]{:S(2)}, u32[]{:S(2)}) collective-permute-start(bf16[128,2048]{1,0:T(8,128)(2,1)} %add_parts.3), channel_id=1, source_target_pairs={{0,2},{1,15},{2,4},{3,1},{4,6},{5,3},{6,8},{7,5},{8,10},{9,7},{10,... | collective-permute-start | bytes 1572872 | tf_op jit(solution)/shard_map/ppermute | solution.py:219
  90.5 14.6 %all-to-all-start.3 = ((bf16[16,64,128]{2,1,0:T(8,128)(2,1)}), bf16[16,64,128]{2,1,0:T(8,128)(2,1)S(1)}, u32[]{:S(2)}, u32[]{:S(2)}) async-start(bf16[16,64,128]{2,1,0:T(8,128)(2,1)} %sum_parts.1), calls=%async_computation.3 | async-start | bytes 524288 | tf_op jit(solution)/shard_map/all_to_all | solution.py:427
  94.1 3.4 %collective-permute-start.6 = (bf16[64,2048]{1,0:T(8,128)(2,1)S(1)}, bf16[64,2048]{1,0:T(8,128)(2,1)S(1)}, u32[]{:S(2)}, u32[]{:S(2)}) collective-permute-start(bf16[64,2048]{1,0:T(8,128)(2,1)S(1)} %get-tuple-element.37), channel_id=1, source_target_pairs={{0,1},{1,0},{2,3},{3,2},{4,5},{5,4},{6,7},{7,6},{8,9},{9,8},{10,11... | collective-permute-start | bytes 786440 | tf_op jit(solution)/shard_map/ppermute | solution.py:224

commit v8 on v7

--- a/solution.py
+++ b/solution.py
@@ -119,12 +119,15 @@
             part = slice(i * rows, (i + 1) * rows)
             product = jnp.dot(mine[part], chosen[g], preferred_element_type=jnp.float32)
             stage[g, :, part] = product.astype(stage.dtype).T
-        for ref, start in group:
-            copy = pltpu.make_async_copy(
-                stage.at[g, pl.ds(start, ref.shape[0])], ref, out_sems.at[len(leave)]
-            )
-            copy.start()
-            leave.append(copy)
+            span_of = pl.ds(i * rows, rows)
+            for ref, start in group:
+                copy = pltpu.make_async_copy(
+                    stage.at[g, pl.ds(start, ref.shape[0]), span_of],
+                    ref.at[:, span_of],
+                    out_sems.at[len(leave)],
+                )
+                copy.start()
+                leave.append(copy)
     for copy in leave:
         copy.wait()
 
@@ -146,7 +149,7 @@
             pltpu.VMEM((4, features, 2 * span), kind),
             pltpu.VMEM((4, 2 * span, tokens), kind),
             pltpu.SemaphoreType.DMA((1 + PROJECT_PARTS,)),
-            pltpu.SemaphoreType.DMA((len(heights),)),
+            pltpu.SemaphoreType.DMA((len(heights) * PROJECT_PARTS,)),
         ],
         cost_estimate=cost(0, 0),
         compiler_params=pltpu.CompilerParams(vmem_limit_bytes=PROJECT_VMEM),

time: 107 us -> 107 us (level)
  no operation moved by 1% of the time
where the time goes in v8:
time: 107 us
  starting transfers between devices  54.6 us (51%)
  waiting for transfers between devices  21.9 us (20%)
  Pallas kernels  19.7 us (18%)
  blocking collectives  7.46 us (7%)
  local copies, waits for them, and re-layouts  2.47 us (2%)
    ppermute x4, starting transfers between devices, hop(): return lax.ppermute(value, TENSOR, pairs)  21.5 us
    all_to_all x2, starting transfers between devices, on_device(): down = lax.all_to_all(down, TENSOR, 0, 0)  13.2 us
    all_to_all x2, waiting for transfers between devices, on_device(): down = lax.all_to_all(down, TENSOR, 0, 0)  12.2 us
    ppermute x3, starting transfers between devices, along(): return lax.ppermute(value, axis, [(i, (i + step) % n) for i in range(n)])  8.63 us
    all_to_all x1, starting transfers between devices, on_device(): row = lax.all_to_all(copies, 'y', 0, 0)  7.66 us
    psum x1, blocking collectives, on_device(): lax.psum(jnp.where(mine, rollout_adapter[None, :], 0), 'x').reshape(-1)  7.46 us
    pallas_call x5, Pallas kernels, vmem_call(): pl.pallas_call(kernel, out_shape=out_shape, in_specs=[spec] * len(operand...  6.38 us
    pallas_call x1, Pallas kernels, project(): pl.pallas_call(project_kernel, out_shape=[jax.ShapeDtypeStruct((height, t...  5.83 us
  transfers between devices with their start and end apart: 11, of which 6 were waited for; matrix products, arithmetic and copies ran while one was open for 0% of the time, Pallas kernels for 15%

profile of v8, /device:TPU:1, one launch (start us, length us, event | category | flops | bytes accessed | tf_op | source)
XLA Modules:
  0.0 106.7 jit_solution(4450067939754321972)
XLA Ops:
  0.0 2.1 %factor_copies.1 = bf16[8,144,512]{2,1,0:T(8,128)(2,1)} custom-call(bf16[2,64,512]{2,1,0:T(8,128)(2,1)} %bitcast.2, bf16[2,64,64]{2,1,0:T(8,128)(2,1)} %up_ref.1), custom_call_target="tpu_custom_call" | custom-call | bytes 1179648 | tf_op jit(solution)/shard_map/factor_copies/pallas_call | solution.py:52
  2.1 7.7 %all-to-all-start = ((bf16[8,144,512]{2,1,0:T(8,128)(2,1)}), bf16[8,144,512]{2,1,0:T(8,128)(2,1)S(1)}, u32[]{:S(2)}, u32[]{:S(2)}) async-start(bf16[8,144,512]{2,1,0:T(8,128)(2,1)} %factor_copies.1), calls=%async_computation | async-start | bytes 2359296 | tf_op jit(solution)/shard_map/all_to_all | solution.py:388
  9.7 5.8 %project.1 = (bf16[256,2048]{1,0:T(8,128)(2,1)}, bf16[256,2048]{1,0:T(8,128)(2,1)}, bf16[128,2048]{1,0:T(8,128)(2,1)}, bf16[128,2048]{1,0:T(8,128)(2,1)}, bf16[1...) custom-call(bf16[2048,512]{1,0:T(8,128)(2,1)} %hidden_ref.3, bf16[512,1024]{1,0:T(8,128)(2,1)} %matrix_ref.1), custom_call_target="tpu_custom_call" | custom-call | tf_op jit(solution)/shard_map/project/pallas_call | solution.py:141
  15.6 4.7 %collective-permute-start = (bf16[256,2048]{1,0:T(8,128)(2,1)}, bf16[256,2048]{1,0:T(8,128)(2,1)S(1)}, u32[]{:S(2)}, u32[]{:S(2)}) collective-permute-start(bf16[256,2048]{1,0:T(8,128)(2,1)} %get-tuple-element.29), channel_id=1, source_target_pairs={{0,1},{1,0},{2,3},{3,2},{4,5},{5,4},{6,7},{7,6},{8,9},{9,8},{10,11... | collective-permute-start | bytes 3145736 | tf_op jit(solution)/shard_map/ppermute | solution.py:227
  20.3 1.9 %collective-permute-start.1 = (bf16[256,2048]{1,0:T(8,128)(2,1)}, bf16[256,2048]{1,0:T(8,128)(2,1)}, u32[]{:S(2)}, u32[]{:S(2)}) collective-permute-start(bf16[256,2048]{1,0:T(8,128)(2,1)} %get-tuple-element.32), channel_id=1, source_target_pairs={{0,1},{1,0},{2,3},{3,2},{4,5},{5,4},{6,7},{7,6},{8,9},{9,8},{10,11... | collective-permute-start | bytes 3145736 | tf_op jit(solution)/shard_map/ppermute | solution.py:227
  24.0 9.0 %collective-permute-start.2 = (bf16[64,2048]{1,0:T(8,128)(2,1)S(1)}, bf16[64,2048]{1,0:T(8,128)(2,1)S(1)}, u32[]{:S(2)}, u32[]{:S(2)}) collective-permute-start(bf16[64,2048]{1,0:T(8,128)(2,1)S(1)} %get-tuple-element.35), channel_id=1, source_target_pairs={{0,2},{1,15},{2,4},{3,1},{4,6},{5,3},{6,8},{7,5},{8,10},{9,7},{10,... | collective-permute-start | bytes 786440 | tf_op jit(solution)/shard_map/ppermute | solution.py:222
  33.1 7.5 %psum.7 = s32[16]{0:T(128)S(1)} all-reduce(s32[16]{0:T(128)S(1)} %eq.28), channel_id=1, replica_groups=mesh['x'=4,'y'=8,'z'=8,'core'=2] {'x'}, use_global_device_ids=true, to_apply=%region_0.1 | all-reduce | flops 16 | bytes 128 | tf_op jit(solution)/shard_map/psum | solution.py:417
  41.9 2.0 %collective-permute-start.3 = (bf16[128,2048]{1,0:T(8,128)(2,1)}, bf16[128,2048]{1,0:T(8,128)(2,1)}, u32[]{:S(2)}, u32[]{:S(2)}) collective-permute-start(bf16[128,2048]{1,0:T(8,128)(2,1)} %add_own.1), channel_id=1, source_target_pairs={{0,2},{1,15},{2,4},{3,1},{4,6},{5,3},{6,8},{7,5},{8,10},{9,7},{10,... | collective-permute-start | bytes 1572872 | tf_op jit(solution)/shard_map/ppermute | solution.py:222
  44.1 1.8 %pick_factors.1 = bf16[4,288,512]{2,1,0:T(8,128)(2,1)} custom-call(s32[16]{0:T(128)S(1)} %subtract_clamp_fusion.index_ref, bf16[8,144,512]{2,1,0:T(8,128)(2,1)S(1)} %all-to-all-done.row_ref), custom_call_target="tpu_custom_call" | custom-call | bytes 2359296 | tf_op jit(solution)/shard_map/pick_factors/pallas_call | solution.py:262
  45.8 3.5 %all-to-all-start.1 = ((bf16[4,288,512]{2,1,0:T(8,128)(2,1)}), bf16[4,288,512]{2,1,0:T(8,128)(2,1)S(1)}, u32[]{:S(2)}, u32[]{:S(2)}) async-start(bf16[4,288,512]{2,1,0:T(8,128)(2,1)} %pick_factors.1), calls=%async_computation.1 | async-start | bytes 2359296 | tf_op jit(solution)/shard_map/all_to_all | solution.py:426
  49.4 3.1 %collective-permute-done.3.came_ref = bf16[128,2048]{1,0:T(8,128)(2,1)} collective-permute-done((bf16[128,2048]{1,0:T(8,128)(2,1)}, bf16[128,2048]{1,0:T(8,128)(2,1)}, u32[]{:S(2)}, u32[]{:S(2)}) %collective-permute-start.3) | collective-permute-done | bytes 524320 | tf_op jit(solution)/shard_map/ppermute | solution.py:222
  52.5 2.5 %add_parts.2 = bf16[128,2048]{1,0:T(8,128)(2,1)} custom-call(bf16[128,2048]{1,0:T(8,128)(2,1)} %get-tuple-element.33.part_ref, bf16[256,2048]{1,0:T(8,128)(2,1)} %collective-permute-done.1.other_ref, bf16[128,2048]{1,0:T(8,128)(2,1)} %collective-permute-done.3.came_ref), custom_call_target="tpu_custom_call" | custom-call | flops 262144 | bytes 1572864 | tf_op jit(solution)/shard_map/add_parts/pallas_call | solution.py:164
  55.0 5.9 %collective-permute-start.4 = (bf16[128,2048]{1,0:T(8,128)(2,1)}, bf16[128,2048]{1,0:T(8,128)(2,1)}, u32[]{:S(2)}, u32[]{:S(2)}) collective-permute-start(bf16[128,2048]{1,0:T(8,128)(2,1)} %add_parts.2), channel_id=1, source_target_pairs={{0,2},{1,15},{2,4},{3,1},{4,6},{5,3},{6,8},{7,5},{8,10},{9,7},{10,... | collective-permute-start | bytes 1572872 | tf_op jit(solution)/shard_map/ppermute | solution.py:222
  60.9 4.7 %all-to-all-done.1.factor_ref = bf16[4,288,512]{2,1,0:T(8,128)(2,1)S(1)} async-done(((bf16[4,288,512]{2,1,0:T(8,128)(2,1)}), bf16[4,288,512]{2,1,0:T(8,128)(2,1)S(1)}, u32[]{:S(2)}, u32[]{:S(2)}) %all-to-all-start.1) | async-done | bytes 1179680 | tf_op jit(solution)/shard_map/all_to_all | solution.py:426
  65.6 1.3 %down_projection.1 = (bf16[16,64,128]{2,1,0:T(8,128)(2,1)S(1)}, bf16[4,16,512]{2,1,0:T(8,128)(2,1)S(1)}) custom-call(s32[4]{0:T(128)S(1)} %and_select_fusion.own_row_ref, bf16[2048,512]{1,0:T(8,128)(2,1)S(1)} %copy-done, bf16[4,288,512]{2,1,0:T(8,128)(2,1)S(1)} %all-to-all-done.1.factor_ref), custom_call_target="tpu_custom_call" | custom-call | flops 134217728 | bytes 2359296 | tf_op jit(solution)/shard_map/down_projection/pallas_call | solution.py:298
  68.2 9.8 %all-to-all-start.2 = ((bf16[16,64,128]{2,1,0:T(8,128)(2,1)}), bf16[16,64,128]{2,1,0:T(8,128)(2,1)S(1)}, u32[]{:S(2)}, u32[]{:S(2)}) async-start(bf16[16,64,128]{2,1,0:T(8,128)(2,1)} %copy-done.3), calls=%async_computation.2 | async-start | bytes 524288 | tf_op jit(solution)/shard_map/all_to_all | solution.py:428
  78.0 2.5 %add_parts.3 = bf16[128,2048]{1,0:T(8,128)(2,1)} custom-call(bf16[128,2048]{1,0:T(8,128)(2,1)} %get-tuple-element.31.part_ref, bf16[256,2048]{1,0:T(8,128)(2,1)} %collective-permute-done.1.other_ref, bf16[128,2048]{1,0:T(8,128)(2,1)} %collective-permute-done.4.came_ref), custom_call_target="tpu_custom_call" | custom-call | flops 13107200000 | bytes 1572864 | tf_op jit(solution)/shard_map/add_parts/pallas_call | solution.py:164
  80.6 4.6 %collective-permute-start.5 = (bf16[128,2048]{1,0:T(8,128)(2,1)}, bf16[128,2048]{1,0:T(8,128)(2,1)S(1)}, u32[]{:S(2)}, u32[]{:S(2)}) collective-permute-start(bf16[128,2048]{1,0:T(8,128)(2,1)} %add_parts.3), channel_id=1, source_target_pairs={{0,2},{1,15},{2,4},{3,1},{4,6},{5,3},{6,8},{7,5},{8,10},{9,7},{10,... | collective-permute-start | bytes 1572872 | tf_op jit(solution)/shard_map/ppermute | solution.py:222
  85.2 4.6 %all-to-all-done.2.parts_ref = bf16[16,64,128]{2,1,0:T(8,128)(2,1)S(1)} async-done(((bf16[16,64,128]{2,1,0:T(8,128)(2,1)}), bf16[16,64,128]{2,1,0:T(8,128)(2,1)S(1)}, u32[]{:S(2)}, u32[]{:S(2)}) %all-to-all-start.2) | async-done | bytes 262176 | tf_op jit(solution)/shard_map/all_to_all | solution.py:428
  90.5 3.4 %all-to-all-start.3 = ((bf16[16,64,128]{2,1,0:T(8,128)(2,1)}), bf16[16,64,128]{2,1,0:T(8,128)(2,1)S(1)}, u32[]{:S(2)}, u32[]{:S(2)}) async-start(bf16[16,64,128]{2,1,0:T(8,128)(2,1)} %sum_parts.1), calls=%async_computation.3 | async-start | bytes 524288 | tf_op jit(solution)/shard_map/all_to_all | solution.py:430
  94.1 2.0 %collective-permute-start.6 = (bf16[64,2048]{1,0:T(8,128)(2,1)S(1)}, bf16[64,2048]{1,0:T(8,128)(2,1)S(1)}, u32[]{:S(2)}, u32[]{:S(2)}) collective-permute-start(bf16[64,2048]{1,0:T(8,128)(2,1)S(1)} %get-tuple-element.37), channel_id=1, source_target_pairs={{0,1},{1,0},{2,3},{3,2},{4,5},{5,4},{6,7},{7,6},{8,9},{9,8},{10,11... | collective-permute-start | bytes 786440 | tf_op jit(solution)/shard_map/ppermute | solution.py:227
  96.1 1.4 %collective-permute-done.6.refs_1_ = bf16[64,2048]{1,0:T(8,128)(2,1)S(1)} collective-permute-done((bf16[64,2048]{1,0:T(8,128)(2,1)S(1)}, bf16[64,2048]{1,0:T(8,128)(2,1)S(1)}, u32[]{:S(2)}, u32[]{:S(2)}) %collective-permute-start.6) | collective-permute-done | bytes 262176 | tf_op jit(solution)/shard_map/ppermute | solution.py:227
  97.5 7.6 %all-to-all-done.3.refs_2_ = bf16[16,64,128]{2,1,0:T(8,128)(2,1)S(1)} async-done(((bf16[16,64,128]{2,1,0:T(8,128)(2,1)}), bf16[16,64,128]{2,1,0:T(8,128)(2,1)S(1)}, u32[]{:S(2)}, u32[]{:S(2)}) %all-to-all-start.3) | async-done | bytes 262176 | tf_op jit(solution)/shard_map/all_to_all | solution.py:430
  105.1 1.6 %add_update.1 = bf16[64,2048]{1,0:T(8,128)(2,1)} custom-call(s32[4]{0:T(128)S(1)} %copy-done.6, bf16[64,2048]{1,0:T(8,128)(2,1)S(1)} %get-tuple-element.36.refs_0_, bf16[64,2048]{1,0:T(8,128)(2,1)S(1)} %collective-permute-done.6.refs_1_, bf16[16,64,128]{2,1,0:T(8,128)(2,1)S(1)} %all-to-all-done.3.refs_2_, bf16[4,16,512]{2,1,0:T(8,128)(2,1)S(1)} %copy-done.5), custom_call_target="tpu_custom_call" | custom-call | flops 16777216 | bytes 1310720 | tf_op jit(solution)/shard_map/add_update/pallas_call | solution.py:365
  (34 shorter events, 5.5 us)
Async XLA Ops:
  2.1 42.0 %all-to-all-start = ((bf16[8,144,512]{2,1,0:T(8,128)(2,1)}), bf16[8,144,512]{2,1,0:T(8,128)(2,1)S(1)}, u32[]{:S(2)}, u32[]{:S(2)}) async-start(bf16[8,144,512]{2,1,0:T(8,128)(2,1)} %factor_copies.1), calls=%async_computation | async-start | bytes 2359296 | tf_op jit(solution)/shard_map/all_to_all | solution.py:388
  15.6 17.4 %copy-start.7 = (s32[4]{0:T(128)S(1)}, s32[4]{0:T(128)}, u32[]{:S(2)}) copy-start(s32[4]{0:T(128)} %param.12) | copy-start | bytes 52
  15.6 25.0 %copy-start.8 = (s32[64]{0:T(128)S(1)}, s32[64]{0:T(128)}, u32[]{:S(2)}) copy-start(s32[64]{0:T(128)} %param.11) | copy-start | bytes 772
  15.6 7.2 %collective-permute-start = (bf16[256,2048]{1,0:T(8,128)(2,1)}, bf16[256,2048]{1,0:T(8,128)(2,1)S(1)}, u32[]{:S(2)}, u32[]{:S(2)}) collective-permute-start(bf16[256,2048]{1,0:T(8,128)(2,1)} %get-tuple-element.29), channel_id=1, source_target_pairs={{0,1},{1,0},{2,3},{3,2},{4,5},{5,4},{6,7},{7,6},{8,9},{9,8},{10,11... | collective-permute-start | bytes 3145736 | tf_op jit(solution)/shard_map/ppermute | solution.py:227
  20.3 29.1 %collective-permute-start.1 = (bf16[256,2048]{1,0:T(8,128)(2,1)}, bf16[256,2048]{1,0:T(8,128)(2,1)}, u32[]{:S(2)}, u32[]{:S(2)}) collective-permute-start(bf16[256,2048]{1,0:T(8,128)(2,1)} %get-tuple-element.32), channel_id=1, source_target_pairs={{0,1},{1,0},{2,3},{3,2},{4,5},{5,4},{6,7},{7,6},{8,9},{9,8},{10,11... | collective-permute-start | bytes 3145736 | tf_op jit(solution)/shard_map/ppermute | solution.py:227
  22.8 1.0 copy-start.1
  23.8 16.9 %copy-start.2 = (bf16[128,2048]{1,0:T(8,128)(2,1)S(1)}, bf16[128,2048]{1,0:T(8,128)(2,1)}, u32[]{:S(2)}) copy-start(bf16[128,2048]{1,0:T(8,128)(2,1)} %get-tuple-element.34.part_ref) | copy-start | bytes 1572868
  24.0 16.8 %collective-permute-start.2 = (bf16[64,2048]{1,0:T(8,128)(2,1)S(1)}, bf16[64,2048]{1,0:T(8,128)(2,1)S(1)}, u32[]{:S(2)}, u32[]{:S(2)}) collective-permute-start(bf16[64,2048]{1,0:T(8,128)(2,1)S(1)} %get-tuple-element.35), channel_id=1, source_target_pairs={{0,2},{1,15},{2,4},{3,1},{4,6},{5,3},{6,8},{7,5},{8,10},{9,7},{10,... | collective-permute-start | bytes 786440 | tf_op jit(solution)/shard_map/ppermute | solution.py:222
  41.9 10.5 %collective-permute-start.3 = (bf16[128,2048]{1,0:T(8,128)(2,1)}, bf16[128,2048]{1,0:T(8,128)(2,1)}, u32[]{:S(2)}, u32[]{:S(2)}) collective-permute-start(bf16[128,2048]{1,0:T(8,128)(2,1)} %add_own.1), channel_id=1, source_target_pairs={{0,2},{1,15},{2,4},{3,1},{4,6},{5,3},{6,8},{7,5},{8,10},{9,7},{10,... | collective-permute-start | bytes 1572872 | tf_op jit(solution)/shard_map/ppermute | solution.py:222
  45.8 19.7 %all-to-all-start.1 = ((bf16[4,288,512]{2,1,0:T(8,128)(2,1)}), bf16[4,288,512]{2,1,0:T(8,128)(2,1)S(1)}, u32[]{:S(2)}, u32[]{:S(2)}) async-start(bf16[4,288,512]{2,1,0:T(8,128)(2,1)} %pick_factors.1), calls=%async_computation.1 | async-start | bytes 2359296 | tf_op jit(solution)/shard_map/all_to_all | solution.py:426
  49.4 16.2 %copy-start = (bf16[2048,512]{1,0:T(8,128)(2,1)S(1)}, bf16[2048,512]{1,0:T(8,128)(2,1)}, u32[]{:S(2)}) copy-start(bf16[2048,512]{1,0:T(8,128)(2,1)} %hidden_ref.3) | copy-start | bytes 6291460
  55.0 23.1 %collective-permute-start.4 = (bf16[128,2048]{1,0:T(8,128)(2,1)}, bf16[128,2048]{1,0:T(8,128)(2,1)}, u32[]{:S(2)}, u32[]{:S(2)}) collective-permute-start(bf16[128,2048]{1,0:T(8,128)(2,1)} %add_parts.2), channel_id=1, source_target_pairs={{0,2},{1,15},{2,4},{3,1},{4,6},{5,3},{6,8},{7,5},{8,10},{9,7},{10,... | collective-permute-start | bytes 1572872 | tf_op jit(solution)/shard_map/ppermute | solution.py:222
  66.9 0.7 copy-start.3
  67.6 0.6 copy-start.4
  68.2 21.5 %all-to-all-start.2 = ((bf16[16,64,128]{2,1,0:T(8,128)(2,1)}), bf16[16,64,128]{2,1,0:T(8,128)(2,1)S(1)}, u32[]{:S(2)}, u32[]{:S(2)}) async-start(bf16[16,64,128]{2,1,0:T(8,128)(2,1)} %copy-done.3), calls=%async_computation.2 | async-start | bytes 524288 | tf_op jit(solution)/shard_map/all_to_all | solution.py:428
  80.6 24.5 %copy-start.5 = (bf16[4,16,512]{2,1,0:T(8,128)(2,1)S(1)}, bf16[4,16,512]{2,1,0:T(8,128)(2,1)}, u32[]{:S(2)}) copy-start(bf16[4,16,512]{2,1,0:T(8,128)(2,1)} %copy-done.4) | copy-start | bytes 196612
  80.6 24.5 %copy-start.6 = (s32[4]{0:T(128)S(1)}, s32[4]{0:T(128)}, u32[]{:S(2)}) copy-start(s32[4]{0:T(128)} %lengths_ref.1) | copy-start | bytes 52
  80.6 13.4 %collective-permute-start.5 = (bf16[128,2048]{1,0:T(8,128)(2,1)}, bf16[128,2048]{1,0:T(8,128)(2,1)S(1)}, u32[]{:S(2)}, u32[]{:S(2)}) collective-permute-start(bf16[128,2048]{1,0:T(8,128)(2,1)} %add_parts.3), channel_id=1, source_target_pairs={{0,2},{1,15},{2,4},{3,1},{4,6},{5,3},{6,8},{7,5},{8,10},{9,7},{10,... | collective-permute-start | bytes 1572872 | tf_op jit(solution)/shard_map/ppermute | solution.py:222
  90.5 14.6 %all-to-all-start.3 = ((bf16[16,64,128]{2,1,0:T(8,128)(2,1)}), bf16[16,64,128]{2,1,0:T(8,128)(2,1)S(1)}, u32[]{:S(2)}, u32[]{:S(2)}) async-start(bf16[16,64,128]{2,1,0:T(8,128)(2,1)} %sum_parts.1), calls=%async_computation.3 | async-start | bytes 524288 | tf_op jit(solution)/shard_map/all_to_all | solution.py:430
  94.1 3.4 %collective-permute-start.6 = (bf16[64,2048]{1,0:T(8,128)(2,1)S(1)}, bf16[64,2048]{1,0:T(8,128)(2,1)S(1)}, u32[]{:S(2)}, u32[]{:S(2)}) collective-permute-start(bf16[64,2048]{1,0:T(8,128)(2,1)S(1)} %get-tuple-element.37), channel_id=1, source_target_pairs={{0,1},{1,0},{2,3},{3,2},{4,5},{5,4},{6,7},{7,6},{8,9},{9,8},{10,11... | collective-permute-start | bytes 786440 | tf_op jit(solution)/shard_map/ppermute | solution.py:227
